TPU v7x, 32 devices: a whole 2x2x4 slice. The times are simulated.
32 devices in a mesh: dp: 16 (over z, x, core), tensor: 2 (over y).
Axes of the slice: x: 2, y: 2, z: 4, core: 2. Of those that a mesh axis runs over, the one named last changes fastest.
Arguments:
- images_in: bfloat16 [8352, 768], P('dp')
- small_counts: int32 [16], P('dp'), may hold values from 0 to 1, as said below
- large_counts: int32 [16], P('dp'), may hold values from 0 to 1, as said below
- norm1_gain: float32 [768], replicated, may hold values from 0.25 to 1.75
- norm1_bias: float32 [768], replicated, may hold values from -4 to 4
- qkv_weight: bfloat16 [768, 3, 768], P(None, None, 'tensor'), may hold values from -0.3125 to 0.3125
- qv_bias: float32 [2, 768], P(None, 'tensor'), may hold values from -6 to 6
- out_weight: bfloat16 [768, 768], P('tensor'), may hold values from -0.875 to 0.875
- out_bias: float32 [768], replicated, may hold values from -4 to 4
- norm2_gain: float32 [768], replicated, may hold values from 0.25 to 1.75
- norm2_bias: float32 [768], replicated, may hold values from -4 to 4
- up_weight: bfloat16 [768, 3072], P(None, 'tensor'), may hold values from -0.21875 to 0.21875
- up_bias: float32 [3072], P('tensor'), may hold values from -6 to 6
- down_weight: bfloat16 [3072, 768], P('tensor'), may hold values from -0.15625 to 0.15625
- down_bias: float32 [768], replicated, may hold values from -4 to 4
- out_cotangent: bfloat16 [8352, 768], P('dp'), may hold values from -6 to 6
Outputs:
- block_out: bfloat16 [8352, 768], P('dp')
- input_grad: float32 [8352, 768], P('dp')
- norm1_gain_grad: float32 [768], replicated
- norm1_bias_grad: float32 [768], replicated
- qkv_weight_grad: float32 [768, 3, 768], P('dp', None, 'tensor')
- qv_bias_grad: float32 [2, 768], P(None, 'tensor')
- out_weight_grad: float32 [768, 768], P('tensor', 'dp')
- out_bias_grad: float32 [768], replicated
- norm2_gain_grad: float32 [768], replicated
- norm2_bias_grad: float32 [768], replicated
- up_weight_grad: float32 [768, 3072], P('dp', 'tensor')
- up_bias_grad: float32 [3072], P('tensor')
- down_weight_grad: float32 [3072, 768], P('tensor', 'dp')
- down_bias_grad: float32 [768], replicated
Inputs may be any that keep to these rules, and one draw needn't show every extreme that they name: `small_counts`: the first 197 rows of each index's block hold its small images, slots below the count are used, some index uses all 1 and some uses none. `large_counts`: large image slots below the count are used, some index uses all 1 and some uses none.
All inputs are finite; a program needn't handle non-finite values.
Results may differ from a plain program's by a relative error of at most 0.012.
The roundings to bfloat16 on the way count: a program that leaves them out, or rounds other values in their place, can miss the bound.
Values sent between devices are 32-bit elements; how exact they have to be, the bound alone decides.
No kernel may reach another device: no remote copies, remote signals or barrier semaphores. Data moves between devices by JAX's collectives and lax.ppermute only.
A program may use at most 128 MiB of HBM per device.

v0:
```python
import jax
import jax.numpy as jnp
from jax import lax
from jax.sharding import PartitionSpec as P

HEAD_DIM = 64
SMALL_LEN = 197
LARGE_LEN = 325
SMALL_SLOTS = 1
LARGE_SLOTS = 1


NORM_EPS = 1e-06


def norm_parts(values):
    row_mean = jnp.mean(values, axis=-1, keepdims=True)
    centered = values - row_mean
    variance = jnp.mean(centered * centered, axis=-1, keepdims=True)
    inverse = lax.rsqrt(variance + NORM_EPS)
    return (centered * inverse, inverse)


def norm_back(grad_normed_out, normed, inverse, gain):
    scaled = grad_normed_out * gain
    row_inner = jnp.mean(scaled, axis=-1, keepdims=True)
    row_cross = jnp.mean(scaled * normed, axis=-1, keepdims=True)
    grad_values = inverse * (scaled - row_inner - normed * row_cross)
    return (
        grad_values,
        jnp.sum(grad_normed_out * normed, axis=0),
        jnp.sum(grad_normed_out, axis=0),
    )


def row_mask(small_count, large_count):
    small_live = (jnp.arange(SMALL_SLOTS) < small_count).astype(jnp.float32)
    large_live = (jnp.arange(LARGE_SLOTS) < large_count).astype(jnp.float32)
    small_rows = jnp.broadcast_to(small_live[:, None], (SMALL_SLOTS, SMALL_LEN)).reshape(-1)
    large_rows = jnp.broadcast_to(large_live[:, None], (LARGE_SLOTS, LARGE_LEN)).reshape(-1)
    return jnp.concatenate([small_rows, large_rows], axis=0)


def split_groups(rows):
    split_at = SMALL_SLOTS * SMALL_LEN
    heads_here = rows.shape[1] // HEAD_DIM
    small_part = rows[:split_at].reshape(SMALL_SLOTS, SMALL_LEN, heads_here, HEAD_DIM)
    large_part = rows[split_at:].reshape(LARGE_SLOTS, LARGE_LEN, heads_here, HEAD_DIM)
    return (small_part, large_part)


def join_groups(parts):
    width = parts[0].shape[2] * parts[0].shape[3]
    return jnp.concatenate([parts[0].reshape(-1, width), parts[1].reshape(-1, width)], axis=0)


def scores_of(queries, key_rows, scaling):
    return (
        jnp.einsum("blhe,bmhe->bhlm", queries, key_rows, preferred_element_type=jnp.float32)
        * scaling
    )


def attend_forward(queries, key_rows, value_rows, scaling):
    scores = scores_of(queries, key_rows, scaling)
    row_top = jnp.max(scores, axis=-1, keepdims=True)
    exp_scores = jnp.exp(scores - row_top)
    row_total = jnp.sum(exp_scores, axis=-1, keepdims=True)
    soft_low = (exp_scores / row_total).astype(jnp.bfloat16)
    result = jnp.einsum("bhlm,bmhe->blhe", soft_low, value_rows, preferred_element_type=jnp.float32)
    return (result, row_top + jnp.log(row_total))


def attend_backward(queries, key_rows, value_rows, log_total, grad_result, scaling):
    scores = scores_of(queries, key_rows, scaling)
    soft_full = jnp.exp(scores - log_total)
    grad_values = jnp.einsum(
        "bhlm,blhe->bmhe",
        soft_full.astype(jnp.bfloat16),
        grad_result,
        preferred_element_type=jnp.float32,
    )
    grad_soft = jnp.einsum(
        "blhe,bmhe->bhlm", grad_result, value_rows, preferred_element_type=jnp.float32
    )
    row_inner = jnp.sum(grad_soft * soft_full, axis=-1, keepdims=True)
    grad_scores = (soft_full * (grad_soft - row_inner)).astype(jnp.bfloat16)
    grad_queries = (
        jnp.einsum("bhlm,bmhe->blhe", grad_scores, key_rows, preferred_element_type=jnp.float32)
        * scaling
    )
    grad_keys = (
        jnp.einsum("bhlm,blhe->bmhe", grad_scores, queries, preferred_element_type=jnp.float32)
        * scaling
    )
    return (grad_queries, grad_keys, grad_values)


def gelu_exact(pre_values):
    return jax.nn.gelu(pre_values, approximate=False)


def per_device(
    images_in,
    small_counts,
    large_counts,
    norm1_gain,
    norm1_bias,
    qkv_weight,
    qv_bias,
    out_weight,
    out_bias,
    norm2_gain,
    norm2_bias,
    up_weight,
    up_bias,
    down_weight,
    down_bias,
    out_cotangent,
):
    scaling = HEAD_DIM ** (-0.5)
    live_rows = row_mask(small_counts[0], large_counts[0])[:, None]
    inputs = images_in.astype(jnp.float32)
    normed_one, inverse_one = norm_parts(inputs)
    first_low = (normed_one * norm1_gain + norm1_bias).astype(jnp.bfloat16)
    projected = jnp.einsum("td,dcj->tcj", first_low, qkv_weight, preferred_element_type=jnp.float32)
    queries = (projected[:, 0] + qv_bias[0]).astype(jnp.bfloat16)
    key_rows = projected[:, 1].astype(jnp.bfloat16)
    value_rows = (projected[:, 2] + qv_bias[1]).astype(jnp.bfloat16)
    query_groups = split_groups(queries)
    key_groups = split_groups(key_rows)
    value_groups = split_groups(value_rows)
    results = []
    log_totals = []
    for which_group in range(2):
        result, log_total = attend_forward(
            query_groups[which_group], key_groups[which_group], value_groups[which_group], scaling
        )
        results.append(result)
        log_totals.append(log_total)
    mixed_heads = join_groups(results).astype(jnp.bfloat16)
    attn_part = jnp.dot(mixed_heads, out_weight, preferred_element_type=jnp.float32)
    attn_branch = lax.psum(attn_part, "tensor") + out_bias
    hidden = inputs + live_rows * attn_branch
    normed_two, inverse_two = norm_parts(hidden)
    second_low = (normed_two * norm2_gain + norm2_bias).astype(jnp.bfloat16)
    pre_act = jnp.dot(second_low, up_weight, preferred_element_type=jnp.float32) + up_bias
    act_full, gelu_pull = jax.vjp(gelu_exact, pre_act)
    act_low = act_full.astype(jnp.bfloat16)
    mlp_part = jnp.dot(act_low, down_weight, preferred_element_type=jnp.float32)
    mlp_branch = lax.psum(mlp_part, "tensor") + down_bias
    block_out = (hidden + live_rows * mlp_branch).astype(jnp.bfloat16)
    grad_output = out_cotangent.astype(jnp.float32)
    grad_mlp = (live_rows * grad_output).astype(jnp.bfloat16)
    down_bias_grad = jnp.sum(grad_mlp.astype(jnp.float32), axis=0)
    down_weight_grad = jnp.einsum(
        "tf,td->fd", act_low, grad_mlp, preferred_element_type=jnp.float32
    )
    grad_act = jnp.einsum("td,fd->tf", grad_mlp, down_weight, preferred_element_type=jnp.float32)
    grad_pre = gelu_pull(grad_act)[0].astype(jnp.bfloat16)
    up_bias_grad = jnp.sum(grad_pre.astype(jnp.float32), axis=0)
    up_weight_grad = jnp.einsum(
        "td,tf->df", second_low, grad_pre, preferred_element_type=jnp.float32
    )
    second_part = jnp.einsum("tf,df->td", grad_pre, up_weight, preferred_element_type=jnp.float32)
    grad_second = lax.psum(second_part, "tensor")
    grad_hidden_norm, norm2_gain_grad, norm2_bias_grad = norm_back(
        grad_second, normed_two, inverse_two, norm2_gain
    )
    grad_hidden = grad_output + grad_hidden_norm
    grad_attn = (live_rows * grad_hidden).astype(jnp.bfloat16)
    out_bias_grad = jnp.sum(grad_attn.astype(jnp.float32), axis=0)
    out_weight_grad = jnp.einsum(
        "tj,td->jd", mixed_heads, grad_attn, preferred_element_type=jnp.float32
    )
    grad_mixed = jnp.einsum(
        "td,jd->tj", grad_attn, out_weight, preferred_element_type=jnp.float32
    ).astype(jnp.bfloat16)
    grad_groups = split_groups(grad_mixed)
    query_grads = []
    key_grads = []
    value_grads = []
    for which_group in range(2):
        grad_q, grad_k, grad_v = attend_backward(
            query_groups[which_group],
            key_groups[which_group],
            value_groups[which_group],
            log_totals[which_group],
            grad_groups[which_group],
            scaling,
        )
        query_grads.append(grad_q)
        key_grads.append(grad_k)
        value_grads.append(grad_v)
    grad_queries = join_groups(query_grads).astype(jnp.bfloat16)
    grad_keys = join_groups(key_grads).astype(jnp.bfloat16)
    grad_values = join_groups(value_grads).astype(jnp.bfloat16)
    qv_bias_grad = jnp.stack(
        [
            jnp.sum(grad_queries.astype(jnp.float32), axis=0),
            jnp.sum(grad_values.astype(jnp.float32), axis=0),
        ],
        axis=0,
    )
    grad_projected = jnp.stack([grad_queries, grad_keys, grad_values], axis=1)
    qkv_weight_grad = jnp.einsum(
        "td,tcj->dcj", first_low, grad_projected, preferred_element_type=jnp.float32
    )
    first_part = jnp.einsum(
        "tcj,dcj->td", grad_projected, qkv_weight, preferred_element_type=jnp.float32
    )
    grad_first = lax.psum(first_part, "tensor")
    grad_input_norm, norm1_gain_grad, norm1_bias_grad = norm_back(
        grad_first, normed_one, inverse_one, norm1_gain
    )
    input_grad = grad_hidden + grad_input_norm
    qkv_weight_grad, out_weight_grad, up_weight_grad, down_weight_grad = (
        lax.psum_scatter(qkv_weight_grad, "dp", scatter_dimension=0, tiled=True),
        lax.psum_scatter(out_weight_grad, "dp", scatter_dimension=1, tiled=True),
        lax.psum_scatter(up_weight_grad, "dp", scatter_dimension=0, tiled=True),
        lax.psum_scatter(down_weight_grad, "dp", scatter_dimension=1, tiled=True),
    )
    summed = lax.psum(
        (
            norm1_gain_grad,
            norm1_bias_grad,
            qv_bias_grad,
            out_bias_grad,
            norm2_gain_grad,
            norm2_bias_grad,
            up_bias_grad,
            down_bias_grad,
        ),
        "dp",
    )
    return (
        block_out,
        input_grad,
        summed[0],
        summed[1],
        qkv_weight_grad,
        summed[2],
        out_weight_grad,
        summed[3],
        summed[4],
        summed[5],
        up_weight_grad,
        summed[6],
        down_weight_grad,
        summed[7],
    )


def solution(mesh):
    placed = (
        P("dp", None),
        P("dp"),
        P("dp"),
        P(),
        P(),
        P(None, None, "tensor"),
        P(None, "tensor"),
        P("tensor", None),
        P(),
        P(),
        P(),
        P(None, "tensor"),
        P("tensor"),
        P("tensor", None),
        P(),
        P("dp", None),
    )
    return jax.shard_map(
        per_device,
        mesh=mesh,
        in_specs=placed,
        out_specs=(
            P("dp", None),
            P("dp", None),
            P(),
            P(),
            P("dp", None, "tensor"),
            P(None, "tensor"),
            P("tensor", "dp"),
            P(),
            P(),
            P(),
            P("dp", "tensor"),
            P("tensor"),
            P("tensor", "dp"),
            P(),
        ),
        check_vma=False,
    )
```

profile of v0, /device:TPU:0, one launch (start us, length us, event | category | flops | bytes accessed | tf_op | source)
XLA Modules:
  0.0 573.5 jit_solution(8668564910149023787)
XLA Ops:
  10.4 2.9 fusion.64
  18.9 1.8 copy.61
  34.2 1.9 fusion.46
  37.8 53.9 %all-reduce.7.cloned.1.call-done = f32[522,768]{1,0:T(8,128)} async-done(((f32[522,768]{1,0:T(8,128)}), f32[522,768]{1,0:T(8,128)}) %all-reduce.7.cloned.1.call-update) | async-done | bytes 1603600 | tf_op jit(solution)/shard_map/psum | solution.py:143
  91.6 1.9 fusion.63
  94.3 9.1 %multiply_convert_fusion = (bf16[522,1536]{1,0:T(8,128)(2,1)}, f32[522,1536]{1,0:T(8,128)S(1)}, f32[522,1536]{1,0:T(8,128)S(1)}) fusion(f32[1536]{0:T(1024)S(1)} %copy-done.53, bf16[768,1536]{1,0:T(8,128)(2,1)S(1)} %copy-done, f32[522,768]{1,0:T(8,128)S(1)} %get-tuple-element.40, f32[768]{0:T(1024)S(1)} %copy-done.56, f32[768]{0:T(1024)S(1)} %copy-done.42, ...), kind=kOutput, calls=%fused_computation.4 | convolution fusion | flops 1286475264 | bytes 11997264 | tf_op jit(solution)/shard_map/dot_general | solution.py:147
  103.5 3.2 convert_reduce_fusion
  107.8 2.6 fusion.67
  110.8 4.9 fusion.66
  115.7 47.5 %all-reduce.9.cloned.1.call-done = f32[522,768]{1,0:T(8,128)} async-done(((f32[522,768]{1,0:T(8,128)}), f32[522,768]{1,0:T(8,128)}) %all-reduce.9.cloned.1.call-update) | async-done | bytes 1603600 | tf_op jit(solution)/shard_map/psum | solution.py:166
  163.2 2.9 multiply_reduce_fusion.2
  166.1 2.6 convert_reduce_fusion.3
  182.3 4.0 convolution_bitcast_fusion
  187.6 1.8 fusion.45
  189.5 4.9 fusion.47
  195.9 5.8 %fusion.61 = f32[768,1536]{1,0:T(8,128)} fusion(bf16[522,1536]{1,0:T(8,128)(2,1)} %copy-done.58, f32[522,768]{1,0:T(8,128)S(1)} %copy-done.6, f32[768]{0:T(1024)S(1)} %copy-done.57, f32[768]{0:T(1024)S(1)} %copy-done.42, f32[522]{0:T(1024)S(1)} %add_rsqrt_fusion, f32[522]{0:T(1024)S(1)} %broadcast_multiply_fusion.4), kind=kOutput, calls=%fused_computation.119 | convolution fusion | flops 1233556992 | bytes 7936080 | tf_op jit(solution)/shard_map/td,tf->df/dot_general | solution.py:162
  201.7 5.9 %fusion.55 = f32[1536,768]{0,1:T(8,128)} fusion(bf16[522,1536]{1,0:T(8,128)(2,1)} %get-tuple-element.37, bf16[522,768]{1,0:T(8,128)(2,1)} %param.31, f32[522]{0:T(1024)S(1)} %concatenate.58), kind=kOutput, calls=%fused_computation.117 | convolution fusion | flops 1232755200 | bytes 7126056 | tf_op jit(solution)/shard_map/tf,td->fd/dot_general | solution.py:156
  209.4 65.3 %all-reduce.11.cloned.1.call-done = (f32[522,768]{1,0:T(8,128)}, f32[522,768]{1,0:T(8,128)}) async-done(((f32[522,768]{1,0:T(8,128)}, f32[522,768]{1,0:T(8,128)}), (f32[522,768]{1,0:T(8,128)}, f32[522,768]{1,0:T(8,128)})) %all-reduce.11.cloned.1.call-update) | async-done | bytes 3207184 | tf_op jit(solution)/shard_map/psum | solution.py:151
  274.6 2.2 fusion.20
  276.9 62.0 %all-reduce.1 = (f32[768]{0:T(1024)}, f32[768]{0:T(1024)}, f32[2,384]{1,0:T(2,128)}, f32[768]{0:T(1024)}, f32[768]{0:T(1024)}, /*index=5*/f32[768]{0:T(1024)}, f32[1536]{0:T(1024)}, f32[768]{0:T(1024)}) all-reduce(f32[768]{0:T(1024)S(1)} %get-tuple-element.16, ...), channel_id=1, replica_groups=mesh['dp'=16,'tensor'=2] {'dp'}, use_global_device_ids=true, to_apply=%region_19.0 | all-reduce | flops 6912 | bytes 55296 | tf_op jit(solution)/shard_map/psum | solution.py:223
  338.9 2.7 add_convert_fusion.1
  343.4 64.8 %reduce-scatter.5.cloned.1.call-done = f32[48,3,384]{2,0,1:T(8,128)} async-done(((f32[768,3,384]{2,0,1:T(8,128)}), f32[48,3,384]{2,0,1:T(8,128)}) %reduce-scatter.5.cloned.1.call-update) | async-done | bytes 221200 | tf_op jit(solution)/shard_map/reduce_scatter | solution.py:218
  408.2 78.8 %reduce-scatter.9.cloned.1.call-done = f32[48,1536]{1,0:T(8,128)} async-done(((f32[768,1536]{1,0:T(8,128)}), f32[48,1536]{1,0:T(8,128)}) %reduce-scatter.9.cloned.1.call-update) | async-done | bytes 294928 | tf_op jit(solution)/shard_map/reduce_scatter | solution.py:220
  487.0 79.6 %reduce-scatter.11.cloned.1.call-done = f32[1536,48]{0,1:T(8,128)} async-done(((f32[1536,768]{0,1:T(8,128)}), f32[1536,48]{0,1:T(8,128)}) %reduce-scatter.11.cloned.1.call-update) | async-done | bytes 294928 | tf_op jit(solution)/shard_map/reduce_scatter | solution.py:221
  (193 shorter events, 44.2 us)
Async XLA Ops:
  7.2 86.7 %copy-start = (bf16[768,1536]{1,0:T(8,128)(2,1)S(1)}, bf16[768,1536]{1,0:T(8,128)(2,1)}, u32[]{:S(2)}) copy-start(bf16[768,1536]{1,0:T(8,128)(2,1)} %param.27) | copy-start | bytes 7077892
  7.2 84.4 %all-reduce.7.cloned.1.call-start = ((), (), s32[]{:S(2)}) async-start(), calls=%async_computation.4 | async-start | bytes 3244032 | tf_op jit(solution)/shard_map/psum | solution.py:143
  18.9 11.6 %copy-start.18 = (bf16[325,384]{0,1:T(8,128)(2,1)}, bf16[325,384]{0,1:T(8,128)(2,1)S(1)}, u32[]{:S(2)}) copy-start(bf16[325,384]{0,1:T(8,128)(2,1)S(1)} %copy.65) | copy-start | bytes 748804
  34.2 57.4 %copy-start.49 = (f32[768]{0:T(1024)S(1)}, f32[768]{0:T(1024)}, u32[]{:S(2)}) copy-start(f32[768]{0:T(1024)} %param.24) | copy-start | bytes 9220
  36.2 127.0 %all-reduce.9.cloned.1.call-start = ((), (), s32[]{:S(2)}) async-start(), calls=%async_computation.5 | async-start | bytes 3244032 | tf_op jit(solution)/shard_map/psum | solution.py:166
  93.5 10.0 %copy-start.4 = (f32[522,768]{1,0:T(8,128)}, f32[522,768]{1,0:T(8,128)S(1)}, u32[]{:S(2)}) copy-start(f32[522,768]{1,0:T(8,128)S(1)} %get-tuple-element.40) | copy-start | bytes 4810756
  94.3 9.1 %copy-start.29 = (bf16[522,768]{1,0:T(8,128)(2,1)S(1)}, bf16[522,768]{1,0:T(8,128)(2,1)}, u32[]{:S(2)}) copy-start(bf16[522,768]{1,0:T(8,128)(2,1)} %param.31) | copy-start | bytes 2405380
  94.3 9.1 %copy-start.52 = (bf16[1536,768]{1,0:T(8,128)(2,1)S(1)}, bf16[1536,768]{1,0:T(8,128)(2,1)}, u32[]{:S(2)}) copy-start(bf16[1536,768]{1,0:T(8,128)(2,1)} %param.29) | copy-start | bytes 7077892
  110.5 164.1 %all-reduce.11.cloned.1.call-start = ((), (), s32[]{:S(2)}) async-start(), calls=%async_computation.10 | async-start | bytes 6488064 | tf_op jit(solution)/shard_map/psum | solution.py:151
  110.8 52.4 %copy-start.5 = (f32[522,768]{1,0:T(8,128)S(1)}, f32[522,768]{1,0:T(8,128)}, u32[]{:S(2)}) copy-start(f32[522,768]{1,0:T(8,128)} %copy-done.4) | copy-start | bytes 4810756
  181.1 5.2 copy-start.39
  181.7 4.6 copy-start.40
  181.8 4.5 copy-start.41
  186.4 157.0 %reduce-scatter.7.cloned.1.call-start = ((), (), s32[]{:S(2)}) async-start(), calls=%async_computation.7 | async-start | bytes 1253376 | tf_op jit(solution)/shard_map/reduce_scatter | solution.py:219
  189.4 218.8 %reduce-scatter.5.cloned.1.call-start = ((), (), s32[]{:S(2)}) async-start(), calls=%async_computation.6 | async-start | bytes 3760128 | tf_op jit(solution)/shard_map/reduce_scatter | solution.py:218
  194.5 292.6 %reduce-scatter.9.cloned.1.call-start = ((), (), s32[]{:S(2)}) async-start(), calls=%async_computation.8 | async-start | bytes 5013504 | tf_op jit(solution)/shard_map/reduce_scatter | solution.py:220
  201.7 365.0 %reduce-scatter.11.cloned.1.call-start = ((), (), s32[]{:S(2)}) async-start(), calls=%async_computation.9 | async-start | bytes 5013504 | tf_op jit(solution)/shard_map/reduce_scatter | solution.py:221
  207.7 69.2 %copy-start.44 = (f32[768]{0:T(1024)S(1)}, f32[768]{0:T(1024)}, u32[]{:S(2)}) copy-start(f32[768]{0:T(1024)} %get-tuple-element.14) | copy-start | bytes 9220
  207.7 69.2 %copy-start.45 = (f32[768]{0:T(1024)S(1)}, f32[768]{0:T(1024)}, u32[]{:S(2)}) copy-start(f32[768]{0:T(1024)} %get-tuple-element.20) | copy-start | bytes 9220
  207.7 69.2 %copy-start.46 = (f32[768]{0:T(1024)S(1)}, f32[768]{0:T(1024)}, u32[]{:S(2)}) copy-start(f32[768]{0:T(1024)} %get-tuple-element.34) | copy-start | bytes 9220
  207.7 69.2 %copy-start.47 = (f32[768]{0:T(1024)S(1)}, f32[768]{0:T(1024)}, u32[]{:S(2)}) copy-start(f32[768]{0:T(1024)} %get-tuple-element.43) | copy-start | bytes 9220
  207.7 69.2 %copy-start.48 = (f32[1536]{0:T(1024)S(1)}, f32[1536]{0:T(1024)}, u32[]{:S(2)}) copy-start(f32[1536]{0:T(1024)} %get-tuple-element.55) | copy-start | bytes 18436
  208.1 130.9 %copy-start.50 = (f32[768]{0:T(1024)S(1)}, f32[768]{0:T(1024)}, u32[]{:S(2)}) copy-start(f32[768]{0:T(1024)} %param.30) | copy-start | bytes 9220
  341.6 225.0 %copy-start.1 = (bf16[768,1536]{1,0:T(8,128)(2,1)S(1)}, bf16[768,1536]{1,0:T(8,128)(2,1)}, u32[]{:S(2)}) copy-start(bf16[768,1536]{1,0:T(8,128)(2,1)} %param.27) | copy-start | bytes 7077892
  (42 other events, 79.9 us)
Sparse Core Ops, SparseCore 0:
  36.3 55.2 all-reduce.6
  110.6 52.5 all-reduce.8
  186.5 88.0 all-reduce.10
  278.7 58.0 reduce-scatter.6
  341.1 67.0 reduce-scatter.4
  412.5 74.4 reduce-scatter.8
  492.0 74.6 reduce-scatter.10
where the time goes:
time: 574 us; the launch traced here: 573 us
  waiting for transfers between devices  390 us (68%)
  blocking collectives  62 us (11%)
  matrix products  57 us (10%)
  local copies, waits for them, and re-layouts  26.4 us (5%)
  other arithmetic  20.9 us (4%)
  between operations  16.2 us (3%)
    reduce_scatter x1, waiting for transfers between devices, per_device(): lax.psum_scatter(down_weight_grad, 'dp', scatter_dimension=1, tiled=True)  79.6 us
    reduce_scatter x1, waiting for transfers between devices, per_device(): lax.psum_scatter(up_weight_grad, 'dp', scatter_dimension=0, tiled=True)  78.8 us
    psum x1, waiting for transfers between devices, per_device(): mlp_branch = lax.psum(mlp_part, 'tensor') + down_bias  65.3 us
    reduce_scatter x1, waiting for transfers between devices, per_device(): lax.psum_scatter(qkv_weight_grad, 'dp', scatter_dimension=0, tiled=True)  64.8 us
    psum x1, blocking collectives, per_device(): lax.psum((norm1_gain_grad, norm1_bias_grad, qv_bias_grad, out_bias_grad,...  62 us
    psum x1, waiting for transfers between devices, per_device(): attn_branch = lax.psum(attn_part, 'tensor') + out_bias  53.9 us
    psum x1, waiting for transfers between devices, per_device(): grad_second = lax.psum(second_part, 'tensor')  47.5 us
  transfers between devices with their start and end apart: 7, of which 6 were waited for; matrix products, arithmetic and copies ran while one was open for 6% of the time, Pallas kernels for 0%

commit v1 on v0

v1 whole, which is shorter than its diff:
```python
import functools

import jax
import jax.numpy as jnp
from jax import lax
from jax.experimental import pallas as pl
from jax.experimental.pallas import tpu as pltpu
from jax.sharding import PartitionSpec as P

HEAD_DIM = 64
PAIR = 2 * HEAD_DIM
LENGTHS = (197, 325)
PADDED = tuple(-(-length // 16) * 16 for length in LENGTHS)
NORM_EPS = 1e-06
F32 = jnp.float32
BF16 = jnp.bfloat16
VMEM_LIMIT = 56 * 1024 * 1024


def norm_parts(values):
    row_mean = jnp.mean(values, axis=-1, keepdims=True)
    centered = values - row_mean
    variance = jnp.mean(centered * centered, axis=-1, keepdims=True)
    inverse = lax.rsqrt(variance + NORM_EPS)
    return (centered * inverse, inverse)


def mm(left, right, dims=((1,), (0,))):
    return lax.dot_general(left, right, (dims, ((), ())), preferred_element_type=F32)


NT = ((1,), (1,))
TN = ((0,), (0,))


def col_sum(values):
    return jnp.sum(values, axis=0, keepdims=True)


def low_lanes(rows):
    return lax.broadcasted_iota(jnp.int32, (rows, PAIR), 1) < HEAD_DIM


def key_mask(padded, length):
    return lax.broadcasted_iota(jnp.int32, (padded, padded), 0) < length


def forward_kernel(x_ref, gain_ref, bias_ref, w_ref, qvb_ref, *outs):
    scaling = HEAD_DIM ** (-0.5)
    start = 0
    for group in range(2):
        first_ref, qkv_ref, mix_ref, lse_ref = outs[4 * group : 4 * group + 4]
        rows, length = PADDED[group], LENGTHS[group]
        normed, _ = norm_parts(x_ref[start : start + rows, :].astype(F32))
        start += rows
        first = (normed * gain_ref[...] + bias_ref[...]).astype(BF16)
        first_ref[...] = first
        qkv_ref[0] = (mm(first, w_ref[0]) + qvb_ref[0:1, :]).astype(BF16)
        qkv_ref[1] = mm(first, w_ref[1]).astype(BF16)
        qkv_ref[2] = (mm(first, w_ref[2]) + qvb_ref[1:2, :]).astype(BF16)
        low = low_lanes(rows)
        keep_keys = key_mask(rows, length)
        for pair in range(qkv_ref.shape[2] // PAIR):
            lanes = slice(pair * PAIR, (pair + 1) * PAIR)
            queries, keys = qkv_ref[0, :, lanes], qkv_ref[1, :, lanes]
            values_t = qkv_ref[2, :, lanes].T
            mixed_t = []
            for side in range(2):
                own = low if side == 0 else jnp.logical_not(low)
                scores = mm(keys, jnp.where(own, queries, jnp.zeros_like(queries)), NT) * scaling
                scores = jnp.where(keep_keys, scores, -jnp.inf)
                top = jnp.max(scores, axis=0, keepdims=True)
                exps = jnp.exp(scores - top)
                total = jnp.sum(exps, axis=0, keepdims=True)
                soft_low = (exps / total).astype(BF16)
                mixed_t.append(mm(values_t[side * HEAD_DIM : (side + 1) * HEAD_DIM], soft_low))
                head = 2 * pair + side
                lse_ref[head : head + 1, :] = top + jnp.log(total)
            mix_ref[:, lanes] = jnp.concatenate(mixed_t, axis=0).T.astype(BF16).astype(F32)


def mlp_kernel(
    group, info_ref, x_ref, ct_ref, mix_ref, mix2_ref, ow_ref, ow1_ref, ow2_ref, ob_ref,
    gain_ref, bias_ref, up_ref, upb_ref, down_ref,
    hidden_ref, second_ref, gmlp_ref, act_ref, gpre_ref, gs_ref, upsum_ref, downsum_ref,
    ow_all, mix_all,
):
    step = pl.program_id(0)

    @pl.when(step == 0)
    def _():
        side, core = info_ref[0], info_ref[1]
        live = (info_ref[2 + group] > 0).astype(F32)
        span, half = ow_ref.shape[0], ow1_ref.shape[0]
        mine, other = side * span, (1 - side) * span
        ow_all[pl.ds(pl.multiple_of(mine, span), span), :] = ow_ref[...]
        at1 = pl.multiple_of(other + core * half, half)
        at2 = pl.multiple_of(other + (1 - core) * half, half)
        ow_all[pl.ds(at1, half), :] = ow1_ref[...].astype(BF16)
        ow_all[pl.ds(at2, half), :] = ow2_ref[...].astype(BF16)
        mix_all[:, pl.ds(pl.multiple_of(mine, span), span)] = mix_ref[...].astype(BF16)
        mix_all[:, pl.ds(pl.multiple_of(other, span), span)] = mix2_ref[...].astype(BF16)
        branch = mm(mix_all[...], ow_all[...]) + ob_ref[...]
        hidden = x_ref[...].astype(F32) + live * branch
        hidden_ref[...] = hidden
        normed, _ = norm_parts(hidden)
        second_ref[...] = (normed * gain_ref[...] + bias_ref[...]).astype(BF16)
        gmlp = live * ct_ref[...].astype(F32)
        gmlp_ref[...] = gmlp.astype(BF16)
        downsum_ref[...] = col_sum(gmlp)

    pre = mm(second_ref[...], up_ref[...]) + upb_ref[...]
    cdf = 0.5 * (1.0 + lax.erf(pre * (0.5**0.5)))
    act_ref[...] = (pre * cdf).astype(BF16)
    slope = cdf + pre * (jnp.exp(-0.5 * pre * pre) * 0.3989422804014327)
    grad_act = mm(gmlp_ref[...], down_ref[...], NT)
    gpre = (grad_act * slope).astype(BF16)
    gpre_ref[...] = gpre
    upsum_ref[...] = col_sum(gpre.astype(F32))
    part = mm(gpre, up_ref[...], NT)

    @pl.when(step == 0)
    def _():
        gs_ref[...] = part

    @pl.when(step > 0)
    def _():
        gs_ref[...] += part


def scatter_rows(core, grad_ref, keep_ref, send_ref, cols):
    blocks, height = keep_ref.shape[0], keep_ref.shape[1]
    bits = blocks.bit_length() - 1
    for place in range(blocks):
        index = sum(((place >> (bits - 1 - b)) & 1) << b for b in range(bits))
        even = grad_ref[2 * index * height : (2 * index + 1) * height, :]
        odd = grad_ref[(2 * index + 1) * height : (2 * index + 2) * height, :]
        keep_ref[place, :, cols] = jnp.where(core == 0, even, odd)
        send_ref[place, :, cols] = jnp.where(core == 0, odd, even)


def mlp_weights_kernel(
    info_ref, seca_ref, secb_ref, gma_ref, gmb_ref, acta_ref, actb_ref, gpa_ref, gpb_ref,
    keepd_ref, sendd_ref, keepu_ref, sendu_ref, grad,
):
    core = info_ref[1]
    grad[...] = mm(gma_ref[...], acta_ref[...], TN) + mm(gmb_ref[...], actb_ref[...], TN)
    scatter_rows(core, grad, keepd_ref, sendd_ref, slice(None))
    grad[...] = mm(seca_ref[...], gpa_ref[...], TN) + mm(secb_ref[...], gpb_ref[...], TN)
    scatter_rows(core, grad, keepu_ref, sendu_ref, slice(None))


def attn_weights_kernel(
    info_ref, firsta_ref, firstb_ref, da_ref, db_ref, ga_ref, gb_ref, mixa_ref, mixb_ref,
    keep_ref, send_ref, grad,
):
    core = info_ref[1]
    width = grad.shape[1]
    for part in range(3):
        grad[...] = mm(firsta_ref[...], da_ref[part], TN) + mm(firstb_ref[...], db_ref[part], TN)
        scatter_rows(core, grad, keep_ref, send_ref, slice(part * width, (part + 1) * width))
    grad[...] = mm(ga_ref[...], mixa_ref[...].astype(BF16), TN) + mm(
        gb_ref[...], mixb_ref[...].astype(BF16), TN
    )
    scatter_rows(core, grad, keep_ref, send_ref, slice(3 * width, 4 * width))


def norm_back(grad, normed, inverse, gain):
    scaled = grad * gain
    row_inner = jnp.mean(scaled, axis=-1, keepdims=True)
    row_cross = jnp.mean(scaled * normed, axis=-1, keepdims=True)
    return inverse * (scaled - row_inner - normed * row_cross)


def backward_kernel(
    group, info_ref, gs_ref, gs2_ref, hidden_ref, ct_ref, gain_ref, ow_ref, qkv_ref, lse_ref, w_ref,
    act_ref, down_ref,
    dqkv_ref, gattn_ref, gh_ref, gf_ref, mlp_ref, sums_ref, gmix,
):
    scaling = HEAD_DIM ** (-0.5)
    rows, length = PADDED[group], LENGTHS[group]
    live = (info_ref[2 + group] > 0).astype(F32)
    grad_second = gs_ref[...] + gs2_ref[...]
    normed, inverse = norm_parts(hidden_ref[...])
    grad_hidden = ct_ref[...].astype(F32) + norm_back(grad_second, normed, inverse, gain_ref[...])
    gh_ref[...] = grad_hidden
    sums_ref[0:1, :] = col_sum(grad_second * normed)
    sums_ref[1:2, :] = col_sum(grad_second)
    gattn = (live * grad_hidden).astype(BF16)
    gattn_ref[...] = gattn
    sums_ref[2:3, :] = col_sum(gattn.astype(F32))
    gmix[...] = mm(gattn, ow_ref[...], NT).astype(BF16)
    low = low_lanes(rows)
    keep_keys = key_mask(rows, length)
    for pair in range(qkv_ref.shape[2] // PAIR):
        lanes = slice(pair * PAIR, (pair + 1) * PAIR)
        queries, keys, values = (qkv_ref[c, :, lanes] for c in range(3))
        grads = gmix[:, lanes]
        keys_t = keys.T
        zero = jnp.zeros_like(queries)
        dq_t, dk, dv = [], [], []
        for side in range(2):
            own = low if side == 0 else jnp.logical_not(low)
            head = 2 * pair + side
            scores = mm(keys, jnp.where(own, queries, zero), NT) * scaling
            soft = jnp.where(keep_keys, jnp.exp(scores - lse_ref[head : head + 1, :]), 0.0)
            grad_soft = mm(values, jnp.where(own, grads, zero), NT)
            inner = jnp.sum(grad_soft * soft, axis=0, keepdims=True)
            grad_scores = (soft * (grad_soft - inner)).astype(BF16)
            dv.append(mm(soft.astype(BF16), grads))
            dk.append(mm(grad_scores, queries))
            dq_t.append(mm(keys_t[side * HEAD_DIM : (side + 1) * HEAD_DIM], grad_scores))
        dqkv_ref[0, :, lanes] = (jnp.concatenate(dq_t, axis=0).T * scaling).astype(BF16)
        dqkv_ref[1, :, lanes] = (jnp.where(low, dk[0], dk[1]) * scaling).astype(BF16)
        dqkv_ref[2, :, lanes] = jnp.where(low, dv[0], dv[1]).astype(BF16)
    gf_ref[...] = (
        mm(dqkv_ref[0], w_ref[0], NT) + mm(dqkv_ref[1], w_ref[1], NT) + mm(dqkv_ref[2], w_ref[2], NT)
    )
    half = qkv_ref.shape[2]
    sums_ref[3:4, :half] = col_sum(dqkv_ref[0].astype(F32))
    sums_ref[3:4, half:] = col_sum(dqkv_ref[2].astype(F32))
    mlp_ref[...] = mm(act_ref[...], down_ref[...])


def input_kernel(
    xa_ref, gfa_ref, gfa2_ref, gha_ref, xb_ref, gfb_ref, gfb2_ref, ghb_ref, gain_ref,
    sa_ref, sb_ref, ua_ref, ub_ref, da_ref, db_ref, grad_ref, small_ref,
):
    start, gains, biases = 0, 0.0, 0.0
    for group, (x_ref, gf_ref, gf2_ref, gh_ref) in enumerate(
        ((xa_ref, gfa_ref, gfa2_ref, gha_ref), (xb_ref, gfb_ref, gfb2_ref, ghb_ref))
    ):
        length = LENGTHS[group]
        grad_first = gf_ref[...] + gf2_ref[...]
        normed, inverse = norm_parts(x_ref[...].astype(F32))
        value = gh_ref[...] + norm_back(grad_first, normed, inverse, gain_ref[...])
        grad_ref[start : start + length, :] = value[:length]
        start += length
        gains += col_sum(grad_first * normed)
        biases += col_sum(grad_first)
    width = grad_ref.shape[1]
    small_ref[...] = jnp.zeros_like(small_ref)
    small_ref[0:1, :] = gains
    small_ref[1:2, :] = biases
    small_ref[2:6, :] = sa_ref[0:4, :] + sb_ref[0:4, :]
    small_ref[6:7, :] = ua_ref[:, :width] + ub_ref[:, :width]
    small_ref[7:8, :] = ua_ref[:, width:] + ub_ref[:, width:]
    small_ref[8:9, :] = da_ref[...] + db_ref[...]


def output_kernel(
    info_ref, ha_ref, ma_ref, ma2_ref, hb_ref, mb_ref, mb2_ref, bias_ref, out_ref, rows_ref
):
    start = 0
    for group, (h_ref, m_ref, m2_ref) in enumerate(
        ((ha_ref, ma_ref, ma2_ref), (hb_ref, mb_ref, mb2_ref))
    ):
        live = (info_ref[2 + group] > 0).astype(F32)
        length = LENGTHS[group]
        value = h_ref[...] + live * (m_ref[...] + m2_ref[...] + bias_ref[...])
        rows_ref[start : start + length, :] = value[:length]
        start += length
    out_ref[...] = rows_ref[...].astype(BF16)


SMEM_SPEC = pl.BlockSpec(memory_space=pltpu.SMEM)


def whole(*shape):
    zeros = (0,) * len(shape)
    return pl.BlockSpec(shape, lambda *_: zeros)


def shaped(*shape, dtype=F32):
    return jax.ShapeDtypeStruct(shape, dtype)


def call(kernel, name, outs, flops, moved, exps=0, **kwargs):
    return pl.pallas_call(
        kernel,
        out_shape=outs,
        name=name,
        compiler_params=pltpu.CompilerParams(vmem_limit_bytes=VMEM_LIMIT),
        cost_estimate=pl.CostEstimate(
            flops=int(flops), bytes_accessed=int(moved), transcendentals=int(exps)
        ),
        **kwargs,
    )


def swap_sides(value):
    return lax.ppermute(value, "tensor", [(0, 1), (1, 0)])


def swap_bit(value, size, bit):
    return lax.ppermute(value, "dp", [(i, i ^ (1 << bit)) for i in range(size)])


def take(value, which):
    return lax.dynamic_index_in_dim(value, which, 0, keepdims=False)


def reduce_blocks(keep, send, size, index):
    bits = size.bit_length() - 1
    terms = [keep, swap_bit(send, size, 0)]
    for bit in range(1, bits):
        mine = (index >> bit) & 1
        halves = [t.reshape((2, t.shape[0] // 2) + t.shape[1:]) for t in terms]
        out = functools.reduce(jnp.add, [take(h, 1 - mine) for h in halves])
        terms = [take(h, mine) for h in halves]
        terms.append(swap_bit(out, size, bit))
    return functools.reduce(jnp.add, terms)[0]


def per_device(
    dp_size,
    images_in,
    small_counts,
    large_counts,
    norm1_gain,
    norm1_bias,
    qkv_weight,
    qv_bias,
    out_weight,
    out_bias,
    norm2_gain,
    norm2_bias,
    up_weight,
    up_bias,
    down_weight,
    down_bias,
    out_cotangent,
):
    width = images_in.shape[1]
    heads_width = out_weight.shape[0]
    units = down_weight.shape[0]
    index = lax.axis_index("dp")
    side = lax.axis_index("tensor")
    core = index & 1
    info = jnp.stack([side, core, small_counts[0], large_counts[0]]).astype(jnp.int32)
    row = lambda v: v.reshape(1, -1)

    half = heads_width // 2
    ow_send = lax.dynamic_slice_in_dim(out_weight, core * half, half, 0).astype(F32)
    ow_first = swap_sides(ow_send)
    ow_second = swap_bit(ow_first, dp_size, 0)

    def parts_of(array):
        pieces, at = [], 0
        for length, padded in zip(LENGTHS, PADDED):
            pieces.append(jnp.pad(array[at : at + length], ((0, padded - length), (0, 0))))
            at += length
        return pieces

    x_parts, ct_parts = parts_of(images_in), parts_of(out_cotangent)
    x_all = jnp.concatenate(x_parts, axis=0)
    weights = qkv_weight.transpose(1, 0, 2)
    total = sum(PADDED)
    head_count = heads_width // HEAD_DIM
    squares = sum(p * p for p in PADDED)
    outs = []
    for padded in PADDED:
        outs += [
            shaped(padded, width, dtype=BF16),
            shaped(3, padded, heads_width, dtype=BF16),
            shaped(padded, heads_width),
            shaped(head_count, padded),
        ]
    forward = call(
        forward_kernel, "attn_forward", tuple(outs),
        2 * total * width * 3 * heads_width + 4 * squares * heads_width, 8e6, squares * head_count,
    )(x_all, row(norm1_gain), row(norm1_bias), weights, qv_bias)
    firsts, qkvs, mixes, lses = (forward[i::4] for i in range(4))
    mixes2 = [swap_sides(m) for m in mixes]

    chunk = 512
    steps = units // chunk
    mlp = []
    for group, padded in enumerate(PADDED):
        blocks = lambda rows: pl.BlockSpec((rows, chunk), lambda i: (0, i))
        in_specs = [
            SMEM_SPEC, whole(padded, width), whole(padded, width), whole(padded, heads_width),
            whole(padded, heads_width), whole(heads_width, width), whole(half, width), whole(half, width),
            whole(1, width), whole(1, width), whole(1, width), blocks(width), blocks(1),
            pl.BlockSpec((chunk, width), lambda i: (i, 0)),
        ]
        mlp.append(
            call(
                functools.partial(mlp_kernel, group), "mlp_" + "ab"[group],
                (
                    shaped(padded, width), shaped(padded, width, dtype=BF16), shaped(padded, width, dtype=BF16),
                    shaped(padded, units, dtype=BF16), shaped(padded, units, dtype=BF16), shaped(padded, width),
                    shaped(1, units), shaped(1, width),
                ),
                2 * padded * width * (3 * units + 2 * heads_width), 12e6, padded * units,
                grid=(steps,), in_specs=in_specs,
                out_specs=(
                    whole(padded, width), whole(padded, width), whole(padded, width), blocks(padded),
                    blocks(padded), whole(padded, width), blocks(1), whole(1, width),
                ),
                scratch_shapes=[pltpu.VMEM((2 * heads_width, width), BF16), pltpu.VMEM((padded, 2 * heads_width), BF16)],
            )(
                info, x_parts[group], ct_parts[group], mixes[group], mixes2[group], out_weight, ow_first, ow_second,
                row(out_bias), row(norm2_gain), row(norm2_bias), up_weight, row(up_bias), down_weight,
            )
        )
    hidden, second, gmlp, act, gpre, gs, upsum, downsum = zip(*mlp)
    gs2 = [swap_sides(g) for g in gs]

    half_blocks, height = dp_size // 2, width // dp_size
    rows_spec = lambda n: [whole(p, n) for p in PADDED]
    cols_spec = lambda: [pl.BlockSpec((p, chunk), lambda i: (0, i)) for p in PADDED]
    grad_blocks = pl.BlockSpec((half_blocks, height, chunk), lambda i: (0, 0, i))
    keep_d, send_d, keep_u, send_u = call(
        mlp_weights_kernel, "mlp_weights", (shaped(half_blocks, height, units),) * 4,
        4 * total * width * units, 16e6, grid=(steps,),
        in_specs=[SMEM_SPEC, *rows_spec(width), *rows_spec(width), *cols_spec(), *cols_spec()],
        out_specs=(grad_blocks,) * 4,
        scratch_shapes=[pltpu.VMEM((width, chunk), F32)],
    )(info, *second, *gmlp, *act, *gpre)
    down_block = reduce_blocks(keep_d, send_d, dp_size, index)
    up_block = reduce_blocks(keep_u, send_u, dp_size, index)

    back = []
    for group, padded in enumerate(PADDED):
        back.append(
            call(
                functools.partial(backward_kernel, group), "attn_backward_" + "ab"[group],
                (
                    shaped(3, padded, heads_width, dtype=BF16), shaped(padded, width, dtype=BF16),
                    shaped(padded, width), shaped(padded, width), shaped(padded, width), shaped(8, width),
                ),
                2 * padded * width * (4 * heads_width + units) + 10 * padded * padded * heads_width, 10e6,
                padded * padded * head_count,
                in_specs=[SMEM_SPEC] + [pl.BlockSpec()] * 11,
                scratch_shapes=[pltpu.VMEM((padded, heads_width), BF16)],
            )(
                info, gs[group], gs2[group], hidden[group], ct_parts[group], row(norm2_gain), out_weight,
                qkvs[group], lses[group], weights, act[group], down_weight,
            )
        )
    dqkv, gattn, gh, gf, mlp_part, sums = zip(*back)
    gf2 = [swap_sides(g) for g in gf]
    mlp2 = [swap_sides(m) for m in mlp_part]

    keep_a, send_a = call(
        attn_weights_kernel, "attn_weights", (shaped(half_blocks, height, 4 * heads_width),) * 2,
        8 * total * width * heads_width, 8e6,
        in_specs=[SMEM_SPEC] + [pl.BlockSpec()] * 8,
        scratch_shapes=[pltpu.VMEM((width, heads_width), F32)],
    )(info, *firsts, *dqkv, *gattn, *mixes)
    attn_block = reduce_blocks(keep_a, send_a, dp_size, index)

    input_grad, small = call(
        input_kernel, "input_back", (shaped(*images_in.shape), shaped(16, width)), 30 * total * width, 8e6,
    )(
        x_parts[0], gf[0], gf2[0], gh[0], x_parts[1], gf[1], gf2[1], gh[1], row(norm1_gain),
        *sums, *upsum, *downsum,
    )
    block_out = call(
        output_kernel, "block_out", shaped(*images_in.shape, dtype=BF16), 5 * total * width, 6e6,
        in_specs=[SMEM_SPEC] + [pl.BlockSpec()] * 7,
        scratch_shapes=[pltpu.VMEM(images_in.shape, F32)],
    )(info, hidden[0], mlp_part[0], mlp2[0], hidden[1], mlp_part[1], mlp2[1], row(down_bias))
    for bit in range(dp_size.bit_length() - 1):
        small = small + swap_bit(small, dp_size, bit)

    return (
        block_out,
        input_grad,
        small[0],
        small[1],
        attn_block[:, : 3 * heads_width].reshape(height, 3, heads_width),
        small[5].reshape(2, heads_width),
        attn_block[:, 3 * heads_width :].T,
        small[4],
        small[2],
        small[3],
        up_block,
        small[6:8].reshape(-1),
        down_block.T,
        small[8],
    )


def solution(mesh):
    placed = (
        P("dp", None),
        P("dp"),
        P("dp"),
        P(),
        P(),
        P(None, None, "tensor"),
        P(None, "tensor"),
        P("tensor", None),
        P(),
        P(),
        P(),
        P(None, "tensor"),
        P("tensor"),
        P("tensor", None),
        P(),
        P("dp", None),
    )
    return jax.shard_map(
        functools.partial(per_device, mesh.shape["dp"]),
        mesh=mesh,
        in_specs=placed,
        out_specs=(
            P("dp", None),
            P("dp", None),
            P(),
            P(),
            P("dp", None, "tensor"),
            P(None, "tensor"),
            P("tensor", "dp"),
            P(),
            P(),
            P(),
            P("dp", "tensor"),
            P("tensor"),
            P("tensor", "dp"),
            P(),
        ),
        check_vma=False,
    )
```

time: 574 us -> 262 us (0.46)
  waiting for transfers between devices: 390 us -> 119 us
  Pallas kernels: 0 us -> 68.9 us
  blocking collectives: 62 us -> 0 us
  matrix products: 57 us -> 0 us
  starting transfers between devices: 0.95 us -> 27.6 us
  between operations: 16.2 us -> 2.22 us
  local copies, waits for them, and re-layouts: 26.4 us -> 13.3 us
  other arithmetic: 20.9 us -> 30.9 us
    reduce_scatter x4 -> x0, waiting for transfers between devices: 223 us -> none  [the longest x1 79.6 us: per_device(): lax.psum_scatter(down_weight_grad, 'dp', scatter_dimension=1, tiled=True)]
    psum x3 -> x0, waiting for transfers between devices: 167 us -> none  [the longest x1 65.3 us: per_device(): mlp_branch = lax.psum(mlp_part, 'tensor') + down_bias]
    ppermute x0 -> x26, waiting for transfers between devices: none -> 119 us  [the longest x9 72.6 us: swap_sides(): return lax.ppermute(value, 'tensor', [(0, 1), (1, 0)])]
    pallas_call x0 -> x9, Pallas kernels: none -> 68.9 us  [the longest x2 18.9 us: per_device(): call(functools.partial(backward_kernel, group), 'attn_backward_' + 'ab'[g...]
    psum x1 -> x0, blocking collectives: 62 us -> none  [per_device(): lax.psum((norm1_gain_grad, norm1_bias_grad, qv_bias_grad, out_bias_grad,...]
    dot_general x24 -> x0, matrix products: 57 us -> none  [the longest x1 9.13 us: per_device(): jnp.dot(second_low, up_weight, preferred_element_type=jnp.float32) + up_bias]
    ppermute x0 -> x26, starting transfers between devices: none -> 27.6 us  [the longest x17 15.8 us: swap_bit(): return lax.ppermute(value, 'dp', [(i, i ^ 1 << bit) for i in range(size)])]
    slice x17 -> x5, local copies, waits for them, and re-layouts: 16.5 us -> 0.91 us  [the longest x1 0.65 us: per_device(): small[8]]
  transfers between devices with their start and end apart: 7 -> 26, of which waited for: 6 -> 11; matrix products, arithmetic and copies ran while one was open for 6% -> 14% of each run, Pallas kernels for 0% -> 26%
where the time goes in v1:
time: 262 us
  waiting for transfers between devices  119 us (45%)
  Pallas kernels  68.9 us (26%)
  other arithmetic  30.9 us (12%)
  starting transfers between devices  27.6 us (11%)
  local copies, waits for them, and re-layouts  13.3 us (5%)
    ppermute x9, waiting for transfers between devices, swap_sides(): return lax.ppermute(value, 'tensor', [(0, 1), (1, 0)])  72.6 us
    ppermute x17, waiting for transfers between devices, swap_bit(): return lax.ppermute(value, 'dp', [(i, i ^ 1 << bit) for i in range(size)])  46.1 us
    pallas_call x2, Pallas kernels, per_device(): call(functools.partial(backward_kernel, group), 'attn_backward_' + 'ab'[g...  18.9 us
    pallas_call x2, Pallas kernels, per_device(): call(functools.partial(mlp_kernel, group), 'mlp_' + 'ab'[group], (shaped(...  17.9 us
    ppermute x17, starting transfers between devices, swap_bit(): return lax.ppermute(value, 'dp', [(i, i ^ 1 << bit) for i in range(size)])  15.8 us
    ppermute x9, starting transfers between devices, swap_sides(): return lax.ppermute(value, 'tensor', [(0, 1), (1, 0)])  11.8 us
    dynamic_slice x3, other arithmetic, take(): return lax.dynamic_index_in_dim(value, which, 0, keepdims=False)  10.4 us
    add x6, other arithmetic, reduce_blocks(): out = functools.reduce(jnp.add, [take(h, 1 - mine) for h in halves])  8.97 us
  transfers between devices with their start and end apart: 26, of which 11 were waited for; matrix products, arithmetic and copies ran while one was open for 14% of the time, Pallas kernels for 26%

profile of v1, /device:TPU:0, one launch (start us, length us, event | category | flops | bytes accessed | tf_op | source)
XLA Modules:
  0.0 261.5 jit_solution(96471400986850822)
XLA Ops:
  1.8 3.0 %collective-permute-start.1 = (f32[192,768]{1,0:T(8,128)S(1)}, f32[192,768]{1,0:T(8,128)}, u32[]{:S(2)}, u32[]{:S(2)}) collective-permute-start(f32[192,768]{1,0:T(8,128)S(1)} %dynamic-slice_convert_fusion), channel_id=1, source_target_pairs={{0,1},{1,0},{2,3},{3,2},{4,5},{5,4},{6,7},{7,6},{8,9},{9,8},{10,11... | collective-permute-start | bytes 1769480 | tf_op jit(solution)/shard_map/ppermute | solution.py:292
  8.1 10.1 %collective-permute-done.1.ow1_ref = f32[192,768]{1,0:T(8,128)} collective-permute-done((f32[192,768]{1,0:T(8,128)S(1)}, f32[192,768]{1,0:T(8,128)}, u32[]{:S(2)}, u32[]{:S(2)}) %collective-permute-start.1) | collective-permute-done | bytes 589856 | tf_op jit(solution)/shard_map/ppermute | solution.py:292
  18.3 7.9 %attn_forward.1 = (bf16[208,768]{1,0:T(8,128)(2,1)}, bf16[3,208,384]{2,1,0:T(8,128)(2,1)}, f32[208,384]{1,0:T(8,128)}, f32[6,208]{1,0:T(8,128)}, bf16[336,768]{1...) custom-call(bf16[544,768]{1,0:T(8,128)(2,1)} %pad_maximum_fusion.x_ref, ...), custom_call_target="tpu_custom_call" | custom-call | flops 1202454528 | bytes 8000000 | tf_op jit(solution)/shard_map/attn_forward/pallas_call | solution.py:369
  33.4 7.5 %collective-permute-done.5.mix2_ref = f32[336,384]{1,0:T(8,128)S(1)} collective-permute-done((f32[336,384]{1,0:T(8,128)}, f32[336,384]{1,0:T(8,128)S(1)}, u32[]{:S(2)}, u32[]{:S(2)}) %collective-permute-start.5) | collective-permute-done | bytes 516128 | tf_op jit(solution)/shard_map/ppermute | solution.py:292
  42.7 9.7 %mlp_b.1 = (f32[336,768]{1,0:T(8,128)}, bf16[336,768]{1,0:T(8,128)(2,1)}, bf16[336,768]{1,0:T(8,128)(2,1)}, bf16[336,1536]{1,0:T(8,128)(2,1)}, bf16[336,1536]{1,...) custom-call(s32[4]{0:T(128)} %pad_add_fusion.info_ref, bf16[336,768]{1,0:T(8,128)(2,1)} %copy-done.3, ...), custom_call_target="tpu_custom_call" | custom-call | flops 2774532096 | bytes 12000000 | tf_op jit(solution)/shard_map/mlp_b/pallas_call | solution.py:388
  54.9 8.2 %mlp_a.1 = (f32[208,768]{1,0:T(8,128)}, bf16[208,768]{1,0:T(8,128)(2,1)}, bf16[208,768]{1,0:T(8,128)(2,1)}, bf16[208,1536]{1,0:T(8,128)(2,1)}, bf16[208,1536]{1,...) custom-call(s32[4]{0:T(128)} %pad_add_fusion.info_ref, bf16[208,768]{1,0:T(8,128)(2,1)} %copy-done, ...), custom_call_target="tpu_custom_call" | custom-call | flops 1717567488 | bytes 12000000 | tf_op jit(solution)/shard_map/mlp_a/pallas_call | solution.py:388
  63.1 8.1 %mlp_weights.1 = (f32[8,48,1536]{2,1,0:T(8,128)}, f32[8,48,1536]{2,1,0:T(8,128)}, f32[8,48,1536]{2,1,0:T(8,128)}, f32[8,48,1536]{2,1,0:T(8,128)}) custom-call(s32[4]{0:T(128)} %pad_add_fusion.info_ref, bf16[208,768]{1,0:T(8,128)(2,1)} %get-tuple-element.92.seca_ref, bf16[336,768]{1,0:T(8,128)(2,1)} %get-tuple-element.93.secb_ref, ...), custom_call_target="tpu_custom_call" | custom-call | flops 2566914048 | bytes 16000000 | tf_op jit(solution)/shard_map/mlp_weights/pallas_call | solution.py:414
  71.8 18.6 %collective-permute-done.3.gs2_ref = f32[208,768]{1,0:T(8,128)S(1)} collective-permute-done((f32[208,768]{1,0:T(8,128)S(1)}, f32[208,768]{1,0:T(8,128)S(1)}, u32[]{:S(2)}, u32[]{:S(2)}) %collective-permute-start.3) | collective-permute-done | bytes 639008 | tf_op jit(solution)/shard_map/ppermute | solution.py:292
  91.2 8.0 %attn_backward_a.1 = (bf16[3,208,384]{2,1,0:T(8,128)(2,1)}, bf16[208,768]{1,0:T(8,128)(2,1)}, f32[208,768]{1,0:T(8,128)}, f32[208,768]{1,0:T(8,128)}, f32[208,768]{1,0:T(8,128)}, /*index=5*/f32[8,768]{1,0:T(8,128)}) custom-call(s32[4]{0:T(128)} %pad_add_fusion.info_ref, f32[208,768]{1,0:T(8,128)} %get-tuple-element.60.gs_ref, f32[208,768]{1,0:T(8,128)} %copy-done.11, ...), custom_call_target="tpu_custom_call" | custom-call | flops 1147600896 | bytes 10000000 | tf_op jit(solution)/shard_map/attn_backward_a/pallas_call | solution.py:427
  100.2 11.0 %attn_backward_b.1 = (bf16[3,336,384]{2,1,0:T(8,128)(2,1)}, bf16[336,768]{1,0:T(8,128)(2,1)}, f32[336,768]{1,0:T(8,128)}, f32[336,768]{1,0:T(8,128)}, f32[336,768]{1,0:T(8,128)}, /*index=5*/f32[8,768]{1,0:T(8,128)}) custom-call(s32[4]{0:T(128)} %pad_add_fusion.info_ref, f32[336,768]{1,0:T(8,128)} %get-tuple-element.67.gs_ref, f32[336,768]{1,0:T(8,128)} %copy-done.7, ...), custom_call_target="tpu_custom_call" | custom-call | flops 2018967552 | bytes 10000000 | tf_op jit(solution)/shard_map/attn_backward_b/pallas_call | solution.py:427
  111.1 6.8 %attn_weights.1 = (f32[8,48,1536]{2,1,0:T(8,128)}, f32[8,48,1536]{2,1,0:T(8,128)}) custom-call(s32[4]{0:T(128)} %pad_add_fusion.info_ref, bf16[208,768]{1,0:T(8,128)(2,1)} %get-tuple-element.84.firsta_ref, bf16[336,768]{1,0:T(8,128)(2,1)} %get-tuple-element.85.firstb_ref, bf16[3,208,384]{2,1,0:T(8,128)(2,1)} %get-tuple-element.86.da_ref, ...), custom_call_target="tpu_custom_call" | custom-call | flops 1283457024 | bytes 8000000 | tf_op jit(solution)/shard_map/attn_weights/pallas_call | solution.py:446
  119.9 3.6 %constant_dynamic-slice_fusion.2 = (f32[1,4,48,1536]{3,2,1,0:T(8,128)S(1)}, f32[4,48,1536]{2,1,0:T(8,128)}, f32[1,4,48,1536]{3,2,1,0:T(8,128)}) fusion(f32[2,4,48,1536]{3,2,1,0:T(8,128)S(1)} %bitcast.91, s32[]{:T(128)S(6)} %select_n.79, f32[2,4,48,1536]{3,2,1,0:T(8,128)} %bitcast.16, s32[]{:T(128)S(6)} %select_n.84), kind=kLoop, calls=%fused_computation.26 | loop fusion | flops 294912 | bytes 8257544 | tf_op jit(solution)/shard_map/jit(dynamic_index_in_dim)/dynamic_slice | solution.py:300
  125.3 3.3 %constant_dynamic-slice_fusion = (f32[1,4,48,1536]{3,2,1,0:T(8,128)S(1)}, f32[4,48,1536]{2,1,0:T(8,128)}, f32[1,4,48,1536]{3,2,1,0:T(8,128)S(1)}) fusion(f32[2,4,48,1536]{3,2,1,0:T(8,128)S(1)} %bitcast.90, s32[]{:T(128)S(6)} %select_n.79, f32[2,4,48,1536]{3,2,1,0:T(8,128)} %bitcast.26, s32[]{:T(128)S(6)} %select_n.84), kind=kLoop, calls=%fused_computation.24 | loop fusion | flops 294912 | bytes 8257544 | tf_op jit(solution)/shard_map/jit(dynamic_index_in_dim)/dynamic_slice | solution.py:300
  128.9 28.2 %collective-permute-done.8.gfa2_ref = f32[208,768]{1,0:T(8,128)S(1)} collective-permute-done((f32[208,768]{1,0:T(8,128)}, f32[208,768]{1,0:T(8,128)S(1)}, u32[]{:S(2)}, u32[]{:S(2)}) %collective-permute-start.8) | collective-permute-done | bytes 639008 | tf_op jit(solution)/shard_map/ppermute | solution.py:292
  158.8 5.4 %input_back.1 = (f32[522,768]{1,0:T(8,128)}, f32[16,768]{1,0:T(8,128)}) custom-call(bf16[208,768]{1,0:T(8,128)(2,1)} %copy-done, f32[208,768]{1,0:T(8,128)} %get-tuple-element.72.gfa_ref, f32[208,768]{1,0:T(8,128)} %copy-done.12, f32[208,768]{1,0:T(8,128)} %get-tuple-element.73.gha_ref, bf16[336,768]{1,0:T(8,128)(2,1)} %copy-done.3, ...), custom_call_target="tpu_custom_call" | custom-call | flops 12533760 | bytes 8000000 | tf_op jit(solution)/shard_map/input_back/pallas_call | solution.py:454
  168.8 3.5 %constant_dynamic-slice_fusion.5 = (f32[1,4,48,1536]{3,2,1,0:T(8,128)}, f32[4,48,1536]{2,1,0:T(8,128)}, f32[1,4,48,1536]{3,2,1,0:T(8,128)}) fusion(f32[2,4,48,1536]{3,2,1,0:T(8,128)S(1)} %bitcast.89, s32[]{:T(128)S(6)} %select_n.79, f32[2,4,48,1536]{3,2,1,0:T(8,128)} %bitcast.5, s32[]{:T(128)S(6)} %select_n.84), kind=kLoop, calls=%fused_computation.29 | loop fusion | flops 294912 | bytes 8257544 | tf_op jit(solution)/shard_map/jit(dynamic_index_in_dim)/dynamic_slice | solution.py:300
  172.3 5.6 %collective-permute-done.11 = f32[16,768]{1,0:T(8,128)S(1)} collective-permute-done((f32[16,768]{1,0:T(8,128)S(1)}, f32[16,768]{1,0:T(8,128)S(1)}, u32[]{:S(2)}, u32[]{:S(2)}) %collective-permute-start.11) | collective-permute-done | bytes 49184 | tf_op jit(solution)/shard_map/ppermute | solution.py:296
  182.8 2.2 add_bitcast_fusion.4
  187.5 8.1 %collective-permute-done.4.ma2_ref = f32[208,768]{1,0:T(8,128)} collective-permute-done((f32[208,768]{1,0:T(8,128)}, f32[208,768]{1,0:T(8,128)}, u32[]{:S(2)}, u32[]{:S(2)}) %collective-permute-start.4) | collective-permute-done | bytes 639008 | tf_op jit(solution)/shard_map/ppermute | solution.py:292
  195.6 2.8 %collective-permute-start.13 = (f32[16,768]{1,0:T(8,128)}, f32[16,768]{1,0:T(8,128)}, u32[]{:S(2)}, u32[]{:S(2)}) collective-permute-start(f32[16,768]{1,0:T(8,128)} %add.409), channel_id=1, source_target_pairs={{0,16},{2,18},{4,20},{6,22},{8,24},{10,26},{12,28},{14,30},{16,0},... | collective-permute-start | bytes 147464 | tf_op jit(solution)/shard_map/ppermute | solution.py:296
  199.0 3.9 %block_out.1 = bf16[522,768]{1,0:T(8,128)(2,1)} custom-call(s32[4]{0:T(128)} %pad_add_fusion.info_ref, f32[208,768]{1,0:T(8,128)} %get-tuple-element.59.hidden_ref.ha_ref, f32[208,768]{1,0:T(8,128)} %get-tuple-element.64.ma_ref, f32[208,768]{1,0:T(8,128)} %collective-permute-done.4.ma2_ref, f32[336,768]{1,0:T(8,128)} %get-tuple-element.66.hidden_ref.hb_ref, ...), custom_call_target="tpu_custom_call" | custom-call | flops 2088960 | bytes 6000000 | tf_op jit(solution)/shard_map/block_out/pallas_call | solution.py:460
  213.2 15.4 %collective-permute-done.24 = f32[2,48,1536]{2,1,0:T(8,128)} collective-permute-done((f32[2,48,1536]{2,1,0:T(8,128)}, f32[2,48,1536]{2,1,0:T(8,128)}, u32[]{:S(2)}, u32[]{:S(2)}) %collective-permute-start.24) | collective-permute-done | bytes 589856 | tf_op jit(solution)/shard_map/ppermute | solution.py:296
  232.9 12.2 %collective-permute-done.16 = f32[2,48,1536]{2,1,0:T(8,128)S(1)} collective-permute-done((f32[2,48,1536]{2,1,0:T(8,128)S(1)}, f32[2,48,1536]{2,1,0:T(8,128)S(1)}, u32[]{:S(2)}, u32[]{:S(2)}) %collective-permute-start.16) | collective-permute-done | bytes 589856 | tf_op jit(solution)/shard_map/ppermute | solution.py:296
  248.1 11.0 %collective-permute-done.17 = f32[1,48,1536]{2,1,0:T(8,128)S(1)} collective-permute-done((f32[1,48,1536]{2,1,0:T(8,128)S(1)}, f32[1,48,1536]{2,1,0:T(8,128)S(1)}, u32[]{:S(2)}, u32[]{:S(2)}) %collective-permute-start.17) | collective-permute-done | bytes 294944 | tf_op jit(solution)/shard_map/ppermute | solution.py:296
  (127 shorter events, 55.0 us)
Async XLA Ops:
  1.8 16.5 %collective-permute-start.1 = (f32[192,768]{1,0:T(8,128)S(1)}, f32[192,768]{1,0:T(8,128)}, u32[]{:S(2)}, u32[]{:S(2)}) collective-permute-start(f32[192,768]{1,0:T(8,128)S(1)} %dynamic-slice_convert_fusion), channel_id=1, source_target_pairs={{0,1},{1,0},{2,3},{3,2},{4,5},{5,4},{6,7},{7,6},{8,9},{9,8},{10,11... | collective-permute-start | bytes 1769480 | tf_op jit(solution)/shard_map/ppermute | solution.py:292
  18.2 22.7 %collective-permute-start.2 = (f32[192,768]{1,0:T(8,128)}, f32[192,768]{1,0:T(8,128)S(1)}, u32[]{:S(2)}, u32[]{:S(2)}) collective-permute-start(f32[192,768]{1,0:T(8,128)} %collective-permute-done.1.ow1_ref), channel_id=1, source_target_pairs={{0,2},{2,0},{4,6},{6,4},{8,10},{10,8},{12,14},{14,12},{16,18},{18,... | collective-permute-start | bytes 1769480 | tf_op jit(solution)/shard_map/ppermute | solution.py:296
  26.2 14.8 %collective-permute-start.5 = (f32[336,384]{1,0:T(8,128)}, f32[336,384]{1,0:T(8,128)S(1)}, u32[]{:S(2)}, u32[]{:S(2)}) collective-permute-start(f32[336,384]{1,0:T(8,128)} %get-tuple-element.65.mix_ref.mixb_ref), channel_id=1, source_target_pairs={{0,1},{1,0},{2,3},{3,2},{4,5},{5,4},{6,7},{7,6},{8,9},{9,8},{10,11... | collective-permute-start | bytes 1548296 | tf_op jit(solution)/shard_map/ppermute | solution.py:292
  28.0 26.2 %collective-permute-start = (f32[208,384]{1,0:T(8,128)}, f32[208,384]{1,0:T(8,128)S(1)}, u32[]{:S(2)}, u32[]{:S(2)}) collective-permute-start(f32[208,384]{1,0:T(8,128)} %get-tuple-element.58.mix_ref.mixa_ref), channel_id=1, source_target_pairs={{0,1},{1,0},{2,3},{3,2},{4,5},{5,4},{6,7},{7,6},{8,9},{9,8},{10,11... | collective-permute-start | bytes 958472 | tf_op jit(solution)/shard_map/ppermute | solution.py:292
  52.4 46.8 %collective-permute-start.6 = (f32[336,768]{1,0:T(8,128)}, f32[336,768]{1,0:T(8,128)S(1)}, u32[]{:S(2)}, u32[]{:S(2)}) collective-permute-start(f32[336,768]{1,0:T(8,128)} %get-tuple-element.67.gs_ref), channel_id=1, source_target_pairs={{0,1},{1,0},{2,3},{3,2},{4,5},{5,4},{6,7},{7,6},{8,9},{9,8},{10,11... | collective-permute-start | bytes 3096584 | tf_op jit(solution)/shard_map/ppermute | solution.py:292
  71.2 48.8 %collective-permute-start.18 = (f32[8,48,1536]{2,1,0:T(8,128)}, f32[8,48,1536]{2,1,0:T(8,128)}, u32[]{:S(2)}, u32[]{:S(2)}) collective-permute-start(f32[8,48,1536]{2,1,0:T(8,128)} %get-tuple-element.99), channel_id=1, source_target_pairs={{0,2},{2,0},{4,6},{6,4},{8,10},{10,8},{12,14},{14,12},{16,18},{18,... | collective-permute-start | bytes 7077896 | tf_op jit(solution)/shard_map/ppermute | solution.py:296
  71.3 19.1 %collective-permute-start.3 = (f32[208,768]{1,0:T(8,128)S(1)}, f32[208,768]{1,0:T(8,128)S(1)}, u32[]{:S(2)}, u32[]{:S(2)}) collective-permute-start(f32[208,768]{1,0:T(8,128)S(1)} %copy-done.10), channel_id=1, source_target_pairs={{0,1},{1,0},{2,3},{3,2},{4,5},{5,4},{6,7},{7,6},{8,9},{9,8},{10,11... | collective-permute-start | bytes 1916936 | tf_op jit(solution)/shard_map/ppermute | solution.py:292
  71.6 53.7 %collective-permute-start.22 = (f32[8,48,1536]{2,1,0:T(8,128)}, f32[8,48,1536]{2,1,0:T(8,128)}, u32[]{:S(2)}, u32[]{:S(2)}) collective-permute-start(f32[8,48,1536]{2,1,0:T(8,128)} %get-tuple-element.101), channel_id=1, source_target_pairs={{0,2},{2,0},{4,6},{6,4},{8,10},{10,8},{12,14},{14,12},{16,18},{18,... | collective-permute-start | bytes 7077896 | tf_op jit(solution)/shard_map/ppermute | solution.py:296
  117.9 49.3 %collective-permute-start.14 = (f32[8,48,1536]{2,1,0:T(8,128)}, f32[8,48,1536]{2,1,0:T(8,128)}, u32[]{:S(2)}, u32[]{:S(2)}) collective-permute-start(f32[8,48,1536]{2,1,0:T(8,128)} %get-tuple-element.91), channel_id=1, source_target_pairs={{0,2},{2,0},{4,6},{6,4},{8,10},{10,8},{12,14},{14,12},{16,18},{18,... | collective-permute-start | bytes 7077896 | tf_op jit(solution)/shard_map/ppermute | solution.py:296
  117.9 40.9 %collective-permute-start.9 = (f32[336,768]{1,0:T(8,128)}, f32[336,768]{1,0:T(8,128)}, u32[]{:S(2)}, u32[]{:S(2)}) collective-permute-start(f32[336,768]{1,0:T(8,128)} %get-tuple-element.74.gfb_ref), channel_id=1, source_target_pairs={{0,1},{1,0},{2,3},{3,2},{4,5},{5,4},{6,7},{7,6},{8,9},{9,8},{10,11... | collective-permute-start | bytes 3096584 | tf_op jit(solution)/shard_map/ppermute | solution.py:292
  119.6 37.4 %collective-permute-start.8 = (f32[208,768]{1,0:T(8,128)}, f32[208,768]{1,0:T(8,128)S(1)}, u32[]{:S(2)}, u32[]{:S(2)}) collective-permute-start(f32[208,768]{1,0:T(8,128)} %get-tuple-element.72.gfa_ref), channel_id=1, source_target_pairs={{0,1},{1,0},{2,3},{3,2},{4,5},{5,4},{6,7},{7,6},{8,9},{9,8},{10,11... | collective-permute-start | bytes 1916936 | tf_op jit(solution)/shard_map/ppermute | solution.py:292
  123.6 57.5 %collective-permute-start.19 = (f32[4,48,1536]{2,1,0:T(8,128)}, f32[4,48,1536]{2,1,0:T(8,128)}, u32[]{:S(2)}, u32[]{:S(2)}) collective-permute-start(f32[4,48,1536]{2,1,0:T(8,128)} %get-tuple-element.127), channel_id=1, source_target_pairs={{0,4},{2,6},{4,0},{6,2},{8,12},{10,14},{12,8},{14,10},{16,20},{18,... | collective-permute-start | bytes 3538952 | tf_op jit(solution)/shard_map/ppermute | solution.py:296
  128.6 75.2 %collective-permute-start.23 = (f32[4,48,1536]{2,1,0:T(8,128)}, f32[4,48,1536]{2,1,0:T(8,128)}, u32[]{:S(2)}, u32[]{:S(2)}) collective-permute-start(f32[4,48,1536]{2,1,0:T(8,128)} %get-tuple-element.124), channel_id=1, source_target_pairs={{0,4},{2,6},{4,0},{6,2},{8,12},{10,14},{12,8},{14,10},{16,20},{18,... | collective-permute-start | bytes 3538952 | tf_op jit(solution)/shard_map/ppermute | solution.py:296
  157.0 42.0 %collective-permute-start.7 = (f32[336,768]{1,0:T(8,128)}, f32[336,768]{1,0:T(8,128)}, u32[]{:S(2)}, u32[]{:S(2)}) collective-permute-start(f32[336,768]{1,0:T(8,128)} %get-tuple-element.71.mb_ref), channel_id=1, source_target_pairs={{0,1},{1,0},{2,3},{3,2},{4,5},{5,4},{6,7},{7,6},{8,9},{9,8},{10,11... | collective-permute-start | bytes 3096584 | tf_op jit(solution)/shard_map/ppermute | solution.py:292
  165.6 30.0 %collective-permute-start.4 = (f32[208,768]{1,0:T(8,128)}, f32[208,768]{1,0:T(8,128)}, u32[]{:S(2)}, u32[]{:S(2)}) collective-permute-start(f32[208,768]{1,0:T(8,128)} %get-tuple-element.64.ma_ref), channel_id=1, source_target_pairs={{0,1},{1,0},{2,3},{3,2},{4,5},{5,4},{6,7},{7,6},{8,9},{9,8},{10,11... | collective-permute-start | bytes 1916936 | tf_op jit(solution)/shard_map/ppermute | solution.py:292
  167.2 10.7 %collective-permute-start.11 = (f32[16,768]{1,0:T(8,128)S(1)}, f32[16,768]{1,0:T(8,128)S(1)}, u32[]{:S(2)}, u32[]{:S(2)}) collective-permute-start(f32[16,768]{1,0:T(8,128)S(1)} %add.407), channel_id=1, source_target_pairs={{0,4},{2,6},{4,0},{6,2},{8,12},{10,14},{12,8},{14,10},{16,20},{18,... | collective-permute-start | bytes 147464 | tf_op jit(solution)/shard_map/ppermute | solution.py:296
  178.6 33.1 %collective-permute-start.15 = (f32[4,48,1536]{2,1,0:T(8,128)}, f32[4,48,1536]{2,1,0:T(8,128)}, u32[]{:S(2)}, u32[]{:S(2)}) collective-permute-start(f32[4,48,1536]{2,1,0:T(8,128)} %get-tuple-element.130), channel_id=1, source_target_pairs={{0,4},{2,6},{4,0},{6,2},{8,12},{10,14},{12,8},{14,10},{16,20},{18,... | collective-permute-start | bytes 3538952 | tf_op jit(solution)/shard_map/ppermute | solution.py:296
  185.3 23.9 %collective-permute-start.20 = (f32[2,48,1536]{2,1,0:T(8,128)}, f32[2,48,1536]{2,1,0:T(8,128)}, u32[]{:S(2)}, u32[]{:S(2)}) collective-permute-start(f32[2,48,1536]{2,1,0:T(8,128)} %add_bitcast_fusion.4), channel_id=1, source_target_pairs={{0,8},{2,10},{4,12},{6,14},{8,0},{10,2},{12,4},{14,6},{16,24},{18,... | collective-permute-start | bytes 1769480 | tf_op jit(solution)/shard_map/ppermute | solution.py:296
  195.6 7.3 %collective-permute-start.13 = (f32[16,768]{1,0:T(8,128)}, f32[16,768]{1,0:T(8,128)}, u32[]{:S(2)}, u32[]{:S(2)}) collective-permute-start(f32[16,768]{1,0:T(8,128)} %add.409), channel_id=1, source_target_pairs={{0,16},{2,18},{4,20},{6,22},{8,24},{10,26},{12,28},{14,30},{16,0},... | collective-permute-start | bytes 147464 | tf_op jit(solution)/shard_map/ppermute | solution.py:296
  205.8 22.9 %collective-permute-start.24 = (f32[2,48,1536]{2,1,0:T(8,128)}, f32[2,48,1536]{2,1,0:T(8,128)}, u32[]{:S(2)}, u32[]{:S(2)}) collective-permute-start(f32[2,48,1536]{2,1,0:T(8,128)} %add_bitcast_fusion.3), channel_id=1, source_target_pairs={{0,8},{2,10},{4,12},{6,14},{8,0},{10,2},{12,4},{14,6},{16,24},{18,... | collective-permute-start | bytes 1769480 | tf_op jit(solution)/shard_map/ppermute | solution.py:296
  210.5 20.5 %collective-permute-start.21 = (f32[1,48,1536]{2,1,0:T(8,128)S(1)}, f32[1,48,1536]{2,1,0:T(8,128)S(1)}, u32[]{:S(2)}, u32[]{:S(2)}) collective-permute-start(f32[1,48,1536]{2,1,0:T(8,128)S(1)} %bitcast_add_fusion.2), channel_id=1, source_target_pairs={{0,16},{2,18},{4,20},{6,22},{8,24},{10,26},{12,28},{14,30},{16,0},... | collective-permute-start | bytes 884744 | tf_op jit(solution)/shard_map/ppermute | solution.py:296
  213.1 32.1 %collective-permute-start.16 = (f32[2,48,1536]{2,1,0:T(8,128)S(1)}, f32[2,48,1536]{2,1,0:T(8,128)S(1)}, u32[]{:S(2)}, u32[]{:S(2)}) collective-permute-start(f32[2,48,1536]{2,1,0:T(8,128)S(1)} %add_bitcast_fusion.5), channel_id=1, source_target_pairs={{0,8},{2,10},{4,12},{6,14},{8,0},{10,2},{12,4},{14,6},{16,24},{18,... | collective-permute-start | bytes 1769480 | tf_op jit(solution)/shard_map/ppermute | solution.py:296
  229.8 16.5 %collective-permute-start.25 = (f32[1,48,1536]{2,1,0:T(8,128)S(1)}, f32[1,48,1536]{2,1,0:T(8,128)S(1)}, u32[]{:S(2)}, u32[]{:S(2)}) collective-permute-start(f32[1,48,1536]{2,1,0:T(8,128)S(1)} %bitcast_add_fusion), channel_id=1, source_target_pairs={{0,16},{2,18},{4,20},{6,22},{8,24},{10,26},{12,28},{14,30},{16,0},... | collective-permute-start | bytes 884744 | tf_op jit(solution)/shard_map/ppermute | solution.py:296
  246.2 12.9 %collective-permute-start.17 = (f32[1,48,1536]{2,1,0:T(8,128)S(1)}, f32[1,48,1536]{2,1,0:T(8,128)S(1)}, u32[]{:S(2)}, u32[]{:S(2)}) collective-permute-start(f32[1,48,1536]{2,1,0:T(8,128)S(1)} %bitcast_add_fusion.4), channel_id=1, source_target_pairs={{0,16},{2,18},{4,20},{6,22},{8,24},{10,26},{12,28},{14,30},{16,0},... | collective-permute-start | bytes 884744 | tf_op jit(solution)/shard_map/ppermute | solution.py:296
  (28 other events, 175.6 us)

commit v2 on v0

v2 whole, which is shorter than its diff:
```python
import functools

import jax
import jax.numpy as jnp
from jax import lax
from jax.experimental import pallas as pl
from jax.experimental.pallas import tpu as pltpu
from jax.sharding import PartitionSpec as P

HEAD_DIM = 64
PAIR = 2 * HEAD_DIM
LENGTHS = (197, 325)
PADDED = tuple(-(-length // 16) * 16 for length in LENGTHS)
SENT = tuple(-(-length // 8) * 8 for length in LENGTHS)
STARTS = (0, PADDED[0])
SENT_STARTS = (0, SENT[0])
ROWS = sum(PADDED)
SENT_ROWS = sum(SENT)
NORM_EPS = 1e-06
F32 = jnp.float32
BF16 = jnp.bfloat16
MIB = 1024 * 1024
NT = ((1,), (1,))
TN = ((0,), (0,))


def norm_parts(values):
    row_mean = jnp.mean(values, axis=-1, keepdims=True)
    centered = values - row_mean
    variance = jnp.mean(centered * centered, axis=-1, keepdims=True)
    inverse = lax.rsqrt(variance + NORM_EPS)
    return (centered * inverse, inverse)


def norm_back(grad, normed, inverse, gain):
    scaled = grad * gain
    row_inner = jnp.mean(scaled, axis=-1, keepdims=True)
    row_cross = jnp.mean(scaled * normed, axis=-1, keepdims=True)
    return inverse * (scaled - row_inner - normed * row_cross)


def mm(left, right, dims=((1,), (0,))):
    return lax.dot_general(left, right, (dims, ((), ())), preferred_element_type=F32)


def col_sum(values):
    return jnp.sum(values, axis=0, keepdims=True)


def row(ref):
    return ref[...].reshape(1, -1)


def low_lanes(rows):
    return lax.broadcasted_iota(jnp.int32, (rows, PAIR), 1) < HEAD_DIM


def key_mask(padded, length):
    return lax.broadcasted_iota(jnp.int32, (padded, padded), 0) < length


def of_group(group):
    return slice(STARTS[group], STARTS[group] + PADDED[group])


def sent_of(group):
    return slice(SENT_STARTS[group], SENT_STARTS[group] + SENT[group])


def filled(rows, padded):
    return jnp.concatenate([rows, jnp.zeros((padded - rows.shape[0], rows.shape[1]), rows.dtype)], axis=0)


def live_of(info_ref, group):
    return (info_ref[2 + group] > 0).astype(F32)


def forward_kernel(
    info_ref, x_ref, ct_ref, gain_ref, bias_ref, w_ref, qvb_ref,
    first_ref, qkv_ref, xpad_ref, ctpad_ref, lse0_ref, lse1_ref, mix0_ref, mix1_ref, wide,
):
    scaling = HEAD_DIM ** (-0.5)
    for source, target in ((ct_ref, ctpad_ref), (x_ref, xpad_ref)):
        wide[: source.shape[0], :] = source[...].astype(F32)
        start = 0
        for group in range(2):
            rows, length = PADDED[group], LENGTHS[group]
            real = lax.broadcasted_iota(jnp.int32, (rows, x_ref.shape[1]), 0) < length
            piece = jnp.where(real, wide[start : start + rows, :], 0.0)
            target[of_group(group), :] = piece.astype(BF16)
            start += length
    normed, _ = norm_parts(xpad_ref[...].astype(F32))
    first = (normed * row(gain_ref) + row(bias_ref)).astype(BF16)
    first_ref[...] = first
    qkv_ref[0] = (mm(first, w_ref[0]) + qvb_ref[0:1, :]).astype(BF16)
    qkv_ref[1] = mm(first, w_ref[1]).astype(BF16)
    qkv_ref[2] = (mm(first, w_ref[2]) + qvb_ref[1:2, :]).astype(BF16)
    for group, lse_ref, mix_ref in ((0, lse0_ref, mix0_ref), (1, lse1_ref, mix1_ref)):
        rows, length = PADDED[group], LENGTHS[group]
        low = low_lanes(rows)
        keep_keys = key_mask(rows, length)
        for pair in range(qkv_ref.shape[2] // PAIR):
            lanes = slice(pair * PAIR, (pair + 1) * PAIR)
            queries, keys, values = (qkv_ref[c, of_group(group), lanes] for c in range(3))
            values_t = values.T
            mixed_t = []
            for side in range(2):
                own = low if side == 0 else jnp.logical_not(low)
                scores = mm(keys, jnp.where(own, queries, jnp.zeros_like(queries)), NT) * scaling
                scores = jnp.where(keep_keys, scores, -jnp.inf)
                top = jnp.max(scores, axis=0, keepdims=True)
                exps = jnp.exp(scores - top)
                total = jnp.sum(exps, axis=0, keepdims=True)
                soft_low = (exps / total).astype(BF16)
                mixed_t.append(mm(values_t[side * HEAD_DIM : (side + 1) * HEAD_DIM], soft_low))
                head = 2 * pair + side
                lse_ref[head : head + 1, :] = top + jnp.log(total)
            mixed = jnp.concatenate(mixed_t, axis=0).T.astype(BF16).astype(F32)
            mix_ref[:, lanes] = mixed[: SENT[group]]


def relay_kernel(info_ref, in_ref, out_ref):
    out_ref[...] = in_ref[...]


def join_kernel(info_ref, ow_ref, one_ref, two_ref, got1_ref, got2_ref, ow_all):
    side, core, near = info_ref[0], info_ref[1], info_ref[5]
    span = ow_ref.shape[0]
    quarter = span // 4
    mine, other = side * span, (1 - side) * span
    ow_all[pl.ds(pl.multiple_of(mine, span), span), :] = ow_ref[...]
    for ref, where, x in (
        (one_ref, core, near), (two_ref, core, 1 - near), (got1_ref, 1 - core, near), (got2_ref, 1 - core, 1 - near),
    ):
        at = pl.multiple_of(other + (2 * where + x) * quarter, quarter)
        ow_all[pl.ds(at, quarter), :] = ref[...].astype(BF16)


def mlp_kernel(
    group, chunk, info_ref, x_ref, ct_ref, mix_ref, mix2_ref, ow_ref, ob_ref, gain_ref, bias_ref,
    up_ref, upb_ref, down_ref, *refs,
):
    *earlier, hidden_ref, second_ref, gmlp_ref, act_ref, gpre_ref, upsum_ref, downsum_ref, gs_ref, mix_all = refs
    side, live = info_ref[0], live_of(info_ref, group)
    span = mix_ref.shape[1]
    for which, ref in ((side, mix_ref), (1 - side, mix2_ref)):
        at = pl.ds(pl.multiple_of(which * span, span), span)
        mix_all[:, at] = filled(ref[...], PADDED[group]).astype(BF16)
    branch = mm(mix_all[...], ow_ref[...]) + row(ob_ref)
    hidden = x_ref[of_group(group), :].astype(F32) + live * branch
    hidden_ref[...] = hidden
    normed, _ = norm_parts(hidden)
    second = (normed * row(gain_ref) + row(bias_ref)).astype(BF16)
    second_ref[...] = second
    gmlp = live * ct_ref[of_group(group), :].astype(F32)
    downsum_ref[...] = col_sum(gmlp)
    gmlp = gmlp.astype(BF16)
    gmlp_ref[...] = gmlp
    bias = row(upb_ref)
    rows = slice(None)
    if earlier:
        gs_ref[sent_of(1 - group), :] = earlier[0][...]
        rows = sent_of(group)
    for step in range(up_ref.shape[1] // chunk):
        cols = slice(step * chunk, (step + 1) * chunk)
        pre = mm(second, up_ref[:, cols]) + bias[:, cols]
        cdf = 0.5 * (1.0 + lax.erf(pre * (0.5**0.5)))
        act_ref[:, cols] = (pre * cdf).astype(BF16)
        slope = cdf + pre * (jnp.exp(-0.5 * pre * pre) * 0.3989422804014327)
        gpre = (mm(gmlp, down_ref[cols, :], NT) * slope).astype(BF16)
        gpre_ref[:, cols] = gpre
        upsum_ref[:, cols] = col_sum(gpre.astype(F32))
        part = mm(gpre, up_ref[:, cols], NT)[: SENT[group]]
        gs_ref[rows, :] = part if step == 0 else gs_ref[rows, :] + part


def pick_blocks(wide, parity, height, length, order):
    count, bits = 1 << len(order), len(order)
    found = []
    for place in range(count):
        index = sum(((place >> (bits - 1 - n)) & 1) << (bit - 1) for n, bit in enumerate(order))
        even = wide[2 * index * height : (2 * index + 1) * height, :length]
        odd = wide[(2 * index + 1) * height : (2 * index + 2) * height, :length]
        found.append(jnp.where(parity == 0, even, odd))
    return jnp.concatenate(found, axis=0).astype(BF16)


def turned(core, height, order, left, wide):
    length = left.shape[0]
    wide[:, :length] = left.astype(F32).T
    return tuple(pick_blocks(wide, parity, height, length, order) for parity in (core, 1 - core))


def weights_kernel(height, piece, order, info_ref, l0_ref, l1_ref, r0_ref, r1_ref, keep_ref, *refs):
    *send_refs, wide = refs
    core = info_ref[1]
    keep0, send0 = turned(core, height, order, l0_ref[...], wide)
    keep1, send1 = turned(core, height, order, l1_ref[...], wide)
    for step, send_ref in enumerate(send_refs):
        cols = slice(step * piece, (step + 1) * piece)
        right0, right1 = r0_ref[:, cols], r1_ref[:, cols]
        send_ref[...] = mm(send0, right0) + mm(send1, right1)
        keep_ref[:, cols] = mm(keep0, right0) + mm(keep1, right1)


def attn_weights_kernel(
    height, order1, order2, info_ref, first_ref, dqkv0_ref, dqkv1_ref, ga0_ref, ga1_ref, mix0_ref, mix1_ref,
    s0_ref, s1_ref, u0_ref, u1_ref, d0_ref, d1_ref,
    keep1_ref, keep2_ref, small_ref, send1_ref, send2_ref, send3_ref, send4_ref, wide,
):
    core = info_ref[1]
    span = mix0_ref.shape[1]
    both = s0_ref[...] + s1_ref[...]
    up = u0_ref[...] + u1_ref[...]
    down = d0_ref[...] + d1_ref[...]
    width = small_ref.shape[1]
    small_ref[...] = jnp.zeros_like(small_ref)
    for at, value in enumerate((both[4:6], both[0:4], up[:, :width], up[:, width:], down)):
        at = (0, 2, 6, 7, 8)[at]
        small_ref[at : at + value.shape[0], :] = value
    rows = keep1_ref.shape[0]
    send1_ref[rows : rows + 16, :] = small_ref[:, :span]
    send1_ref[rows + 16 :, :] = small_ref[:, span:]
    sends = (send1_ref, send2_ref, send3_ref, send4_ref)
    for part in range(4):
        order = order1 if part < 2 else order2
        if part in (0, 2):
            left = [turned(core, height, order, first_ref[of_group(g), :], wide) for g in range(2)]
        if part < 3:
            right = [r[part] for r in (dqkv0_ref, dqkv1_ref)]
        else:
            left = [turned(core, height, order, r[...], wide) for r in (ga0_ref, ga1_ref)]
            right = [filled(r[...], p).astype(BF16) for r, p in zip((mix0_ref, mix1_ref), PADDED)]
        sends[part][: keep1_ref.shape[0], :] = mm(left[0][1], right[0]) + mm(left[1][1], right[1])
        base = part % 2 * span
        keep_ref = keep1_ref if part < 2 else keep2_ref
        keep_ref[:, base : base + span] = mm(left[0][0], right[0]) + mm(left[1][0], right[1])


def backward_kernel(
    group, info_ref, gs_ref, gs2_ref, x_ref, hidden_ref, ct_ref, gain_ref, ow_ref, qkv_ref, lse_ref, w_ref,
    *refs,
):
    *earlier, dqkv_ref, gattn_ref, gh_ref, sums_ref, gf_ref, gmix = refs
    scaling = HEAD_DIM ** (-0.5)
    rows, length = PADDED[group], LENGTHS[group]
    mine = of_group(group)
    live = live_of(info_ref, group)
    sent = sent_of(group)
    grad_second = filled(gs_ref[sent, :] + gs2_ref[sent, :], rows)
    normed, inverse = norm_parts(hidden_ref[...])
    grad_hidden = ct_ref[mine, :].astype(F32) + norm_back(grad_second, normed, inverse, row(gain_ref))
    gh_ref[...] = grad_hidden
    sums_ref[0:1, :] = col_sum(grad_second * normed)
    sums_ref[1:2, :] = col_sum(grad_second)
    gattn = (live * grad_hidden).astype(BF16)
    gattn_ref[...] = gattn
    sums_ref[2:3, :] = col_sum(gattn.astype(F32))
    gmix[...] = mm(gattn, ow_ref[...], NT).astype(BF16)
    low = low_lanes(rows)
    keep_keys = key_mask(rows, length)
    for pair in range(qkv_ref.shape[2] // PAIR):
        lanes = slice(pair * PAIR, (pair + 1) * PAIR)
        queries, keys, values = (qkv_ref[c, mine, lanes] for c in range(3))
        grads = gmix[:, lanes]
        keys_t = keys.T
        zero = jnp.zeros_like(queries)
        dq_t, dk, dv = [], [], []
        for side in range(2):
            own = low if side == 0 else jnp.logical_not(low)
            head = 2 * pair + side
            scores = mm(keys, jnp.where(own, queries, zero), NT) * scaling
            soft = jnp.where(keep_keys, jnp.exp(scores - lse_ref[head : head + 1, :]), 0.0)
            grad_soft = mm(values, jnp.where(own, grads, zero), NT)
            inner = jnp.sum(grad_soft * soft, axis=0, keepdims=True)
            grad_scores = (soft * (grad_soft - inner)).astype(BF16)
            dv.append(mm(soft.astype(BF16), grads))
            dk.append(mm(grad_scores, queries))
            dq_t.append(mm(keys_t[side * HEAD_DIM : (side + 1) * HEAD_DIM], grad_scores))
        dqkv_ref[0, :, lanes] = (jnp.concatenate(dq_t, axis=0).T * scaling).astype(BF16)
        dqkv_ref[1, :, lanes] = (jnp.where(low, dk[0], dk[1]) * scaling).astype(BF16)
        dqkv_ref[2, :, lanes] = jnp.where(low, dv[0], dv[1]).astype(BF16)
    part = mm(dqkv_ref[0], w_ref[0], NT) + mm(dqkv_ref[1], w_ref[1], NT) + mm(dqkv_ref[2], w_ref[2], NT)
    if earlier:
        gf_ref[sent_of(1 - group), :] = earlier[0][...]
        gf_ref[sent, :] = part[: SENT[group]]
    else:
        gf_ref[...] = part[: SENT[group]]
    first_normed, _ = norm_parts(x_ref[mine, :].astype(F32))
    sums_ref[4:5, :] = col_sum(part * first_normed)
    sums_ref[5:6, :] = col_sum(part)
    half = qkv_ref.shape[2]
    sums_ref[3:4, :half] = col_sum(dqkv_ref[0].astype(F32))
    sums_ref[3:4, half:] = col_sum(dqkv_ref[2].astype(F32))


def mlp_part_kernel(info_ref, act0_ref, act1_ref, down_ref, out_ref):
    for group, act_ref in enumerate((act0_ref, act1_ref)):
        out_ref[sent_of(group), :] = mm(act_ref[...], down_ref[...])[: SENT[group]]


def small_end_kernel(info_ref, small_ref, other_ref, gain1, bias1, gain2, bias2, outb, qvb, upb, downb):
    total = small_ref[...]
    width = total.shape[1]
    total = jnp.concatenate([total[0:2] + other_ref[0:2, :], total[2:]], axis=0)
    for n, ref in enumerate((gain1, bias1, gain2, bias2, outb)):
        ref[...] = total[n].reshape(width)
    qvb[0:1, :] = total[5:6, : width // 2]
    qvb[1:2, :] = total[5:6, width // 2 :]
    upb[:width] = total[6].reshape(width)
    upb[width:] = total[7].reshape(width)
    downb[...] = total[8].reshape(width)


def input_kernel(info_ref, x_ref, gh0_ref, gh1_ref, gain_ref, gf_ref, gf2_ref, grad_ref):
    start = 0
    for group, gh_ref in enumerate((gh0_ref, gh1_ref)):
        length, sent = LENGTHS[group], sent_of(group)
        grad_first = gf_ref[sent, :] + gf2_ref[sent, :]
        normed, inverse = norm_parts(x_ref[of_group(group), :].astype(F32)[: SENT[group]])
        value = gh_ref[: SENT[group], :] + norm_back(grad_first, normed, inverse, row(gain_ref))
        grad_ref[start : start + length, :] = value[:length]
        start += length


def output_kernel(info_ref, h0_ref, h1_ref, m_ref, m2_ref, bias_ref, out_ref, wide):
    start = 0
    for group, h_ref in enumerate((h0_ref, h1_ref)):
        length, mine = LENGTHS[group], sent_of(group)
        value = h_ref[: SENT[group], :] + live_of(info_ref, group) * (
            m_ref[mine, :] + m2_ref[mine, :] + row(bias_ref)
        )
        wide[start : start + length, :] = value[:length]
        start += length
    out_ref[...] = wide[...].astype(BF16)


def stage_kernel(bit, count, info_ref, keep_ref, *refs):
    pieces, (send_ref, rest_ref) = refs[:count], refs[count:]
    mine = info_ref[4 + bit]
    half = keep_ref.shape[0] // 2
    at = 0
    for piece in pieces:
        cols = slice(at, at + piece.shape[1])
        at += piece.shape[1]
        low = keep_ref[:half, cols] + piece[:half, :]
        high = keep_ref[half:, cols] + piece[half:, :]
        send_ref[:, cols] = jnp.where(mine == 0, high, low)
        rest_ref[:, cols] = jnp.where(mine == 0, low, high)


def stage_both_kernel(bit, info_ref, keep1_ref, keep2_ref, got1_ref, got2_ref, send_ref, rest_ref):
    cols = keep1_ref.shape[1]
    for n, (keep_ref, got_ref) in enumerate(((keep1_ref, got1_ref), (keep2_ref, got2_ref))):
        at = pl.ds(n * cols, cols)
        stage_kernel(bit, 1, info_ref, keep_ref, got_ref, send_ref.at[:, at], rest_ref.at[:, at])


def both_end_kernel(info_ref, keep_ref, got_ref, down_ref, up_ref):
    cols = down_ref.shape[1]
    down_ref[...] = keep_ref[:, :cols] + got_ref[:, :cols]
    up_ref[...] = keep_ref[:, cols:] + got_ref[:, cols:]


def stage_small_kernel(bit, count, last, info_ref, keep_ref, small_ref, *refs):
    pieces, outs = refs[:count], refs[count:]
    rows, span = keep_ref.shape[0], pieces[0].shape[1]
    if count == 2:
        other = jnp.concatenate([pieces[0][rows : rows + 16, :], pieces[0][rows + 16 :, :]], axis=1)
    else:
        other = pieces[0][rows:, :]
    small = small_ref[...] + other
    if last:
        out_ref, total_ref = outs
        total_ref[...] = small
        out_ref[...] = keep_ref[...] + pieces[0][:rows, :]
        return
    send_ref, rest_ref, total_ref = outs
    total_ref[...] = small
    mine, half, at = info_ref[4 + bit], rows // 2, 0
    for piece in pieces:
        cols = slice(at, at + piece.shape[1])
        at += piece.shape[1]
        low = keep_ref[:half, cols] + piece[:half, :]
        high = keep_ref[half:, cols] + piece[half:rows, :]
        send_ref[:half, cols] = jnp.where(mine == 0, high, low)
        rest_ref[:, cols] = jnp.where(mine == 0, low, high)
    send_ref[half:, :] = small


def last_kernel(info_ref, keep_ref, piece_ref, out_ref):
    out_ref[...] = keep_ref[...] + piece_ref[...]


def attn_last_kernel(info_ref, done1_ref, keep2_ref, got2_ref, qkv_ref, out_ref):
    span = out_ref.shape[1]
    qkv_ref[0] = done1_ref[:, :span]
    qkv_ref[1] = done1_ref[:, span:]
    qkv_ref[2] = keep2_ref[:, :span] + got2_ref[:, :span]
    out_ref[...] = keep2_ref[:, span:] + got2_ref[:, span:]


SMEM_SPEC = pl.BlockSpec(memory_space=pltpu.SMEM)
VMEM_SPEC = pl.BlockSpec(memory_space=pltpu.VMEM)
LATER = pl.BlockSpec(memory_space=pl.ANY)


def held(*shape, dtype=F32):
    return pltpu.VMEM(shape, dtype)


def shaped(*shape, dtype=F32):
    return jax.ShapeDtypeStruct(shape, dtype)


def in_vmem(value):
    return pltpu.with_memory_space_constraint(value, pltpu.VMEM)


def in_hbm(value):
    return pltpu.with_memory_space_constraint(value, pltpu.HBM)


class Order:
    def __init__(self, info, always):
        self.info = info
        self.always = always
        self.last = None

    def together(self, part, *watched):
        before = self.last
        states = [(v, dict(vars(v))) for v in watched]
        shapes = jax.eval_shape(part)
        self.last = before
        for value, state in states:
            vars(value).update(state)
        results = lax.cond(self.always, part, lambda: jax.tree.map(lambda v: jnp.zeros(v.shape, v.dtype), shapes))
        self.last = jax.tree.leaves(results)[0]
        return results

    def call(self, kernel, name, outs, operands, room=3, plain=False, after=(), **kwargs):
        many = isinstance(outs, (tuple, list))
        outs = tuple(outs) if many else (outs,)
        count = len(operands) + 1
        extra = [*after] if self.last is None else [*after, self.last]

        def body(*refs):
            kernel(*refs[:count], *refs[count + len(extra) :])

        results = pl.pallas_call(
            body,
            out_shape=outs,
            name=name,
            in_specs=[SMEM_SPEC] + [pl.BlockSpec() if plain else VMEM_SPEC] * (count - 1) + [LATER] * len(extra),
            out_specs=(VMEM_SPEC,) * len(outs),
            compiler_params=pltpu.CompilerParams(vmem_limit_bytes=room * MIB),
            cost_estimate=pl.CostEstimate(flops=1, bytes_accessed=1, transcendentals=0),
            **kwargs,
        )(self.info, *map(in_hbm if plain else in_vmem, operands), *extra)
        self.last = results[0]
        return results if many else results[0]


def swap_sides(value):
    return lax.ppermute(value, "tensor", [(0, 1), (1, 0)])


def swap_bit(value, size, bit):
    return lax.ppermute(value, "dp", [(i, i ^ (1 << bit)) for i in range(size)])


class Scatter:
    def __init__(self, order, size, bits, keep, send, small=None):
        self.small = small
        self.order, self.size, self.bits, self.keep, self.level = order, size, bits, keep, 0
        self.got = [swap_bit(piece, size, 0) for piece in send]

    def stage(self, name):
        bit = self.bits[self.level]
        self.level += 1
        half = (self.keep.shape[0] // 2, self.keep.shape[1])
        if self.small is not None:
            send, self.keep, self.small = self.order.call(
                functools.partial(stage_small_kernel, bit, len(self.got), False), f"{name}_{self.level}",
                (held(half[0] + 16, half[1]), held(*half), held(16, half[1])), [self.keep, self.small, *self.got],
            )
            self.got = [swap_bit(send, self.size, bit)]
            return
        send, self.keep = self.order.call(
            functools.partial(stage_kernel, bit, len(self.got)), f"{name}_{self.level}",
            (held(*half), held(*half)), [self.keep, *self.got],
        )
        self.got = [swap_bit(send, self.size, bit)]

    def last(self, name):
        return self.order.call(last_kernel, name, shaped(*self.keep.shape), [self.keep, *self.got])


def per_device(
    dp_size,
    images_in,
    small_counts,
    large_counts,
    norm1_gain,
    norm1_bias,
    qkv_weight,
    qv_bias,
    out_weight,
    out_bias,
    norm2_gain,
    norm2_bias,
    up_weight,
    up_bias,
    down_weight,
    down_bias,
    out_cotangent,
):
    width = images_in.shape[1]
    span = out_weight.shape[0]
    units = down_weight.shape[0]
    index = lax.axis_index("dp")
    side = lax.axis_index("tensor")
    core = index & 1
    bits = dp_size.bit_length() - 1
    height = width // dp_size
    order = Order(
        jnp.stack(
            [side, core, small_counts[0], large_counts[0]] + [(index >> b) & 1 for b in range(bits)]
        ).astype(jnp.int32),
        index < dp_size,
    )

    quarter = span // 4
    near = (index >> 1) & 1
    ow_send = lax.dynamic_slice_in_dim(out_weight, (2 * core + near) * quarter, quarter, 0).astype(F32)
    ow_one = swap_sides(ow_send)

    weights = qkv_weight.transpose(1, 0, 2)
    heads = span // HEAD_DIM
    first, qkv, x_pad, ct_pad, *rest = order.call(
        forward_kernel, "attn_forward",
        (
            held(ROWS, width, dtype=BF16), held(3, ROWS, span, dtype=BF16), held(ROWS, width, dtype=BF16),
            held(ROWS, width, dtype=BF16), *(held(heads, p) for p in PADDED), *(held(p, span) for p in SENT),
        ),
        [images_in, out_cotangent, norm1_gain, norm1_bias, weights, qv_bias], room=24, plain=True,
        scratch_shapes=[pltpu.VMEM((LENGTHS[0] + PADDED[1] + 3, width), F32)],
    )
    lse, mix = rest[:2], rest[2:]
    mix2 = [swap_sides(m) for m in mix]
    ow_one = order.call(relay_kernel, "out_weight_relay", held(quarter, width), [ow_one])
    ow_two = swap_bit(ow_one, dp_size, 1)
    ow_got1 = swap_bit(ow_one, dp_size, 0)
    ow_two = order.call(relay_kernel, "out_weight_next", held(quarter, width), [ow_two])
    ow_got2 = swap_bit(ow_two, dp_size, 0)
    ow_all = order.call(
        join_kernel, "out_weight_join", held(2 * span, width, dtype=BF16),
        [out_weight, ow_one, ow_two, ow_got1, ow_got2],
    )

    mlp, gs = [None, None], []
    for group in (1, 0):
        padded = PADDED[group]
        tall = SENT[group] + sum(g.shape[0] for g in gs)
        *mlp[group], total = order.call(
            functools.partial(mlp_kernel, group, 512), "mlp_" + "ab"[group],
            (
                held(padded, width), held(padded, width, dtype=BF16), held(padded, width, dtype=BF16),
                held(padded, units, dtype=BF16), held(padded, units, dtype=BF16),
                held(1, units), held(1, width), held(tall, width),
            ),
            [
                x_pad, ct_pad, mix[group], mix2[group], ow_all, out_bias, norm2_gain, norm2_bias,
                up_weight, up_bias, down_weight, *gs,
            ],
            room=16, scratch_shapes=[pltpu.VMEM((padded, 2 * span), BF16)],
        )
        gs = [total]
    gs = gs[0]
    gs2 = swap_sides(gs)
    hidden, second, gmlp, act, gpre, upsum, downsum = zip(*mlp)

    first_x = tuple(range(1, bits))
    first_z = (2, 1) + first_x[2:]

    def weight_grads(name, bit_order, left, right, piece):
        count = units // piece
        keep, *send = order.call(
            functools.partial(weights_kernel, height, piece, bit_order), name,
            (held(width // 2, units),) + (held(width // 2, piece),) * count, [*left, *right], room=12,
            scratch_shapes=[pltpu.VMEM((width, max(PADDED)), F32)],
        )
        return Scatter(order, dp_size, bit_order, keep, send)

    down_sum = weight_grads("down_weights", first_z, gmlp, act, 768)
    up_sum = weight_grads("up_weights", first_x, second, gpre, 768)
    down_sum.stage("down")
    up_sum.stage("up")
    mlp_part = order.call(mlp_part_kernel, "mlp_part", held(SENT_ROWS, width), [*act, down_weight], room=8)

    def go_back(group, *earlier):
        padded = PADDED[group]
        tall = SENT[group] + sum(e.shape[0] for e in earlier)
        return order.call(
            functools.partial(backward_kernel, group), "attn_backward_" + "ab"[group],
            (
                held(3, padded, span, dtype=BF16), held(padded, width, dtype=BF16),
                held(padded, width), held(8, width), held(tall, width),
            ),
            [
                gs, gs2, x_pad, hidden[group], ct_pad, norm2_gain, out_weight, qkv, lse[group], weights, *earlier,
            ],
            scratch_shapes=[pltpu.VMEM((padded, span), BF16)], room=16,
        )

    down_sum.stage("down")
    up_sum.stage("up")
    mlp_part = order.call(relay_kernel, "mlp_relay", held(SENT_ROWS, width), [mlp_part], after=[gs2])
    mlp2 = swap_sides(mlp_part)
    *back1, gf = go_back(1)
    *back0, gf = go_back(0, gf)
    gf2 = swap_sides(gf)
    dqkv, gattn, gh, sums = zip(back0, back1)

    for n in range(3, bits - 1):
        down_sum.stage("down")
        up_sum.stage("up")
    half = (down_sum.keep.shape[0] // 2, 2 * units)
    both, keep_both = order.call(
        functools.partial(stage_both_kernel, first_x[-1]), "mlp_3", (held(*half), held(*half)),
        [down_sum.keep, up_sum.keep, *down_sum.got, *up_sum.got],
    )
    got_both = swap_bit(both, dp_size, first_x[-1])
    rows = width // 2
    keep1, keep2, small, *send = order.call(
        functools.partial(attn_weights_kernel, height, first_x, first_z), "attn_weights",
        (
            held(rows, 2 * span), held(rows, 2 * span), held(16, width),
            held(rows + 32, span), held(rows, span), held(rows, span), held(rows, span),
        ),
        [first, *dqkv, *gattn, *mix, *sums, *upsum, *downsum], room=12,
        scratch_shapes=[pltpu.VMEM((width, max(PADDED)), F32)],
    )
    attn1 = Scatter(order, dp_size, first_x, keep1, send[:2], small)
    attn2 = Scatter(order, dp_size, first_z, keep2, send[2:])
    attn1.stage("attn1")
    attn2.stage("attn2")
    block_out = order.call(
        output_kernel, "block_out", shaped(*images_in.shape, dtype=BF16),
        [*hidden, mlp_part, mlp2, down_bias], room=8, scratch_shapes=[pltpu.VMEM(images_in.shape, F32)],
    )

    def attn_rest():
        for n in range(1, bits - 1):
            attn1.stage("attn1")
            attn2.stage("attn2")
        done1, total = order.call(
            functools.partial(stage_small_kernel, 0, 1, True), "attn1_end", (held(height, width), held(16, width)),
            [attn1.keep, attn1.small, *attn1.got],
        )
        ends = order.call(
            attn_last_kernel, "attn_end", (held(3, height, span), held(height, span)),
            [done1, attn2.keep, *attn2.got],
        )
        return (*ends, total)

    qkv_block, out_block, small = order.together(attn_rest, attn1, attn2)
    small2 = swap_sides(small)
    down_block, up_block = order.call(
        both_end_kernel, "mlp_end", (shaped(height, units),) * 2, [keep_both, got_both]
    )
    input_grad = order.call(
        input_kernel, "input_back", shaped(*images_in.shape), [x_pad, *gh, norm1_gain, gf, gf2], room=8
    )
    vector = shaped(width)
    small_out = order.call(
        small_end_kernel, "small_end",
        (vector, vector, vector, vector, vector, shaped(2, span), shaped(units), vector),
        [small, small2],
    )

    return (
        block_out,
        input_grad,
        small_out[0],
        small_out[1],
        qkv_block.transpose(1, 0, 2),
        small_out[5],
        out_block.T,
        small_out[4],
        small_out[2],
        small_out[3],
        up_block,
        small_out[6],
        down_block.T,
        small_out[7],
    )


def solution(mesh):
    placed = (
        P("dp", None),
        P("dp"),
        P("dp"),
        P(),
        P(),
        P(None, None, "tensor"),
        P(None, "tensor"),
        P("tensor", None),
        P(),
        P(),
        P(),
        P(None, "tensor"),
        P("tensor"),
        P("tensor", None),
        P(),
        P("dp", None),
    )
    return jax.shard_map(
        functools.partial(per_device, mesh.shape["dp"]),
        mesh=mesh,
        in_specs=placed,
        out_specs=(
            P("dp", None),
            P("dp", None),
            P(),
            P(),
            P("dp", None, "tensor"),
            P(None, "tensor"),
            P("tensor", "dp"),
            P(),
            P(),
            P(),
            P("dp", "tensor"),
            P("tensor"),
            P("tensor", "dp"),
            P(),
        ),
        check_vma=False,
    )
```

time: 574 us -> 191 us (0.33)
  waiting for transfers between devices: 390 us -> 86.2 us
  Pallas kernels: 0 us -> 64 us
  blocking collectives: 62 us -> 0 us
  matrix products: 57 us -> 0 us
  starting transfers between devices: 0.95 us -> 28.1 us
  other arithmetic: 20.9 us -> 0.94 us
  local copies, waits for them, and re-layouts: 26.4 us -> 8.54 us
  between operations: 16.2 us -> 2.33 us
    reduce_scatter x4 -> x0, waiting for transfers between devices: 223 us -> none  [the longest x1 79.6 us: per_device(): lax.psum_scatter(down_weight_grad, 'dp', scatter_dimension=1, tiled=True)]
    psum x3 -> x0, waiting for transfers between devices: 167 us -> none  [the longest x1 65.3 us: per_device(): mlp_branch = lax.psum(mlp_part, 'tensor') + down_bias]
    ppermute x0 -> x29, waiting for transfers between devices: none -> 86.2 us  [the longest x22 51 us: swap_bit(): return lax.ppermute(value, 'dp', [(i, i ^ 1 << bit) for i in range(size)])]
    pallas_call x0 -> x30, Pallas kernels: none -> 64 us  [call(): pl.pallas_call(body, out_shape=outs, name=name, in_specs=[SMEM_SPEC] + [p...]
    psum x1 -> x0, blocking collectives: 62 us -> none  [per_device(): lax.psum((norm1_gain_grad, norm1_bias_grad, qv_bias_grad, out_bias_grad,...]
    dot_general x24 -> x0, matrix products: 57 us -> none  [the longest x1 9.13 us: per_device(): jnp.dot(second_low, up_weight, preferred_element_type=jnp.float32) + up_bias]
    ppermute x0 -> x29, starting transfers between devices: none -> 28.1 us  [the longest x22 20.1 us: swap_bit(): return lax.ppermute(value, 'dp', [(i, i ^ 1 << bit) for i in range(size)])]
    slice x17 -> x0, local copies, waits for them, and re-layouts: 16.5 us -> none  [the longest x8 9.01 us: split_groups(): rows[split_at:].reshape(LARGE_SLOTS, LARGE_LEN, heads_here, HEAD_DIM)]
  transfers between devices with their start and end apart: 7 -> 29, of which waited for: 6 -> 13; matrix products, arithmetic and copies ran while one was open for 6% -> 1% of each run, Pallas kernels for 0% -> 27%
where the time goes in v2:
time: 191 us; the launch traced here: 190 us
  waiting for transfers between devices  86.2 us (45%)
  Pallas kernels  64 us (34%)
  starting transfers between devices  28.1 us (15%)
  local copies, waits for them, and re-layouts  8.54 us (4%)
  between operations  2.33 us (1%)
    pallas_call x30, Pallas kernels, call(): pl.pallas_call(body, out_shape=outs, name=name, in_specs=[SMEM_SPEC] + [p...  64 us
    ppermute x22, waiting for transfers between devices, swap_bit(): return lax.ppermute(value, 'dp', [(i, i ^ 1 << bit) for i in range(size)])  51 us
    ppermute x7, waiting for transfers between devices, swap_sides(): return lax.ppermute(value, 'tensor', [(0, 1), (1, 0)])  35.1 us
    ppermute x22, starting transfers between devices, swap_bit(): return lax.ppermute(value, 'dp', [(i, i ^ 1 << bit) for i in range(size)])  20.1 us
    unnamed x50, local copies, waits for them, and re-layouts  8.46 us
    ppermute x7, starting transfers between devices, swap_sides(): return lax.ppermute(value, 'tensor', [(0, 1), (1, 0)])  7.99 us
  transfers between devices with their start and end apart: 29, of which 13 were waited for; matrix products, arithmetic and copies ran while one was open for 1% of the time, Pallas kernels for 27%

profile of v2, /device:TPU:0, one launch (start us, length us, event | category | flops | bytes accessed | tf_op | source)
XLA Modules:
  0.0 190.1 jit_solution(2534483414544733868)
XLA Ops:
  1.6 3.0 %collective-permute-start.5 = (f32[96,768]{1,0:T(8,128)S(1)}, f32[96,768]{1,0:T(8,128)S(1)}, u32[]{:S(2)}, u32[]{:S(2)}) collective-permute-start(f32[96,768]{1,0:T(8,128)S(1)} %dynamic-slice_convert_fusion), channel_id=1, source_target_pairs={{0,1},{1,0},{2,3},{3,2},{4,5},{5,4},{6,7},{7,6},{8,9},{9,8},{10,11... | collective-permute-start | bytes 884744 | tf_op jit(solution)/shard_map/ppermute | solution.py:465
  6.0 7.9 %attn_forward.1 = (bf16[544,768]{1,0:T(8,128)(2,1)S(1)}, bf16[3,544,384]{2,1,0:T(8,128)(2,1)S(1)}, bf16[544,768]{1,0:T(8,128)(2,1)S(1)}, bf16[544,768]{1,0:T(8,1...) custom-call(s32[8]{0:T(128)S(1)} %stack.27.refs_0_, ...), custom_call_target="tpu_custom_call" | custom-call | flops 1 | bytes 1 | tf_op jit(solution)/shard_map/attn_forward/pallas_call | solution.py:450
  18.1 5.0 %collective-permute-done.6.refs_1_ = f32[96,768]{1,0:T(8,128)S(1)} collective-permute-done((f32[96,768]{1,0:T(8,128)S(1)}, f32[96,768]{1,0:T(8,128)S(1)}, u32[]{:S(2)}, u32[]{:S(2)}) %collective-permute-start.6) | collective-permute-done | bytes 294944 | tf_op jit(solution)/shard_map/ppermute | solution.py:469
  25.9 4.5 %collective-permute-done.9.refs_4_ = f32[328,384]{1,0:T(8,128)S(1)} collective-permute-done((f32[328,384]{1,0:T(8,128)S(1)}, f32[328,384]{1,0:T(8,128)S(1)}, u32[]{:S(2)}, u32[]{:S(2)}) %collective-permute-start.9) | collective-permute-done | bytes 503840 | tf_op jit(solution)/shard_map/ppermute | solution.py:465
  30.5 4.7 %mlp_b.1 = (f32[336,768]{1,0:T(8,128)S(1)}, bf16[336,768]{1,0:T(8,128)(2,1)S(1)}, bf16[336,768]{1,0:T(8,128)(2,1)S(1)}, bf16[336,1536]{1,0:T(8,128)(2,1)S(1)}, b...) custom-call(s32[8]{0:T(128)S(1)} %stack.27.refs_0_, ...), custom_call_target="tpu_custom_call" | custom-call | flops 1 | bytes 1 | tf_op jit(solution)/shard_map/mlp_b/pallas_call | solution.py:450
  35.3 3.6 %mlp_a.1 = (f32[208,768]{1,0:T(8,128)S(1)}, bf16[208,768]{1,0:T(8,128)(2,1)S(1)}, bf16[208,768]{1,0:T(8,128)(2,1)S(1)}, bf16[208,1536]{1,0:T(8,128)(2,1)S(1)}, b...) custom-call(s32[8]{0:T(128)S(1)} %stack.27.refs_0_, ...), custom_call_target="tpu_custom_call" | custom-call | flops 1 | bytes 1 | tf_op jit(solution)/shard_map/mlp_a/pallas_call | solution.py:450
  38.8 3.0 %down_weights.1 = (f32[384,1536]{1,0:T(8,128)S(1)}, f32[384,768]{1,0:T(8,128)S(1)}, f32[384,768]{1,0:T(8,128)S(1)}) custom-call(s32[8]{0:T(128)S(1)} %stack.27.refs_0_, bf16[208,768]{1,0:T(8,128)(2,1)S(1)} %get-tuple-element.138.refs_1_, bf16[336,768]{1,0:T(8,128)(2,1)S(1)} %get-tuple-element.139.refs_2_, ...), custom_call_target="tpu_custom_call" | custom-call | flops 1 | bytes 1 | tf_op jit(solution)/shard_map/down_weights/pallas_call | solution.py:450
  42.5 2.8 %up_weights.1 = (f32[384,1536]{1,0:T(8,128)S(1)}, f32[384,768]{1,0:T(8,128)S(1)}, f32[384,768]{1,0:T(8,128)S(1)}) custom-call(s32[8]{0:T(128)S(1)} %stack.27.refs_0_, bf16[208,768]{1,0:T(8,128)(2,1)S(1)} %get-tuple-element.134.refs_1_, bf16[336,768]{1,0:T(8,128)(2,1)S(1)} %get-tuple-element.135.refs_2_, bf16[208,1536]{1,0:T(8,128)(2,1)S(1)} %get-tuple-element.136.refs_3_, ...), custom_call_target="tpu_custom_call" | custom-call | flops 1 | bytes 1 | tf_op jit(solution)/shard_map/up_weights/pallas_call | solution.py:450
  51.6 2.0 %mlp_part.1.refs_3_.refs_1_ = f32[528,768]{1,0:T(8,128)S(1)} custom-call(s32[8]{0:T(128)S(1)} %stack.27.refs_0_, bf16[208,1536]{1,0:T(8,128)(2,1)S(1)} %get-tuple-element.132.refs_3_.refs_1_, bf16[336,1536]{1,0:T(8,128)(2,1)S(1)} %get-tuple-element.133.refs_4_.refs_2_, bf16[1536,768]{1,0:T(8,128)(2,1)S(1)} %copy-done, f32[192,1536]{1,0:T(8,128)S(1)} %get-tuple-element.147.refs_4_), custom_call_target="tpu_custom_call" | custom-call | flops 1 | bytes 1 | tf_op jit(solution)/shard_map/mlp_part/pallas_call | solution.py:450
  53.6 21.7 %collective-permute-done.16.refs_2_ = f32[192,1536]{1,0:T(8,128)S(1)} collective-permute-done((f32[192,1536]{1,0:T(8,128)S(1)}, f32[192,1536]{1,0:T(8,128)S(1)}, u32[]{:S(2)}, u32[]{:S(2)}) %collective-permute-start.16) | collective-permute-done | bytes 1179680 | tf_op jit(solution)/shard_map/ppermute | solution.py:469
  76.0 2.7 %collective-permute-done.15.refs_2_ = f32[192,1536]{1,0:T(8,128)S(1)} collective-permute-done((f32[192,1536]{1,0:T(8,128)S(1)}, f32[192,1536]{1,0:T(8,128)S(1)}, u32[]{:S(2)}, u32[]{:S(2)}) %collective-permute-start.15) | collective-permute-done | bytes 1179680 | tf_op jit(solution)/shard_map/ppermute | solution.py:469
  81.6 6.9 %collective-permute-done.14.refs_2_ = f32[528,768]{1,0:T(8,128)S(1)} collective-permute-done((f32[528,768]{1,0:T(8,128)S(1)}, f32[528,768]{1,0:T(8,128)S(1)}, u32[]{:S(2)}, u32[]{:S(2)}) %collective-permute-start.14) | collective-permute-done | bytes 1622048 | tf_op jit(solution)/shard_map/ppermute | solution.py:465
  90.0 6.0 %attn_backward_b.1 = (bf16[3,336,384]{2,1,0:T(8,128)(2,1)S(1)}, bf16[336,768]{1,0:T(8,128)(2,1)S(1)}, f32[336,768]{1,0:T(8,128)S(1)}, f32[8,768]{1,0:T(8,128)S(1)}, f32[328,768]{1,0:T(8,128)S(1)}) custom-call(s32[8]{0:T(128)S(1)} %stack.27.refs_0_, f32[528,768]{1,0:T(8,128)S(1)} %get-tuple-element.148.refs_1_, ...), custom_call_target="tpu_custom_call" | custom-call | flops 1 | bytes 1 | tf_op jit(solution)/shard_map/attn_backward_b/pallas_call | solution.py:450
  97.0 5.4 %attn_backward_a.1 = (bf16[3,208,384]{2,1,0:T(8,128)(2,1)S(1)}, bf16[208,768]{1,0:T(8,128)(2,1)S(1)}, f32[208,768]{1,0:T(8,128)S(1)}, f32[8,768]{1,0:T(8,128)S(1)}, f32[528,768]{1,0:T(8,128)}) custom-call(s32[8]{0:T(128)S(1)} %stack.27.refs_0_, f32[528,768]{1,0:T(8,128)S(1)} %get-tuple-element.148.refs_1_, f32[528,768]{1,0:T(8,128)S(1)} %collective-permute-done.14.refs_2_, ...), custom_call_target="tpu_custom_call" | custom-call | flops 1 | bytes 1 | tf_op jit(solution)/shard_map/attn_backward_a/pallas_call | solution.py:450
  104.0 3.3 %attn_weights.1 = (f32[384,768]{1,0:T(8,128)S(1)}, f32[384,768]{1,0:T(8,128)S(1)}, f32[16,768]{1,0:T(8,128)S(1)}, f32[416,384]{1,0:T(8,128)S(1)}, f32[384,384]{1...) custom-call(s32[8]{0:T(128)S(1)} %stack.27.refs_0_, ...), custom_call_target="tpu_custom_call" | custom-call | flops 1 | bytes 1 | tf_op jit(solution)/shard_map/attn_weights/pallas_call | solution.py:450
  119.5 2.6 %collective-permute-start.25 = (f32[48,3072]{1,0:T(8,128)}, f32[48,3072]{1,0:T(8,128)}, u32[]{:S(2)}, u32[]{:S(2)}) collective-permute-start(f32[48,3072]{1,0:T(8,128)} %get-tuple-element.169.refs_14_), channel_id=1, source_target_pairs={{0,16},{2,18},{4,20},{6,22},{8,24},{10,26},{12,28},{14,30},{16,0},... | collective-permute-start | bytes 1769480 | tf_op jit(solution)/shard_map/ppermute | solution.py:469
  122.1 23.7 %collective-permute-done.17.refs_4_ = f32[528,768]{1,0:T(8,128)} collective-permute-done((f32[528,768]{1,0:T(8,128)S(1)}, f32[528,768]{1,0:T(8,128)}, u32[]{:S(2)}, u32[]{:S(2)}) %collective-permute-start.17) | collective-permute-done | bytes 1622048 | tf_op jit(solution)/shard_map/ppermute | solution.py:465
  147.1 3.0 %block_out.1 = bf16[522,768]{1,0:T(8,128)(2,1)} custom-call(s32[8]{0:T(128)S(1)} %stack.27.refs_0_, f32[208,768]{1,0:T(8,128)S(1)} %get-tuple-element.131.refs_5_.refs_4_.refs_1_, f32[336,768]{1,0:T(8,128)S(1)} %copy-done.4, f32[528,768]{1,0:T(8,128)S(1)} %mlp_relay.1.refs_11_.refs_3_, f32[528,768]{1,0:T(8,128)} %collective-permute-done.17.refs_4_, ...), custom_call_target="tpu_custom_call" | custom-call | flops 1 | bytes 1 | tf_op jit(solution)/shard_map/block_out/pallas_call | solution.py:450
  150.1 28.4 %conditional.1 = (f32[3,48,384]{2,1,0:T(8,128)S(1)}, f32[48,384]{1,0:T(8,128)S(1)}, f32[16,768]{1,0:T(8,128)S(1)}) conditional(s32[]{:T(128)} %convert_element_type.7, () %tuple.16, (s32[8]{0:T(128)S(1)}, f32[192,768]{1,0:T(8,128)S(1)}, f32[16,768]{1,0:T(8,128)S(1)}, f32[208,768]{1,0:T(8,128)}, bf16[522,768]{1,0:T(8,128)(2,1)}, ...), branch_computations={%region_0.0_spmd, %region_1.0_spmd} | conditional | flops 6 | bytes 3932350 | solution.py:437
  155.8 4.9 %collective-permute-done.refs_3_ = f32[112,768]{1,0:T(8,128)S(1)} collective-permute-done((f32[112,768]{1,0:T(8,128)S(1)}, f32[112,768]{1,0:T(8,128)S(1)}, u32[]{:S(2)}, u32[]{:S(2)}) %collective-permute-start) | collective-permute-done | bytes 344096 | tf_op jit(solution)/shard_map/cond/branch_1_fun/ppermute | solution.py:469
  161.2 2.6 %collective-permute-start.1 = (f32[64,768]{1,0:T(8,128)S(1)}, f32[64,768]{1,0:T(8,128)S(1)}, u32[]{:S(2)}, u32[]{:S(2)}) collective-permute-start(f32[64,768]{1,0:T(8,128)S(1)} %get-tuple-element.27.refs_3_), channel_id=1, source_target_pairs={{0,16},{2,18},{4,20},{6,22},{8,24},{10,26},{12,28},{14,30},{16,0},... | collective-permute-start | bytes 589832 | tf_op jit(solution)/shard_map/cond/branch_1_fun/ppermute | solution.py:469
  165.3 10.6 %collective-permute-done.1.refs_3_ = f32[64,768]{1,0:T(8,128)S(1)} collective-permute-done((f32[64,768]{1,0:T(8,128)S(1)}, f32[64,768]{1,0:T(8,128)S(1)}, u32[]{:S(2)}, u32[]{:S(2)}) %collective-permute-start.1) | collective-permute-done | bytes 196640 | tf_op jit(solution)/shard_map/cond/branch_1_fun/ppermute | solution.py:469
  179.1 1.9 %mlp_end.1 = (f32[48,1536]{1,0:T(8,128)}, f32[48,1536]{1,0:T(8,128)}) custom-call(s32[8]{0:T(128)S(1)} %stack.27.refs_0_, f32[48,3072]{1,0:T(8,128)S(1)} %copy-done.12, f32[48,3072]{1,0:T(8,128)} %collective-permute-done.25.refs_2_, f32[3,48,384]{2,1,0:T(8,128)S(1)} %get-tuple-element.186.refs_3_), custom_call_target="tpu_custom_call" | custom-call | flops 1 | bytes 1 | tf_op jit(solution)/shard_map/mlp_end/pallas_call | solution.py:450
  182.0 4.3 %input_back.1.refs_3_ = f32[522,768]{1,0:T(8,128)} custom-call(s32[8]{0:T(128)S(1)} %stack.27.refs_0_, bf16[544,768]{1,0:T(8,128)(2,1)S(1)} %get-tuple-element.124.refs_1_.refs_3_, f32[208,768]{1,0:T(8,128)S(1)} %copy-done.10, f32[336,768]{1,0:T(8,128)S(1)} %copy-done.8, f32[768]{0:T(1024)S(1)} %copy-done.20, f32[528,768]{1,0:T(8,128)} %get-tuple-element.181.refs_5_, ...), custom_call_target="tpu_custom_call" | custom-call | flops 1 | bytes 1 | tf_op jit(solution)/shard_map/input_back/pallas_call | solution.py:450
  (117 shorter events, 51.5 us)
Async XLA Ops:
  1.6 12.3 %collective-permute-start.5 = (f32[96,768]{1,0:T(8,128)S(1)}, f32[96,768]{1,0:T(8,128)S(1)}, u32[]{:S(2)}, u32[]{:S(2)}) collective-permute-start(f32[96,768]{1,0:T(8,128)S(1)} %dynamic-slice_convert_fusion), channel_id=1, source_target_pairs={{0,1},{1,0},{2,3},{3,2},{4,5},{5,4},{6,7},{7,6},{8,9},{9,8},{10,11... | collective-permute-start | bytes 884744 | tf_op jit(solution)/shard_map/ppermute | solution.py:465
  14.5 8.5 %collective-permute-start.6 = (f32[96,768]{1,0:T(8,128)S(1)}, f32[96,768]{1,0:T(8,128)S(1)}, u32[]{:S(2)}, u32[]{:S(2)}) collective-permute-start(f32[96,768]{1,0:T(8,128)S(1)} %out_weight_relay.1.refs_2_), channel_id=1, source_target_pairs={{0,4},{2,6},{4,0},{6,2},{8,12},{10,14},{12,8},{14,10},{16,20},{18,... | collective-permute-start | bytes 884744 | tf_op jit(solution)/shard_map/ppermute | solution.py:469
  16.0 14.4 %collective-permute-start.9 = (f32[328,384]{1,0:T(8,128)S(1)}, f32[328,384]{1,0:T(8,128)S(1)}, u32[]{:S(2)}, u32[]{:S(2)}) collective-permute-start(f32[328,384]{1,0:T(8,128)S(1)} %get-tuple-element.128.refs_3_.refs_7_), channel_id=1, source_target_pairs={{0,1},{1,0},{2,3},{3,2},{4,5},{5,4},{6,7},{7,6},{8,9},{9,8},{10,11... | collective-permute-start | bytes 1511432 | tf_op jit(solution)/shard_map/ppermute | solution.py:465
  16.5 18.7 %collective-permute-start.4 = (f32[200,384]{1,0:T(8,128)S(1)}, f32[200,384]{1,0:T(8,128)S(1)}, u32[]{:S(2)}, u32[]{:S(2)}) collective-permute-start(f32[200,384]{1,0:T(8,128)S(1)} %get-tuple-element.126.refs_3_.refs_6_), channel_id=1, source_target_pairs={{0,1},{1,0},{2,3},{3,2},{4,5},{5,4},{6,7},{7,6},{8,9},{9,8},{10,11... | collective-permute-start | bytes 921608 | tf_op jit(solution)/shard_map/ppermute | solution.py:465
  18.1 5.7 %collective-permute-start.7 = (f32[96,768]{1,0:T(8,128)S(1)}, f32[96,768]{1,0:T(8,128)S(1)}, u32[]{:S(2)}, u32[]{:S(2)}) collective-permute-start(f32[96,768]{1,0:T(8,128)S(1)} %out_weight_relay.1.refs_2_), channel_id=1, source_target_pairs={{0,2},{2,0},{4,6},{6,4},{8,10},{10,8},{12,14},{14,12},{16,18},{18,... | collective-permute-start | bytes 884744 | tf_op jit(solution)/shard_map/ppermute | solution.py:469
  42.0 4.5 %collective-permute-start.13 = (f32[384,768]{1,0:T(8,128)S(1)}, f32[384,768]{1,0:T(8,128)S(1)}, u32[]{:S(2)}, u32[]{:S(2)}) collective-permute-start(f32[384,768]{1,0:T(8,128)S(1)} %get-tuple-element.145), channel_id=1, source_target_pairs={{0,2},{2,0},{4,6},{6,4},{8,10},{10,8},{12,14},{14,12},{16,18},{18,... | collective-permute-start | bytes 3538952 | tf_op jit(solution)/shard_map/ppermute | solution.py:469
  45.4 4.5 %collective-permute-start.11 = (f32[384,768]{1,0:T(8,128)S(1)}, f32[384,768]{1,0:T(8,128)S(1)}, u32[]{:S(2)}, u32[]{:S(2)}) collective-permute-start(f32[384,768]{1,0:T(8,128)S(1)} %get-tuple-element.143), channel_id=1, source_target_pairs={{0,2},{2,0},{4,6},{6,4},{8,10},{10,8},{12,14},{14,12},{16,18},{18,... | collective-permute-start | bytes 3538952 | tf_op jit(solution)/shard_map/ppermute | solution.py:469
  47.3 28.1 %collective-permute-start.16 = (f32[192,1536]{1,0:T(8,128)S(1)}, f32[192,1536]{1,0:T(8,128)S(1)}, u32[]{:S(2)}, u32[]{:S(2)}) collective-permute-start(f32[192,1536]{1,0:T(8,128)S(1)} %get-tuple-element.146.refs_4_), channel_id=1, source_target_pairs={{0,8},{2,10},{4,12},{6,14},{8,0},{10,2},{12,4},{14,6},{16,24},{18,... | collective-permute-start | bytes 3538952 | tf_op jit(solution)/shard_map/ppermute | solution.py:469
  50.7 28.1 %collective-permute-start.15 = (f32[192,1536]{1,0:T(8,128)S(1)}, f32[192,1536]{1,0:T(8,128)S(1)}, u32[]{:S(2)}, u32[]{:S(2)}) collective-permute-start(f32[192,1536]{1,0:T(8,128)S(1)} %get-tuple-element.147.refs_4_), channel_id=1, source_target_pairs={{0,4},{2,6},{4,0},{6,2},{8,12},{10,14},{12,8},{14,10},{16,20},{18,... | collective-permute-start | bytes 3538952 | tf_op jit(solution)/shard_map/ppermute | solution.py:469
  51.3 37.2 %collective-permute-start.14 = (f32[528,768]{1,0:T(8,128)S(1)}, f32[528,768]{1,0:T(8,128)S(1)}, u32[]{:S(2)}, u32[]{:S(2)}) collective-permute-start(f32[528,768]{1,0:T(8,128)S(1)} %get-tuple-element.148.refs_1_), channel_id=1, source_target_pairs={{0,1},{1,0},{2,3},{3,2},{4,5},{5,4},{6,7},{7,6},{8,9},{9,8},{10,11... | collective-permute-start | bytes 4866056 | tf_op jit(solution)/shard_map/ppermute | solution.py:465
  79.4 23.0 %collective-permute-start.19 = (f32[96,1536]{1,0:T(8,128)S(1)}, f32[96,1536]{1,0:T(8,128)S(1)}, u32[]{:S(2)}, u32[]{:S(2)}) collective-permute-start(f32[96,1536]{1,0:T(8,128)S(1)} %get-tuple-element.152.refs_3_), channel_id=1, source_target_pairs={{0,8},{2,10},{4,12},{6,14},{8,0},{10,2},{12,4},{14,6},{16,24},{18,... | collective-permute-start | bytes 1769480 | tf_op jit(solution)/shard_map/ppermute | solution.py:469
  81.1 21.3 %collective-permute-start.18 = (f32[96,1536]{1,0:T(8,128)S(1)}, f32[96,1536]{1,0:T(8,128)S(1)}, u32[]{:S(2)}, u32[]{:S(2)}) collective-permute-start(f32[96,1536]{1,0:T(8,128)S(1)} %get-tuple-element.151.refs_3_), channel_id=1, source_target_pairs={{0,4},{2,6},{4,0},{6,2},{8,12},{10,14},{12,8},{14,10},{16,20},{18,... | collective-permute-start | bytes 1769480 | tf_op jit(solution)/shard_map/ppermute | solution.py:469
  107.4 38.4 %collective-permute-start.17 = (f32[528,768]{1,0:T(8,128)S(1)}, f32[528,768]{1,0:T(8,128)}, u32[]{:S(2)}, u32[]{:S(2)}) collective-permute-start(f32[528,768]{1,0:T(8,128)S(1)} %mlp_relay.1.refs_11_.refs_3_), channel_id=1, source_target_pairs={{0,1},{1,0},{2,3},{3,2},{4,5},{5,4},{6,7},{7,6},{8,9},{9,8},{10,11... | collective-permute-start | bytes 4866056 | tf_op jit(solution)/shard_map/ppermute | solution.py:465
  107.8 73.2 %collective-permute-start.24 = (f32[528,768]{1,0:T(8,128)}, f32[528,768]{1,0:T(8,128)}, u32[]{:S(2)}, u32[]{:S(2)}) collective-permute-start(f32[528,768]{1,0:T(8,128)} %get-tuple-element.181.refs_5_), channel_id=1, source_target_pairs={{0,1},{1,0},{2,3},{3,2},{4,5},{5,4},{6,7},{7,6},{8,9},{9,8},{10,11... | collective-permute-start | bytes 4866056 | tf_op jit(solution)/shard_map/ppermute | solution.py:465
  109.5 6.0 %collective-permute-start.20 = (f32[384,384]{1,0:T(8,128)S(1)}, f32[384,384]{1,0:T(8,128)S(1)}, u32[]{:S(2)}, u32[]{:S(2)}) collective-permute-start(f32[384,384]{1,0:T(8,128)S(1)} %get-tuple-element.171), channel_id=1, source_target_pairs={{0,2},{2,0},{4,6},{6,4},{8,10},{10,8},{12,14},{14,12},{16,18},{18,... | collective-permute-start | bytes 1769480 | tf_op jit(solution)/shard_map/ppermute | solution.py:469
  110.0 5.5 %collective-permute-start.21 = (f32[384,384]{1,0:T(8,128)S(1)}, f32[384,384]{1,0:T(8,128)S(1)}, u32[]{:S(2)}, u32[]{:S(2)}) collective-permute-start(f32[384,384]{1,0:T(8,128)S(1)} %get-tuple-element.172), channel_id=1, source_target_pairs={{0,2},{2,0},{4,6},{6,4},{8,10},{10,8},{12,14},{14,12},{16,18},{18,... | collective-permute-start | bytes 1769480 | tf_op jit(solution)/shard_map/ppermute | solution.py:469
  114.1 36.0 %collective-permute-start.26 = (f32[208,768]{1,0:T(8,128)}, f32[208,768]{1,0:T(8,128)}, u32[]{:S(2)}, u32[]{:S(2)}) collective-permute-start(f32[208,768]{1,0:T(8,128)} %get-tuple-element.177.refs_4_), channel_id=1, source_target_pairs={{0,4},{2,6},{4,0},{6,2},{8,12},{10,14},{12,8},{14,10},{16,20},{18,... | collective-permute-start | bytes 1916936 | tf_op jit(solution)/shard_map/ppermute | solution.py:469
  118.0 32.1 %collective-permute-start.27 = (f32[192,768]{1,0:T(8,128)}, f32[192,768]{1,0:T(8,128)}, u32[]{:S(2)}, u32[]{:S(2)}) collective-permute-start(f32[192,768]{1,0:T(8,128)} %get-tuple-element.178.refs_6_), channel_id=1, source_target_pairs={{0,8},{2,10},{4,12},{6,14},{8,0},{10,2},{12,4},{14,6},{16,24},{18,... | collective-permute-start | bytes 1769480 | tf_op jit(solution)/shard_map/ppermute | solution.py:469
  119.5 59.5 %collective-permute-start.25 = (f32[48,3072]{1,0:T(8,128)}, f32[48,3072]{1,0:T(8,128)}, u32[]{:S(2)}, u32[]{:S(2)}) collective-permute-start(f32[48,3072]{1,0:T(8,128)} %get-tuple-element.169.refs_14_), channel_id=1, source_target_pairs={{0,16},{2,18},{4,20},{6,22},{8,24},{10,26},{12,28},{14,30},{16,0},... | collective-permute-start | bytes 1769480 | tf_op jit(solution)/shard_map/ppermute | solution.py:469
  151.4 9.2 %collective-permute-start = (f32[112,768]{1,0:T(8,128)S(1)}, f32[112,768]{1,0:T(8,128)S(1)}, u32[]{:S(2)}, u32[]{:S(2)}) collective-permute-start(f32[112,768]{1,0:T(8,128)S(1)} %get-tuple-element.21.refs_3_), channel_id=1, source_target_pairs={{0,8},{2,10},{4,12},{6,14},{8,0},{10,2},{12,4},{14,6},{16,24},{18,... | collective-permute-start | bytes 1032200 | tf_op jit(solution)/shard_map/cond/branch_1_fun/ppermute | solution.py:469
  154.2 9.7 %collective-permute-start.2 = (f32[96,768]{1,0:T(8,128)S(1)}, f32[96,768]{1,0:T(8,128)S(1)}, u32[]{:S(2)}, u32[]{:S(2)}) collective-permute-start(f32[96,768]{1,0:T(8,128)S(1)} %get-tuple-element.24.refs_4_), channel_id=1, source_target_pairs={{0,4},{2,6},{4,0},{6,2},{8,12},{10,14},{12,8},{14,10},{16,20},{18,... | collective-permute-start | bytes 884744 | tf_op jit(solution)/shard_map/cond/branch_1_fun/ppermute | solution.py:469
  161.2 14.7 %collective-permute-start.1 = (f32[64,768]{1,0:T(8,128)S(1)}, f32[64,768]{1,0:T(8,128)S(1)}, u32[]{:S(2)}, u32[]{:S(2)}) collective-permute-start(f32[64,768]{1,0:T(8,128)S(1)} %get-tuple-element.27.refs_3_), channel_id=1, source_target_pairs={{0,16},{2,18},{4,20},{6,22},{8,24},{10,26},{12,28},{14,30},{16,0},... | collective-permute-start | bytes 589832 | tf_op jit(solution)/shard_map/cond/branch_1_fun/ppermute | solution.py:469
  164.5 13.5 %collective-permute-start.3 = (f32[48,768]{1,0:T(8,128)S(1)}, f32[48,768]{1,0:T(8,128)S(1)}, u32[]{:S(2)}, u32[]{:S(2)}) collective-permute-start(f32[48,768]{1,0:T(8,128)S(1)} %get-tuple-element.29.refs_4_), channel_id=1, source_target_pairs={{0,16},{2,18},{4,20},{6,22},{8,24},{10,26},{12,28},{14,30},{16,0},... | collective-permute-start | bytes 442376 | tf_op jit(solution)/shard_map/cond/branch_1_fun/ppermute | solution.py:469
  178.5 9.0 %collective-permute-start.28 = (f32[16,768]{1,0:T(8,128)S(1)}, f32[16,768]{1,0:T(8,128)S(1)}, u32[]{:S(2)}, u32[]{:S(2)}) collective-permute-start(f32[16,768]{1,0:T(8,128)S(1)} %get-tuple-element.188.refs_1_), channel_id=1, source_target_pairs={{0,1},{1,0},{2,3},{3,2},{4,5},{5,4},{6,7},{7,6},{8,9},{9,8},{10,11... | collective-permute-start | bytes 147464 | tf_op jit(solution)/shard_map/ppermute | solution.py:465
  (29 other events, 244.0 us)

commit v3 on v2

--- a/solution.py
+++ b/solution.py
@@ -20,6 +20,8 @@
 F32 = jnp.float32
 BF16 = jnp.bfloat16
 MIB = 1024 * 1024
+COST = {'attn_backward_b': 100000000000, 'block_out': 100000000000, 'mlp_3': 7000000000}
+OPT = {'tail': 0, 's2': 1, 's3': 1, 'block': 0, 'relay': 0, 'mlp': 1, 'dpiece': 768, 'upiece': 768, 'apiece': 384, 'both': 2, 'input': 0, 'z': 'u'}
 NT = ((1,), (1,))
 TN = ((0,), (0,))
 
@@ -206,8 +208,9 @@
 def attn_weights_kernel(
     height, order1, order2, info_ref, first_ref, dqkv0_ref, dqkv1_ref, ga0_ref, ga1_ref, mix0_ref, mix1_ref,
     s0_ref, s1_ref, u0_ref, u1_ref, d0_ref, d1_ref,
-    keep1_ref, keep2_ref, small_ref, send1_ref, send2_ref, send3_ref, send4_ref, wide,
+    keep1_ref, keep2_ref, small_ref, *send_refs,
 ):
+    *send_refs, wide = send_refs
     core = info_ref[1]
     span = mix0_ref.shape[1]
     both = s0_ref[...] + s1_ref[...]
@@ -219,19 +222,26 @@
         at = (0, 2, 6, 7, 8)[at]
         small_ref[at : at + value.shape[0], :] = value
     rows = keep1_ref.shape[0]
-    send1_ref[rows : rows + 16, :] = small_ref[:, :span]
-    send1_ref[rows + 16 :, :] = small_ref[:, span:]
-    sends = (send1_ref, send2_ref, send3_ref, send4_ref)
+    piece = send_refs[0].shape[1]
+    for n in range(width // piece):
+        send_refs[0][rows + 16 * n : rows + 16 * (n + 1), :] = small_ref[:, n * piece : (n + 1) * piece]
     for part in range(4):
         order = order1 if part < 2 else order2
-        if part in (0, 2):
+        if part == 0 or (part == 2 and order1 != order2):
             left = [turned(core, height, order, first_ref[of_group(g), :], wide) for g in range(2)]
         if part < 3:
             right = [r[part] for r in (dqkv0_ref, dqkv1_ref)]
         else:
             left = [turned(core, height, order, r[...], wide) for r in (ga0_ref, ga1_ref)]
             right = [filled(r[...], p).astype(BF16) for r, p in zip((mix0_ref, mix1_ref), PADDED)]
-        sends[part][: keep1_ref.shape[0], :] = mm(left[0][1], right[0]) + mm(left[1][1], right[1])
+        at = part * span
+        out = mm(left[0][1], right[0]) + mm(left[1][1], right[1])
+        begin = 0
+        while begin < span:
+            inner = (at + begin) % piece
+            count = min(span - begin, piece - inner)
+            send_refs[(at + begin) // piece][:rows, inner : inner + count] = out[:, begin : begin + count]
+            begin += count
         base = part % 2 * span
         keep_ref = keep1_ref if part < 2 else keep2_ref
         keep_ref[:, base : base + span] = mm(left[0][0], right[0]) + mm(left[1][0], right[1])
@@ -364,12 +374,9 @@
 
 def stage_small_kernel(bit, count, last, info_ref, keep_ref, small_ref, *refs):
     pieces, outs = refs[:count], refs[count:]
-    rows, span = keep_ref.shape[0], pieces[0].shape[1]
-    if count == 2:
-        other = jnp.concatenate([pieces[0][rows : rows + 16, :], pieces[0][rows + 16 :, :]], axis=1)
-    else:
-        other = pieces[0][rows:, :]
-    small = small_ref[...] + other
+    rows = keep_ref.shape[0]
+    parts = [pieces[0][at : at + 16, :] for at in range(rows, pieces[0].shape[0], 16)]
+    small = small_ref[...] + jnp.concatenate(parts, axis=1)
     if last:
         out_ref, total_ref = outs
         total_ref[...] = small
@@ -410,7 +417,7 @@
 
 
 def shaped(*shape, dtype=F32):
-    return jax.ShapeDtypeStruct(shape, dtype)
+    return pltpu.HBM(shape, dtype)
 
 
 def in_vmem(value):
@@ -452,9 +459,9 @@
             out_shape=outs,
             name=name,
             in_specs=[SMEM_SPEC] + [pl.BlockSpec() if plain else VMEM_SPEC] * (count - 1) + [LATER] * len(extra),
-            out_specs=(VMEM_SPEC,) * len(outs),
+            out_specs=tuple(VMEM_SPEC if o.memory_space == pltpu.VMEM else pl.BlockSpec() for o in outs),
             compiler_params=pltpu.CompilerParams(vmem_limit_bytes=room * MIB),
-            cost_estimate=pl.CostEstimate(flops=1, bytes_accessed=1, transcendentals=0),
+            cost_estimate=pl.CostEstimate(flops=COST.get(name, 1), bytes_accessed=1, transcendentals=0),
             **kwargs,
         )(self.info, *map(in_hbm if plain else in_vmem, operands), *extra)
         self.last = results[0]
@@ -592,11 +599,35 @@
         )
         return Scatter(order, dp_size, bit_order, keep, send)
 
-    down_sum = weight_grads("down_weights", first_z, gmlp, act, 768)
-    up_sum = weight_grads("up_weights", first_x, second, gpre, 768)
+    mlp_box = []
+
+    def do_mlp():
+        mlp_box[:] = [order.call(mlp_part_kernel, "mlp_part", held(SENT_ROWS, width), [*act, down_weight], room=8)]
+        if not OPT["relay"]:
+            mlp_box.append(swap_sides(mlp_box[0]))
+
+    if OPT["mlp"] == 0:
+        do_mlp()
+    orders = {k: first_z if k in OPT["z"] else first_x for k in "du12"}
+    down_sum = weight_grads("down_weights", orders["d"], gmlp, act, OPT["dpiece"])
+    up_sum = weight_grads("up_weights", orders["u"], second, gpre, OPT["upiece"])
     down_sum.stage("down")
     up_sum.stage("up")
-    mlp_part = order.call(mlp_part_kernel, "mlp_part", held(SENT_ROWS, width), [*act, down_weight], room=8)
+    if OPT["mlp"] == 1:
+        do_mlp()
+
+    def second_stage():
+        down_sum.stage("down")
+        up_sum.stage("up")
+
+    if OPT["s2"] == 0:
+        second_stage()
+    if OPT["mlp"] == 2:
+        do_mlp()
+    if OPT["relay"]:
+        mlp_box[:] = [order.call(relay_kernel, "mlp_relay", held(SENT_ROWS, width), mlp_box, after=[gs2])]
+        mlp_box.append(swap_sides(mlp_box[0]))
+    mlp_part, mlp2 = mlp_box
 
     def go_back(group, *earlier):
         padded = PADDED[group]
@@ -613,47 +644,80 @@
             scratch_shapes=[pltpu.VMEM((padded, span), BF16)], room=16,
         )
 
-    down_sum.stage("down")
-    up_sum.stage("up")
-    mlp_part = order.call(relay_kernel, "mlp_relay", held(SENT_ROWS, width), [mlp_part], after=[gs2])
-    mlp2 = swap_sides(mlp_part)
     *back1, gf = go_back(1)
+    if OPT["s2"] == 1:
+        second_stage()
     *back0, gf = go_back(0, gf)
     gf2 = swap_sides(gf)
     dqkv, gattn, gh, sums = zip(back0, back1)
-
-    for n in range(3, bits - 1):
-        down_sum.stage("down")
-        up_sum.stage("up")
-    half = (down_sum.keep.shape[0] // 2, 2 * units)
-    both, keep_both = order.call(
-        functools.partial(stage_both_kernel, first_x[-1]), "mlp_3", (held(*half), held(*half)),
-        [down_sum.keep, up_sum.keep, *down_sum.got, *up_sum.got],
-    )
-    got_both = swap_bit(both, dp_size, first_x[-1])
+    if OPT["s2"] == 2:
+        second_stage()
+    both_box = []
+
+    def third_stage():
+        for n in range(3, bits - 1):
+            down_sum.stage("down")
+            up_sum.stage("up")
+        half = (down_sum.keep.shape[0] // 2, 2 * units)
+        both, keep_both = order.call(
+            functools.partial(stage_both_kernel, first_x[-1]), "mlp_3", (held(*half), held(*half)),
+            [down_sum.keep, up_sum.keep, *down_sum.got, *up_sum.got],
+        )
+        both_box[:] = [keep_both, swap_bit(both, dp_size, first_x[-1])]
+
+    if OPT["s3"] == 0:
+        third_stage()
     rows = width // 2
+    piece = OPT["apiece"]
     keep1, keep2, small, *send = order.call(
-        functools.partial(attn_weights_kernel, height, first_x, first_z), "attn_weights",
+        functools.partial(attn_weights_kernel, height, orders["1"], orders["2"]), "attn_weights",
         (
             held(rows, 2 * span), held(rows, 2 * span), held(16, width),
-            held(rows + 32, span), held(rows, span), held(rows, span), held(rows, span),
+            held(rows + 16 * (2 * span // piece), piece), *(held(rows, piece),) * (4 * span // piece - 1),
         ),
         [first, *dqkv, *gattn, *mix, *sums, *upsum, *downsum], room=12,
         scratch_shapes=[pltpu.VMEM((width, max(PADDED)), F32)],
     )
-    attn1 = Scatter(order, dp_size, first_x, keep1, send[:2], small)
-    attn2 = Scatter(order, dp_size, first_z, keep2, send[2:])
+    count = len(send) // 2
+    attn1 = Scatter(order, dp_size, orders["1"], keep1, send[:count], small)
+    if OPT["s3"] == 1:
+        third_stage()
     attn1.stage("attn1")
+    attn2 = Scatter(order, dp_size, orders["2"], keep2, send[count:])
     attn2.stage("attn2")
-    block_out = order.call(
-        output_kernel, "block_out", shaped(*images_in.shape, dtype=BF16),
-        [*hidden, mlp_part, mlp2, down_bias], room=8, scratch_shapes=[pltpu.VMEM(images_in.shape, F32)],
-    )
-
-    def attn_rest():
+    if OPT["s3"] == 2:
+        third_stage()
+
+    def do_block():
+        return order.call(
+            output_kernel, "block_out", shaped(*images_in.shape, dtype=BF16),
+            [*hidden, mlp_part, mlp2, down_bias], room=8, scratch_shapes=[pltpu.VMEM(images_in.shape, F32)],
+        )
+
+    def do_input():
+        return order.call(
+            input_kernel, "input_back", shaped(*images_in.shape), [x_pad, *gh, norm1_gain, gf, gf2], room=8
+        )
+
+    def do_both():
+        return order.call(both_end_kernel, "mlp_end", (shaped(height, units),) * 2, both_box)
+
+    if OPT["block"] == 0:
+        block_out = do_block()
+
+    def attn_more():
         for n in range(1, bits - 1):
             attn1.stage("attn1")
             attn2.stage("attn2")
+            if n == 1 and OPT["block"] == 1:
+                boxes.append(do_block())
+            if n == 1 and OPT["both"] == 1:
+                boxes2.append(do_both())
+
+    boxes, boxes2 = [], []
+
+    def attn_rest():
+        attn_more()
         done1, total = order.call(
             functools.partial(stage_small_kernel, 0, 1, True), "attn1_end", (held(height, width), held(16, width)),
             [attn1.keep, attn1.small, *attn1.got],
@@ -664,14 +728,31 @@
         )
         return (*ends, total)
 
-    qkv_block, out_block, small = order.together(attn_rest, attn1, attn2)
+    if OPT["tail"]:
+        qkv_block, out_block, small = order.together(attn_rest, attn1, attn2)
+    else:
+        attn_more()
+        if OPT["both"] == 2:
+            boxes2.append(do_both())
+        if OPT["input"] == 0:
+            input_grad = do_input()
+        done1, small = order.call(
+            functools.partial(stage_small_kernel, 0, 1, True), "attn1_end", (held(height, width), held(16, width)),
+            [attn1.keep, attn1.small, *attn1.got],
+        )
+        if OPT["block"] == 1:
+            block_out = boxes[0]
     small2 = swap_sides(small)
-    down_block, up_block = order.call(
-        both_end_kernel, "mlp_end", (shaped(height, units),) * 2, [keep_both, got_both]
-    )
-    input_grad = order.call(
-        input_kernel, "input_back", shaped(*images_in.shape), [x_pad, *gh, norm1_gain, gf, gf2], room=8
-    )
+    if OPT["block"] == 2:
+        block_out = do_block()
+    down_block, up_block = boxes2[0] if boxes2 else do_both()
+    if OPT["tail"] or OPT["input"] == 1:
+        input_grad = do_input()
+    if not OPT["tail"]:
+        qkv_block, out_block = order.call(
+            attn_last_kernel, "attn_end", (shaped(3, height, span), shaped(height, span)),
+            [done1, attn2.keep, *attn2.got],
+        )
     vector = shaped(width)
     small_out = order.call(
         small_end_kernel, "small_end",

time: 191 us -> 161 us (0.84)
  waiting for transfers between devices: 86.2 us -> 68.1 us
  Pallas kernels: 64 us -> 56.6 us
  local copies, waits for them, and re-layouts: 8.54 us -> 4.61 us
    ppermute x22, waiting for transfers between devices: 51 us -> 34.2 us  [swap_bit(): return lax.ppermute(value, 'dp', [(i, i ^ 1 << bit) for i in range(size)])]
    pallas_call x30 -> x29, Pallas kernels: 64 us -> 56.6 us  [call(): pl.pallas_call(body, out_shape=outs, name=name, in_specs=[SMEM_SPEC] + [p...]
    unnamed x50 -> x28, local copies, waits for them, and re-layouts: 8.46 us -> 4.52 us
  transfers between devices with their start and end apart: 29 -> 29, of which waited for: 13 -> 16; matrix products, arithmetic and copies ran while one was open for 1% -> 0% of each run, Pallas kernels for 27% -> 32%
where the time goes in v3:
time: 161 us
  waiting for transfers between devices  68.1 us (42%)
  Pallas kernels  56.6 us (35%)
  starting transfers between devices  28.1 us (17%)
  local copies, waits for them, and re-layouts  4.61 us (3%)
  between operations  2.3 us (1%)
    pallas_call x29, Pallas kernels, call(): pl.pallas_call(body, out_shape=outs, name=name, in_specs=[SMEM_SPEC] + [p...  56.6 us
    ppermute x22, waiting for transfers between devices, swap_bit(): return lax.ppermute(value, 'dp', [(i, i ^ 1 << bit) for i in range(size)])  34.2 us
    ppermute x7, waiting for transfers between devices, swap_sides(): return lax.ppermute(value, 'tensor', [(0, 1), (1, 0)])  34 us
    ppermute x22, starting transfers between devices, swap_bit(): return lax.ppermute(value, 'dp', [(i, i ^ 1 << bit) for i in range(size)])  18.8 us
    ppermute x7, starting transfers between devices, swap_sides(): return lax.ppermute(value, 'tensor', [(0, 1), (1, 0)])  9.32 us
    unnamed x28, local copies, waits for them, and re-layouts  4.52 us
  transfers between devices with their start and end apart: 29, of which 16 were waited for; matrix products, arithmetic and copies ran while one was open for 0% of the time, Pallas kernels for 32%

profile of v3, /device:TPU:0, one launch (start us, length us, event | category | flops | bytes accessed | tf_op | source)
XLA Modules:
  0.0 160.7 jit_solution(15873883849905332115)
XLA Ops:
  1.6 3.0 %collective-permute-start.1 = (f32[96,768]{1,0:T(8,128)S(1)}, f32[96,768]{1,0:T(8,128)S(1)}, u32[]{:S(2)}, u32[]{:S(2)}) collective-permute-start(f32[96,768]{1,0:T(8,128)S(1)} %dynamic-slice_convert_fusion), channel_id=1, source_target_pairs={{0,1},{1,0},{2,3},{3,2},{4,5},{5,4},{6,7},{7,6},{8,9},{9,8},{10,11... | collective-permute-start | bytes 884744 | tf_op jit(solution)/shard_map/ppermute | solution.py:472
  6.0 7.9 %attn_forward.1 = (bf16[544,768]{1,0:T(8,128)(2,1)S(1)}, bf16[3,544,384]{2,1,0:T(8,128)(2,1)S(1)}, bf16[544,768]{1,0:T(8,128)(2,1)S(1)}, bf16[544,768]{1,0:T(8,1...) custom-call(s32[8]{0:T(128)S(1)} %stack.27.refs_0_, ...), custom_call_target="tpu_custom_call" | custom-call | flops 1 | bytes 1 | tf_op jit(solution)/shard_map/attn_forward/pallas_call | solution.py:457
  18.1 5.0 %collective-permute-done.2.refs_1_ = f32[96,768]{1,0:T(8,128)S(1)} collective-permute-done((f32[96,768]{1,0:T(8,128)S(1)}, f32[96,768]{1,0:T(8,128)S(1)}, u32[]{:S(2)}, u32[]{:S(2)}) %collective-permute-start.2) | collective-permute-done | bytes 294944 | tf_op jit(solution)/shard_map/ppermute | solution.py:476
  25.9 4.5 %collective-permute-done.5.refs_4_ = f32[328,384]{1,0:T(8,128)S(1)} collective-permute-done((f32[328,384]{1,0:T(8,128)S(1)}, f32[328,384]{1,0:T(8,128)S(1)}, u32[]{:S(2)}, u32[]{:S(2)}) %collective-permute-start.5) | collective-permute-done | bytes 503840 | tf_op jit(solution)/shard_map/ppermute | solution.py:472
  30.5 4.8 %mlp_b.1 = (f32[336,768]{1,0:T(8,128)S(1)}, bf16[336,768]{1,0:T(8,128)(2,1)S(1)}, bf16[336,768]{1,0:T(8,128)(2,1)S(1)}, bf16[336,1536]{1,0:T(8,128)(2,1)S(1)}, b...) custom-call(s32[8]{0:T(128)S(1)} %stack.27.refs_0_, ...), custom_call_target="tpu_custom_call" | custom-call | flops 1 | bytes 1 | tf_op jit(solution)/shard_map/mlp_b/pallas_call | solution.py:457
  35.3 3.6 %mlp_a.1 = (f32[208,768]{1,0:T(8,128)S(1)}, bf16[208,768]{1,0:T(8,128)(2,1)S(1)}, bf16[208,768]{1,0:T(8,128)(2,1)S(1)}, bf16[208,1536]{1,0:T(8,128)(2,1)S(1)}, b...) custom-call(s32[8]{0:T(128)S(1)} %stack.27.refs_0_, ...), custom_call_target="tpu_custom_call" | custom-call | flops 1 | bytes 1 | tf_op jit(solution)/shard_map/mlp_a/pallas_call | solution.py:457
  39.5 3.0 %down_weights.1 = (f32[384,1536]{1,0:T(8,128)S(1)}, f32[384,768]{1,0:T(8,128)S(1)}, f32[384,768]{1,0:T(8,128)S(1)}) custom-call(s32[8]{0:T(128)S(1)} %stack.27.refs_0_, bf16[208,768]{1,0:T(8,128)(2,1)S(1)} %get-tuple-element.114.refs_1_, bf16[336,768]{1,0:T(8,128)(2,1)S(1)} %get-tuple-element.115.refs_2_, ...), custom_call_target="tpu_custom_call" | custom-call | flops 1 | bytes 1 | tf_op jit(solution)/shard_map/down_weights/pallas_call | solution.py:457
  43.2 2.8 %up_weights.1 = (f32[384,1536]{1,0:T(8,128)S(1)}, f32[384,768]{1,0:T(8,128)S(1)}, f32[384,768]{1,0:T(8,128)S(1)}) custom-call(s32[8]{0:T(128)S(1)} %stack.27.refs_0_, bf16[208,768]{1,0:T(8,128)(2,1)S(1)} %get-tuple-element.110.refs_1_, bf16[336,768]{1,0:T(8,128)(2,1)S(1)} %get-tuple-element.111.refs_2_, bf16[208,1536]{1,0:T(8,128)(2,1)S(1)} %get-tuple-element.112.refs_3_, ...), custom_call_target="tpu_custom_call" | custom-call | flops 1 | bytes 1 | tf_op jit(solution)/shard_map/up_weights/pallas_call | solution.py:457
  48.9 1.7 %collective-permute-done.7.refs_3_ = f32[384,768]{1,0:T(8,128)S(1)} collective-permute-done((f32[384,768]{1,0:T(8,128)S(1)}, f32[384,768]{1,0:T(8,128)S(1)}, u32[]{:S(2)}, u32[]{:S(2)}) %collective-permute-start.7) | collective-permute-done | bytes 1179680 | tf_op jit(solution)/shard_map/ppermute | solution.py:476
  51.4 2.0 %mlp_part.1.refs_11_.refs_3_ = f32[528,768]{1,0:T(8,128)S(1)} custom-call(s32[8]{0:T(128)S(1)} %stack.27.refs_0_, bf16[208,1536]{1,0:T(8,128)(2,1)S(1)} %get-tuple-element.108.refs_3_.refs_1_, bf16[336,1536]{1,0:T(8,128)(2,1)S(1)} %get-tuple-element.109.refs_4_.refs_2_, bf16[1536,768]{1,0:T(8,128)(2,1)S(1)} %copy-done, ...), custom_call_target="tpu_custom_call" | custom-call | flops 1 | bytes 1 | tf_op jit(solution)/shard_map/mlp_part/pallas_call | solution.py:457
  56.6 20.8 %collective-permute-done.11.refs_2_ = f32[528,768]{1,0:T(8,128)S(1)} collective-permute-done((f32[528,768]{1,0:T(8,128)S(1)}, f32[528,768]{1,0:T(8,128)S(1)}, u32[]{:S(2)}, u32[]{:S(2)}) %collective-permute-start.11) | collective-permute-done | bytes 1622048 | tf_op jit(solution)/shard_map/ppermute | solution.py:472
  77.4 6.1 %attn_backward_b.1 = (bf16[3,336,384]{2,1,0:T(8,128)(2,1)S(1)}, bf16[336,768]{1,0:T(8,128)(2,1)S(1)}, f32[336,768]{1,0:T(8,128)S(1)}, f32[8,768]{1,0:T(8,128)S(1)}, f32[328,768]{1,0:T(8,128)S(1)}) custom-call(s32[8]{0:T(128)S(1)} %stack.27.refs_0_, f32[528,768]{1,0:T(8,128)S(1)} %get-tuple-element.124.refs_1_, ...), custom_call_target="tpu_custom_call" | custom-call | flops 99999997952 | bytes 1 | tf_op jit(solution)/shard_map/attn_backward_b/pallas_call | solution.py:457
  87.1 4.3 %attn_backward_a.1 = (bf16[3,208,384]{2,1,0:T(8,128)(2,1)S(1)}, bf16[208,768]{1,0:T(8,128)(2,1)S(1)}, f32[208,768]{1,0:T(8,128)S(1)}, f32[8,768]{1,0:T(8,128)S(1)}, f32[528,768]{1,0:T(8,128)S(1)}) custom-call(s32[8]{0:T(128)S(1)} %stack.27.refs_0_, f32[528,768]{1,0:T(8,128)S(1)} %get-tuple-element.124.refs_1_, ...), custom_call_target="tpu_custom_call" | custom-call | flops 1 | bytes 1 | tf_op jit(solution)/shard_map/attn_backward_a/pallas_call | solution.py:457
  91.4 3.3 %attn_weights.1 = (f32[384,768]{1,0:T(8,128)S(1)}, f32[384,768]{1,0:T(8,128)S(1)}, f32[16,768]{1,0:T(8,128)S(1)}, f32[416,384]{1,0:T(8,128)S(1)}, f32[384,384]{1...) custom-call(s32[8]{0:T(128)S(1)} %stack.27.refs_0_, ...), custom_call_target="tpu_custom_call" | custom-call | flops 1 | bytes 1 | tf_op jit(solution)/shard_map/attn_weights/pallas_call | solution.py:457
  99.6 2.6 %collective-permute-start.21 = (f32[48,3072]{1,0:T(8,128)S(1)}, f32[48,3072]{1,0:T(8,128)S(1)}, u32[]{:S(2)}, u32[]{:S(2)}) collective-permute-start(f32[48,3072]{1,0:T(8,128)S(1)} %get-tuple-element.152.refs_5_), channel_id=1, source_target_pairs={{0,16},{2,18},{4,20},{6,22},{8,24},{10,26},{12,28},{14,30},{16,0},... | collective-permute-start | bytes 1769480 | tf_op jit(solution)/shard_map/ppermute | solution.py:476
  105.8 6.3 %collective-permute-done.10.refs_4_ = f32[528,768]{1,0:T(8,128)S(1)} collective-permute-done((f32[528,768]{1,0:T(8,128)S(1)}, f32[528,768]{1,0:T(8,128)S(1)}, u32[]{:S(2)}, u32[]{:S(2)}) %collective-permute-start.10) | collective-permute-done | bytes 1622048 | tf_op jit(solution)/shard_map/ppermute | solution.py:472
  112.2 2.1 %block_out.1.refs_4_ = bf16[522,768]{1,0:T(8,128)(2,1)} custom-call(s32[8]{0:T(128)S(1)} %stack.27.refs_0_, f32[208,768]{1,0:T(8,128)S(1)} %get-tuple-element.107.refs_5_.refs_4_.refs_1_, f32[336,768]{1,0:T(8,128)S(1)} %get-tuple-element.106.refs_13_.refs_4_.refs_2_, f32[528,768]{1,0:T(8,128)S(1)} %mlp_part.1.refs_11_.refs_3_, ...), custom_call_target="tpu_custom_call" | custom-call | flops 99999997952 | bytes 1 | tf_op jit(solution)/shard_map/block_out/pallas_call | solution.py:457
  114.3 6.0 %collective-permute-done.23.refs_3_ = f32[208,768]{1,0:T(8,128)S(1)} collective-permute-done((f32[208,768]{1,0:T(8,128)S(1)}, f32[208,768]{1,0:T(8,128)S(1)}, u32[]{:S(2)}, u32[]{:S(2)}) %collective-permute-start.23) | collective-permute-done | bytes 639008 | tf_op jit(solution)/shard_map/ppermute | solution.py:476
  123.7 7.9 %collective-permute-done.22.refs_2_ = f32[192,768]{1,0:T(8,128)S(1)} collective-permute-done((f32[192,768]{1,0:T(8,128)S(1)}, f32[192,768]{1,0:T(8,128)S(1)}, u32[]{:S(2)}, u32[]{:S(2)}) %collective-permute-start.22) | collective-permute-done | bytes 589856 | tf_op jit(solution)/shard_map/ppermute | solution.py:476
  133.9 2.0 %collective-permute-done.25.refs_3_ = f32[112,768]{1,0:T(8,128)S(1)} collective-permute-done((f32[112,768]{1,0:T(8,128)S(1)}, f32[112,768]{1,0:T(8,128)S(1)}, u32[]{:S(2)}, u32[]{:S(2)}) %collective-permute-start.25) | collective-permute-done | bytes 344096 | tf_op jit(solution)/shard_map/ppermute | solution.py:476
  138.1 4.9 %collective-permute-done.24.refs_2_ = f32[96,768]{1,0:T(8,128)S(1)} collective-permute-done((f32[96,768]{1,0:T(8,128)S(1)}, f32[96,768]{1,0:T(8,128)S(1)}, u32[]{:S(2)}, u32[]{:S(2)}) %collective-permute-start.24) | collective-permute-done | bytes 294944 | tf_op jit(solution)/shard_map/ppermute | solution.py:476
  147.2 2.9 %input_back.1.refs_4_ = f32[522,768]{1,0:T(8,128)} custom-call(s32[8]{0:T(128)S(1)} %stack.27.refs_0_, bf16[544,768]{1,0:T(8,128)(2,1)S(1)} %get-tuple-element.100.refs_1_.refs_3_, f32[208,768]{1,0:T(8,128)S(1)} %get-tuple-element.155.refs_2_, f32[336,768]{1,0:T(8,128)S(1)} %get-tuple-element.156.refs_3_, f32[768]{0:T(1024)S(1)} %copy-done.10, ...), custom_call_target="tpu_custom_call" | custom-call | flops 1 | bytes 1 | tf_op jit(solution)/shard_map/input_back/pallas_call | solution.py:457
  150.1 2.3 %collective-permute-done.26.refs_3_ = f32[64,768]{1,0:T(8,128)S(1)} collective-permute-done((f32[64,768]{1,0:T(8,128)S(1)}, f32[64,768]{1,0:T(8,128)S(1)}, u32[]{:S(2)}, u32[]{:S(2)}) %collective-permute-start.26) | collective-permute-done | bytes 196640 | tf_op jit(solution)/shard_map/ppermute | solution.py:476
  156.3 2.3 %collective-permute-done.27.refs_2_ = f32[16,768]{1,0:T(8,128)S(1)} collective-permute-done((f32[16,768]{1,0:T(8,128)S(1)}, f32[16,768]{1,0:T(8,128)S(1)}, u32[]{:S(2)}, u32[]{:S(2)}) %collective-permute-start.27) | collective-permute-done | bytes 49184 | tf_op jit(solution)/shard_map/ppermute | solution.py:472
  (93 shorter events, 46.1 us)
Async XLA Ops:
  1.6 12.3 %collective-permute-start.1 = (f32[96,768]{1,0:T(8,128)S(1)}, f32[96,768]{1,0:T(8,128)S(1)}, u32[]{:S(2)}, u32[]{:S(2)}) collective-permute-start(f32[96,768]{1,0:T(8,128)S(1)} %dynamic-slice_convert_fusion), channel_id=1, source_target_pairs={{0,1},{1,0},{2,3},{3,2},{4,5},{5,4},{6,7},{7,6},{8,9},{9,8},{10,11... | collective-permute-start | bytes 884744 | tf_op jit(solution)/shard_map/ppermute | solution.py:472
  14.5 8.5 %collective-permute-start.2 = (f32[96,768]{1,0:T(8,128)S(1)}, f32[96,768]{1,0:T(8,128)S(1)}, u32[]{:S(2)}, u32[]{:S(2)}) collective-permute-start(f32[96,768]{1,0:T(8,128)S(1)} %out_weight_relay.1.refs_2_), channel_id=1, source_target_pairs={{0,4},{2,6},{4,0},{6,2},{8,12},{10,14},{12,8},{14,10},{16,20},{18,... | collective-permute-start | bytes 884744 | tf_op jit(solution)/shard_map/ppermute | solution.py:476
  16.0 14.4 %collective-permute-start.5 = (f32[328,384]{1,0:T(8,128)S(1)}, f32[328,384]{1,0:T(8,128)S(1)}, u32[]{:S(2)}, u32[]{:S(2)}) collective-permute-start(f32[328,384]{1,0:T(8,128)S(1)} %get-tuple-element.104.refs_3_.refs_7_), channel_id=1, source_target_pairs={{0,1},{1,0},{2,3},{3,2},{4,5},{5,4},{6,7},{7,6},{8,9},{9,8},{10,11... | collective-permute-start | bytes 1511432 | tf_op jit(solution)/shard_map/ppermute | solution.py:472
  16.5 18.8 %collective-permute-start = (f32[200,384]{1,0:T(8,128)S(1)}, f32[200,384]{1,0:T(8,128)S(1)}, u32[]{:S(2)}, u32[]{:S(2)}) collective-permute-start(f32[200,384]{1,0:T(8,128)S(1)} %get-tuple-element.102.refs_3_.refs_6_), channel_id=1, source_target_pairs={{0,1},{1,0},{2,3},{3,2},{4,5},{5,4},{6,7},{7,6},{8,9},{9,8},{10,11... | collective-permute-start | bytes 921608 | tf_op jit(solution)/shard_map/ppermute | solution.py:472
  18.1 5.7 %collective-permute-start.3 = (f32[96,768]{1,0:T(8,128)S(1)}, f32[96,768]{1,0:T(8,128)S(1)}, u32[]{:S(2)}, u32[]{:S(2)}) collective-permute-start(f32[96,768]{1,0:T(8,128)S(1)} %out_weight_relay.1.refs_2_), channel_id=1, source_target_pairs={{0,2},{2,0},{4,6},{6,4},{8,10},{10,8},{12,14},{14,12},{16,18},{18,... | collective-permute-start | bytes 884744 | tf_op jit(solution)/shard_map/ppermute | solution.py:476
  39.0 38.5 %collective-permute-start.11 = (f32[528,768]{1,0:T(8,128)S(1)}, f32[528,768]{1,0:T(8,128)S(1)}, u32[]{:S(2)}, u32[]{:S(2)}) collective-permute-start(f32[528,768]{1,0:T(8,128)S(1)} %get-tuple-element.124.refs_1_), channel_id=1, source_target_pairs={{0,1},{1,0},{2,3},{3,2},{4,5},{5,4},{6,7},{7,6},{8,9},{9,8},{10,11... | collective-permute-start | bytes 4866056 | tf_op jit(solution)/shard_map/ppermute | solution.py:472
  42.7 4.5 %collective-permute-start.9 = (f32[384,768]{1,0:T(8,128)S(1)}, f32[384,768]{1,0:T(8,128)S(1)}, u32[]{:S(2)}, u32[]{:S(2)}) collective-permute-start(f32[384,768]{1,0:T(8,128)S(1)} %get-tuple-element.121), channel_id=1, source_target_pairs={{0,2},{2,0},{4,6},{6,4},{8,10},{10,8},{12,14},{14,12},{16,18},{18,... | collective-permute-start | bytes 3538952 | tf_op jit(solution)/shard_map/ppermute | solution.py:476
  46.1 4.5 %collective-permute-start.7 = (f32[384,768]{1,0:T(8,128)S(1)}, f32[384,768]{1,0:T(8,128)S(1)}, u32[]{:S(2)}, u32[]{:S(2)}) collective-permute-start(f32[384,768]{1,0:T(8,128)S(1)} %get-tuple-element.119), channel_id=1, source_target_pairs={{0,2},{2,0},{4,6},{6,4},{8,10},{10,8},{12,14},{14,12},{16,18},{18,... | collective-permute-start | bytes 3538952 | tf_op jit(solution)/shard_map/ppermute | solution.py:476
  48.0 35.5 %collective-permute-start.13 = (f32[192,1536]{1,0:T(8,128)S(1)}, f32[192,1536]{1,0:T(8,128)S(1)}, u32[]{:S(2)}, u32[]{:S(2)}) collective-permute-start(f32[192,1536]{1,0:T(8,128)S(1)} %get-tuple-element.122.refs_4_), channel_id=1, source_target_pairs={{0,4},{2,6},{4,0},{6,2},{8,12},{10,14},{12,8},{14,10},{16,20},{18,... | collective-permute-start | bytes 3538952 | tf_op jit(solution)/shard_map/ppermute | solution.py:476
  53.4 30.8 %collective-permute-start.12 = (f32[192,1536]{1,0:T(8,128)S(1)}, f32[192,1536]{1,0:T(8,128)S(1)}, u32[]{:S(2)}, u32[]{:S(2)}) collective-permute-start(f32[192,1536]{1,0:T(8,128)S(1)} %get-tuple-element.123.refs_4_), channel_id=1, source_target_pairs={{0,8},{2,10},{4,12},{6,14},{8,0},{10,2},{12,4},{14,6},{16,24},{18,... | collective-permute-start | bytes 3538952 | tf_op jit(solution)/shard_map/ppermute | solution.py:476
  55.1 57.1 %collective-permute-start.10 = (f32[528,768]{1,0:T(8,128)S(1)}, f32[528,768]{1,0:T(8,128)S(1)}, u32[]{:S(2)}, u32[]{:S(2)}) collective-permute-start(f32[528,768]{1,0:T(8,128)S(1)} %mlp_part.1.refs_11_.refs_3_), channel_id=1, source_target_pairs={{0,1},{1,0},{2,3},{3,2},{4,5},{5,4},{6,7},{7,6},{8,9},{9,8},{10,11... | collective-permute-start | bytes 4866056 | tf_op jit(solution)/shard_map/ppermute | solution.py:472
  85.0 11.9 %collective-permute-start.19 = (f32[96,1536]{1,0:T(8,128)S(1)}, f32[96,1536]{1,0:T(8,128)S(1)}, u32[]{:S(2)}, u32[]{:S(2)}) collective-permute-start(f32[96,1536]{1,0:T(8,128)S(1)} %get-tuple-element.133.refs_12_), channel_id=1, source_target_pairs={{0,4},{2,6},{4,0},{6,2},{8,12},{10,14},{12,8},{14,10},{16,20},{18,... | collective-permute-start | bytes 1769480 | tf_op jit(solution)/shard_map/ppermute | solution.py:476
  85.6 11.4 %collective-permute-start.18 = (f32[96,1536]{1,0:T(8,128)S(1)}, f32[96,1536]{1,0:T(8,128)S(1)}, u32[]{:S(2)}, u32[]{:S(2)}) collective-permute-start(f32[96,1536]{1,0:T(8,128)S(1)} %get-tuple-element.132.refs_3_), channel_id=1, source_target_pairs={{0,8},{2,10},{4,12},{6,14},{8,0},{10,2},{12,4},{14,6},{16,24},{18,... | collective-permute-start | bytes 1769480 | tf_op jit(solution)/shard_map/ppermute | solution.py:476
  94.7 4.9 %collective-permute-start.16 = (f32[416,384]{1,0:T(8,128)S(1)}, f32[416,384]{1,0:T(8,128)S(1)}, u32[]{:S(2)}, u32[]{:S(2)}) collective-permute-start(f32[416,384]{1,0:T(8,128)S(1)} %get-tuple-element.148), channel_id=1, source_target_pairs={{0,2},{2,0},{4,6},{6,4},{8,10},{10,8},{12,14},{14,12},{16,18},{18,... | collective-permute-start | bytes 1916936 | tf_op jit(solution)/shard_map/ppermute | solution.py:476
  96.8 6.1 %collective-permute-start.14 = (f32[384,384]{1,0:T(8,128)S(1)}, f32[384,384]{1,0:T(8,128)S(1)}, u32[]{:S(2)}, u32[]{:S(2)}) collective-permute-start(f32[384,384]{1,0:T(8,128)S(1)} %get-tuple-element.144), channel_id=1, source_target_pairs={{0,2},{2,0},{4,6},{6,4},{8,10},{10,8},{12,14},{14,12},{16,18},{18,... | collective-permute-start | bytes 1769480 | tf_op jit(solution)/shard_map/ppermute | solution.py:476
  97.0 7.3 %collective-permute-start.15 = (f32[384,384]{1,0:T(8,128)S(1)}, f32[384,384]{1,0:T(8,128)S(1)}, u32[]{:S(2)}, u32[]{:S(2)}) collective-permute-start(f32[384,384]{1,0:T(8,128)S(1)} %get-tuple-element.145), channel_id=1, source_target_pairs={{0,2},{2,0},{4,6},{6,4},{8,10},{10,8},{12,14},{14,12},{16,18},{18,... | collective-permute-start | bytes 1769480 | tf_op jit(solution)/shard_map/ppermute | solution.py:476
  98.0 48.2 %collective-permute-start.20 = (f32[528,768]{1,0:T(8,128)S(1)}, f32[528,768]{1,0:T(8,128)S(1)}, u32[]{:S(2)}, u32[]{:S(2)}) collective-permute-start(f32[528,768]{1,0:T(8,128)S(1)} %get-tuple-element.157.refs_5_), channel_id=1, source_target_pairs={{0,1},{1,0},{2,3},{3,2},{4,5},{5,4},{6,7},{7,6},{8,9},{9,8},{10,11... | collective-permute-start | bytes 4866056 | tf_op jit(solution)/shard_map/ppermute | solution.py:472
  99.6 45.2 %collective-permute-start.21 = (f32[48,3072]{1,0:T(8,128)S(1)}, f32[48,3072]{1,0:T(8,128)S(1)}, u32[]{:S(2)}, u32[]{:S(2)}) collective-permute-start(f32[48,3072]{1,0:T(8,128)S(1)} %get-tuple-element.152.refs_5_), channel_id=1, source_target_pairs={{0,16},{2,18},{4,20},{6,22},{8,24},{10,26},{12,28},{14,30},{16,0},... | collective-permute-start | bytes 1769480 | tf_op jit(solution)/shard_map/ppermute | solution.py:476
  103.0 17.4 %collective-permute-start.23 = (f32[208,768]{1,0:T(8,128)S(1)}, f32[208,768]{1,0:T(8,128)S(1)}, u32[]{:S(2)}, u32[]{:S(2)}) collective-permute-start(f32[208,768]{1,0:T(8,128)S(1)} %get-tuple-element.153.refs_4_), channel_id=1, source_target_pairs={{0,4},{2,6},{4,0},{6,2},{8,12},{10,14},{12,8},{14,10},{16,20},{18,... | collective-permute-start | bytes 1916936 | tf_op jit(solution)/shard_map/ppermute | solution.py:476
  105.0 26.6 %collective-permute-start.22 = (f32[192,768]{1,0:T(8,128)S(1)}, f32[192,768]{1,0:T(8,128)S(1)}, u32[]{:S(2)}, u32[]{:S(2)}) collective-permute-start(f32[192,768]{1,0:T(8,128)S(1)} %get-tuple-element.154.refs_6_), channel_id=1, source_target_pairs={{0,4},{2,6},{4,0},{6,2},{8,12},{10,14},{12,8},{14,10},{16,20},{18,... | collective-permute-start | bytes 1769480 | tf_op jit(solution)/shard_map/ppermute | solution.py:476
  122.1 13.8 %collective-permute-start.25 = (f32[112,768]{1,0:T(8,128)S(1)}, f32[112,768]{1,0:T(8,128)S(1)}, u32[]{:S(2)}, u32[]{:S(2)}) collective-permute-start(f32[112,768]{1,0:T(8,128)S(1)} %get-tuple-element.162.refs_3_), channel_id=1, source_target_pairs={{0,8},{2,10},{4,12},{6,14},{8,0},{10,2},{12,4},{14,6},{16,24},{18,... | collective-permute-start | bytes 1032200 | tf_op jit(solution)/shard_map/ppermute | solution.py:476
  132.2 10.8 %collective-permute-start.24 = (f32[96,768]{1,0:T(8,128)S(1)}, f32[96,768]{1,0:T(8,128)S(1)}, u32[]{:S(2)}, u32[]{:S(2)}) collective-permute-start(f32[96,768]{1,0:T(8,128)S(1)} %get-tuple-element.164.refs_4_), channel_id=1, source_target_pairs={{0,8},{2,10},{4,12},{6,14},{8,0},{10,2},{12,4},{14,6},{16,24},{18,... | collective-permute-start | bytes 884744 | tf_op jit(solution)/shard_map/ppermute | solution.py:476
  136.5 16.0 %collective-permute-start.26 = (f32[64,768]{1,0:T(8,128)S(1)}, f32[64,768]{1,0:T(8,128)S(1)}, u32[]{:S(2)}, u32[]{:S(2)}) collective-permute-start(f32[64,768]{1,0:T(8,128)S(1)} %get-tuple-element.167.refs_3_), channel_id=1, source_target_pairs={{0,16},{2,18},{4,20},{6,22},{8,24},{10,26},{12,28},{14,30},{16,0},... | collective-permute-start | bytes 589832 | tf_op jit(solution)/shard_map/ppermute | solution.py:476
  143.6 11.4 %collective-permute-start.28 = (f32[48,768]{1,0:T(8,128)S(1)}, f32[48,768]{1,0:T(8,128)S(1)}, u32[]{:S(2)}, u32[]{:S(2)}) collective-permute-start(f32[48,768]{1,0:T(8,128)S(1)} %get-tuple-element.168.refs_3_), channel_id=1, source_target_pairs={{0,16},{2,18},{4,20},{6,22},{8,24},{10,26},{12,28},{14,30},{16,0},... | collective-permute-start | bytes 442376 | tf_op jit(solution)/shard_map/ppermute | solution.py:476
  (19 other events, 126.4 us)

commit v4 on v2

--- a/solution.py
+++ b/solution.py
@@ -20,6 +20,7 @@
 F32 = jnp.float32
 BF16 = jnp.bfloat16
 MIB = 1024 * 1024
+COST = {"attn_backward_b": 10**11, "block_out": 10**11, "mlp_3": 7 * 10**9}
 NT = ((1,), (1,))
 TN = ((0,), (0,))
 
@@ -136,11 +137,21 @@
         ow_all[pl.ds(at, quarter), :] = ref[...].astype(BF16)
 
 
+def grad_act_kernel(info_ref, ct_ref, down_ref, *refs):
+    for group in range(2):
+        gmlp_ref, gact_ref, downsum_ref = refs[3 * group : 3 * group + 3]
+        gmlp = live_of(info_ref, group) * ct_ref[of_group(group), :].astype(F32)
+        downsum_ref[...] = col_sum(gmlp)
+        gmlp = gmlp.astype(BF16)
+        gmlp_ref[...] = gmlp
+        gact_ref[...] = mm(gmlp, down_ref[...], NT)
+
+
 def mlp_kernel(
-    group, chunk, info_ref, x_ref, ct_ref, mix_ref, mix2_ref, ow_ref, ob_ref, gain_ref, bias_ref,
-    up_ref, upb_ref, down_ref, *refs,
+    group, chunk, info_ref, x_ref, gact_ref, mix_ref, mix2_ref, ow_ref, ob_ref, gain_ref, bias_ref,
+    up_ref, upb_ref, *refs,
 ):
-    *earlier, hidden_ref, second_ref, gmlp_ref, act_ref, gpre_ref, upsum_ref, downsum_ref, gs_ref, mix_all = refs
+    *earlier, hidden_ref, second_ref, act_ref, gpre_ref, upsum_ref, gs_ref, mix_all = refs
     side, live = info_ref[0], live_of(info_ref, group)
     span = mix_ref.shape[1]
     for which, ref in ((side, mix_ref), (1 - side, mix2_ref)):
@@ -152,10 +163,6 @@
     normed, _ = norm_parts(hidden)
     second = (normed * row(gain_ref) + row(bias_ref)).astype(BF16)
     second_ref[...] = second
-    gmlp = live * ct_ref[of_group(group), :].astype(F32)
-    downsum_ref[...] = col_sum(gmlp)
-    gmlp = gmlp.astype(BF16)
-    gmlp_ref[...] = gmlp
     bias = row(upb_ref)
     rows = slice(None)
     if earlier:
@@ -167,7 +174,7 @@
         cdf = 0.5 * (1.0 + lax.erf(pre * (0.5**0.5)))
         act_ref[:, cols] = (pre * cdf).astype(BF16)
         slope = cdf + pre * (jnp.exp(-0.5 * pre * pre) * 0.3989422804014327)
-        gpre = (mm(gmlp, down_ref[cols, :], NT) * slope).astype(BF16)
+        gpre = (gact_ref[:, cols] * slope).astype(BF16)
         gpre_ref[:, cols] = gpre
         upsum_ref[:, cols] = col_sum(gpre.astype(F32))
         part = mm(gpre, up_ref[:, cols], NT)[: SENT[group]]
@@ -204,51 +211,71 @@
 
 
 def attn_weights_kernel(
-    height, order1, order2, info_ref, first_ref, dqkv0_ref, dqkv1_ref, ga0_ref, ga1_ref, mix0_ref, mix1_ref,
+    height, order, info_ref, first_ref, dqkv0_ref, dqkv1_ref, ga0_ref, ga1_ref, mix0_ref, mix1_ref,
     s0_ref, s1_ref, u0_ref, u1_ref, d0_ref, d1_ref,
-    keep1_ref, keep2_ref, small_ref, send1_ref, send2_ref, send3_ref, send4_ref, wide,
+    keep1_ref, keep2_ref, small_ref, send1_ref, send2_ref, wide,
 ):
     core = info_ref[1]
-    span = mix0_ref.shape[1]
+    rows, span = keep1_ref.shape[0], mix0_ref.shape[1]
     both = s0_ref[...] + s1_ref[...]
     up = u0_ref[...] + u1_ref[...]
-    down = d0_ref[...] + d1_ref[...]
     width = small_ref.shape[1]
     small_ref[...] = jnp.zeros_like(small_ref)
-    for at, value in enumerate((both[4:6], both[0:4], up[:, :width], up[:, width:], down)):
-        at = (0, 2, 6, 7, 8)[at]
-        small_ref[at : at + value.shape[0], :] = value
-    rows = keep1_ref.shape[0]
-    send1_ref[rows : rows + 16, :] = small_ref[:, :span]
-    send1_ref[rows + 16 :, :] = small_ref[:, span:]
-    sends = (send1_ref, send2_ref, send3_ref, send4_ref)
+    small_ref[0:2, :] = both[4:6]
+    small_ref[2:6, :] = both[0:4]
+    small_ref[6:7, :] = up[:, :width]
+    small_ref[7:8, :] = up[:, width:]
+    small_ref[8:9, :] = d0_ref[...] + d1_ref[...]
+    send1_ref[rows:, :] = small_ref[...]
+    left = [turned(core, height, order, first_ref[of_group(g), :], wide) for g in range(2)]
     for part in range(4):
-        order = order1 if part < 2 else order2
-        if part in (0, 2):
-            left = [turned(core, height, order, first_ref[of_group(g), :], wide) for g in range(2)]
         if part < 3:
             right = [r[part] for r in (dqkv0_ref, dqkv1_ref)]
         else:
             left = [turned(core, height, order, r[...], wide) for r in (ga0_ref, ga1_ref)]
             right = [filled(r[...], p).astype(BF16) for r, p in zip((mix0_ref, mix1_ref), PADDED)]
-        sends[part][: keep1_ref.shape[0], :] = mm(left[0][1], right[0]) + mm(left[1][1], right[1])
-        base = part % 2 * span
-        keep_ref = keep1_ref if part < 2 else keep2_ref
-        keep_ref[:, base : base + span] = mm(left[0][0], right[0]) + mm(left[1][0], right[1])
+        keep_ref, send_ref = ((keep1_ref, send1_ref), (keep2_ref, send2_ref))[part // 2]
+        cols = slice(part % 2 * span, (part % 2 + 1) * span)
+        send_ref[:rows, cols] = mm(left[0][1], right[0]) + mm(left[1][1], right[1])
+        keep_ref[:, cols] = mm(left[0][0], right[0]) + mm(left[1][0], right[1])
+
+
+def again_kernel(
+    info_ref, qkv_ref, lse0_ref, lse1_ref, hidden0_ref, hidden1_ref, x_ref,
+    soft0_ref, soft1_ref, normed0_ref, normed1_ref, inverse0_ref, inverse1_ref, first_ref,
+):
+    scaling = HEAD_DIM ** (-0.5)
+    first_ref[...] = norm_parts(x_ref[...].astype(F32))[0]
+    for group, lse_ref, hidden_ref, soft_ref, normed_ref, inverse_ref in (
+        (0, lse0_ref, hidden0_ref, soft0_ref, normed0_ref, inverse0_ref),
+        (1, lse1_ref, hidden1_ref, soft1_ref, normed1_ref, inverse1_ref),
+    ):
+        normed_ref[...], inverse_ref[...] = norm_parts(hidden_ref[...])
+        rows, mine = PADDED[group], of_group(group)
+        low = low_lanes(rows)
+        keep_keys = key_mask(rows, LENGTHS[group])
+        for head in range(soft_ref.shape[0]):
+            lanes = slice(head // 2 * PAIR, (head // 2 + 1) * PAIR)
+            own = low if head % 2 == 0 else jnp.logical_not(low)
+            queries = qkv_ref[0, mine, lanes]
+            queries = jnp.where(own, queries, jnp.zeros_like(queries))
+            scores = mm(qkv_ref[1, mine, lanes], queries, NT) * scaling
+            soft_ref[head] = jnp.where(keep_keys, jnp.exp(scores - lse_ref[head : head + 1, :]), 0.0)
 
 
 def backward_kernel(
-    group, info_ref, gs_ref, gs2_ref, x_ref, hidden_ref, ct_ref, gain_ref, ow_ref, qkv_ref, lse_ref, w_ref,
+    group, info_ref, gs_ref, gs2_ref, first_ref, normed_ref, inverse_ref, ct_ref, gain_ref, ow_ref, qkv_ref,
+    soft_ref, w_ref,
     *refs,
 ):
     *earlier, dqkv_ref, gattn_ref, gh_ref, sums_ref, gf_ref, gmix = refs
     scaling = HEAD_DIM ** (-0.5)
-    rows, length = PADDED[group], LENGTHS[group]
+    rows = PADDED[group]
     mine = of_group(group)
     live = live_of(info_ref, group)
     sent = sent_of(group)
     grad_second = filled(gs_ref[sent, :] + gs2_ref[sent, :], rows)
-    normed, inverse = norm_parts(hidden_ref[...])
+    normed, inverse = normed_ref[...], inverse_ref[...]
     grad_hidden = ct_ref[mine, :].astype(F32) + norm_back(grad_second, normed, inverse, row(gain_ref))
     gh_ref[...] = grad_hidden
     sums_ref[0:1, :] = col_sum(grad_second * normed)
@@ -258,7 +285,6 @@
     sums_ref[2:3, :] = col_sum(gattn.astype(F32))
     gmix[...] = mm(gattn, ow_ref[...], NT).astype(BF16)
     low = low_lanes(rows)
-    keep_keys = key_mask(rows, length)
     for pair in range(qkv_ref.shape[2] // PAIR):
         lanes = slice(pair * PAIR, (pair + 1) * PAIR)
         queries, keys, values = (qkv_ref[c, mine, lanes] for c in range(3))
@@ -269,8 +295,7 @@
         for side in range(2):
             own = low if side == 0 else jnp.logical_not(low)
             head = 2 * pair + side
-            scores = mm(keys, jnp.where(own, queries, zero), NT) * scaling
-            soft = jnp.where(keep_keys, jnp.exp(scores - lse_ref[head : head + 1, :]), 0.0)
+            soft = soft_ref[head]
             grad_soft = mm(values, jnp.where(own, grads, zero), NT)
             inner = jnp.sum(grad_soft * soft, axis=0, keepdims=True)
             grad_scores = (soft * (grad_soft - inner)).astype(BF16)
@@ -286,7 +311,7 @@
         gf_ref[sent, :] = part[: SENT[group]]
     else:
         gf_ref[...] = part[: SENT[group]]
-    first_normed, _ = norm_parts(x_ref[mine, :].astype(F32))
+    first_normed = first_ref[mine, :]
     sums_ref[4:5, :] = col_sum(part * first_normed)
     sums_ref[5:6, :] = col_sum(part)
     half = qkv_ref.shape[2]
@@ -362,34 +387,22 @@
     up_ref[...] = keep_ref[:, cols:] + got_ref[:, cols:]
 
 
-def stage_small_kernel(bit, count, last, info_ref, keep_ref, small_ref, *refs):
-    pieces, outs = refs[:count], refs[count:]
-    rows, span = keep_ref.shape[0], pieces[0].shape[1]
-    if count == 2:
-        other = jnp.concatenate([pieces[0][rows : rows + 16, :], pieces[0][rows + 16 :, :]], axis=1)
-    else:
-        other = pieces[0][rows:, :]
-    small = small_ref[...] + other
-    if last:
-        out_ref, total_ref = outs
-        total_ref[...] = small
-        out_ref[...] = keep_ref[...] + pieces[0][:rows, :]
-        return
-    send_ref, rest_ref, total_ref = outs
-    total_ref[...] = small
-    mine, half, at = info_ref[4 + bit], rows // 2, 0
-    for piece in pieces:
-        cols = slice(at, at + piece.shape[1])
-        at += piece.shape[1]
-        low = keep_ref[:half, cols] + piece[:half, :]
-        high = keep_ref[half:, cols] + piece[half:rows, :]
-        send_ref[:half, cols] = jnp.where(mine == 0, high, low)
-        rest_ref[:, cols] = jnp.where(mine == 0, low, high)
-    send_ref[half:, :] = small
-
-
-def last_kernel(info_ref, keep_ref, piece_ref, out_ref):
-    out_ref[...] = keep_ref[...] + piece_ref[...]
+def stage_small_kernel(bit, info_ref, keep_ref, small_ref, piece_ref, send_ref, rest_ref, total_ref):
+    rows = keep_ref.shape[0]
+    mine, half = info_ref[4 + bit], rows // 2
+    total = small_ref[...] + piece_ref[rows:, :]
+    total_ref[...] = total
+    low = keep_ref[:half, :] + piece_ref[:half, :]
+    high = keep_ref[half:, :] + piece_ref[half:rows, :]
+    send_ref[:half, :] = jnp.where(mine == 0, high, low)
+    send_ref[half:, :] = total
+    rest_ref[...] = jnp.where(mine == 0, low, high)
+
+
+def attn_done_kernel(info_ref, keep_ref, small_ref, piece_ref, out_ref, total_ref):
+    rows = keep_ref.shape[0]
+    out_ref[...] = keep_ref[...] + piece_ref[:rows, :]
+    total_ref[...] = small_ref[...] + piece_ref[rows:, :]
 
 
 def attn_last_kernel(info_ref, done1_ref, keep2_ref, got2_ref, qkv_ref, out_ref):
@@ -410,7 +423,7 @@
 
 
 def shaped(*shape, dtype=F32):
-    return jax.ShapeDtypeStruct(shape, dtype)
+    return pltpu.HBM(shape, dtype)
 
 
 def in_vmem(value):
@@ -422,27 +435,15 @@
 
 
 class Order:
-    def __init__(self, info, always):
+    def __init__(self, info):
         self.info = info
-        self.always = always
         self.last = None
 
-    def together(self, part, *watched):
-        before = self.last
-        states = [(v, dict(vars(v))) for v in watched]
-        shapes = jax.eval_shape(part)
-        self.last = before
-        for value, state in states:
-            vars(value).update(state)
-        results = lax.cond(self.always, part, lambda: jax.tree.map(lambda v: jnp.zeros(v.shape, v.dtype), shapes))
-        self.last = jax.tree.leaves(results)[0]
-        return results
-
-    def call(self, kernel, name, outs, operands, room=3, plain=False, after=(), **kwargs):
+    def call(self, kernel, name, outs, operands, room=3, plain=False, **kwargs):
         many = isinstance(outs, (tuple, list))
         outs = tuple(outs) if many else (outs,)
         count = len(operands) + 1
-        extra = [*after] if self.last is None else [*after, self.last]
+        extra = [] if self.last is None else [self.last]
 
         def body(*refs):
             kernel(*refs[:count], *refs[count + len(extra) :])
@@ -452,9 +453,9 @@
             out_shape=outs,
             name=name,
             in_specs=[SMEM_SPEC] + [pl.BlockSpec() if plain else VMEM_SPEC] * (count - 1) + [LATER] * len(extra),
-            out_specs=(VMEM_SPEC,) * len(outs),
+            out_specs=tuple(VMEM_SPEC if o.memory_space == pltpu.VMEM else pl.BlockSpec() for o in outs),
             compiler_params=pltpu.CompilerParams(vmem_limit_bytes=room * MIB),
-            cost_estimate=pl.CostEstimate(flops=1, bytes_accessed=1, transcendentals=0),
+            cost_estimate=pl.CostEstimate(flops=COST.get(name, 1), bytes_accessed=1, transcendentals=0),
             **kwargs,
         )(self.info, *map(in_hbm if plain else in_vmem, operands), *extra)
         self.last = results[0]
@@ -481,7 +482,7 @@
         half = (self.keep.shape[0] // 2, self.keep.shape[1])
         if self.small is not None:
             send, self.keep, self.small = self.order.call(
-                functools.partial(stage_small_kernel, bit, len(self.got), False), f"{name}_{self.level}",
+                functools.partial(stage_small_kernel, bit), f"{name}_{self.level}",
                 (held(half[0] + 16, half[1]), held(*half), held(16, half[1])), [self.keep, self.small, *self.got],
             )
             self.got = [swap_bit(send, self.size, bit)]
@@ -491,9 +492,6 @@
             (held(*half), held(*half)), [self.keep, *self.got],
         )
         self.got = [swap_bit(send, self.size, bit)]
-
-    def last(self, name):
-        return self.order.call(last_kernel, name, shaped(*self.keep.shape), [self.keep, *self.got])
 
 
 def per_device(
@@ -526,8 +524,7 @@
     order = Order(
         jnp.stack(
             [side, core, small_counts[0], large_counts[0]] + [(index >> b) & 1 for b in range(bits)]
-        ).astype(jnp.int32),
-        index < dp_size,
+        ).astype(jnp.int32)
     )
 
     quarter = span // 4
@@ -558,6 +555,16 @@
         [out_weight, ow_one, ow_two, ow_got1, ow_got2],
     )
 
+    early = order.call(
+        grad_act_kernel, "grad_act",
+        tuple(
+            spec
+            for p in PADDED
+            for spec in (held(p, width, dtype=BF16), held(p, units), held(1, width))
+        ),
+        [ct_pad, down_weight], room=8,
+    )
+    gmlp, gact, downsum = (early[i::3] for i in range(3))
     mlp, gs = [None, None], []
     for group in (1, 0):
         padded = PADDED[group]
@@ -565,20 +572,20 @@
         *mlp[group], total = order.call(
             functools.partial(mlp_kernel, group, 512), "mlp_" + "ab"[group],
             (
-                held(padded, width), held(padded, width, dtype=BF16), held(padded, width, dtype=BF16),
+                held(padded, width), held(padded, width, dtype=BF16),
                 held(padded, units, dtype=BF16), held(padded, units, dtype=BF16),
-                held(1, units), held(1, width), held(tall, width),
+                held(1, units), held(tall, width),
             ),
             [
-                x_pad, ct_pad, mix[group], mix2[group], ow_all, out_bias, norm2_gain, norm2_bias,
-                up_weight, up_bias, down_weight, *gs,
+                x_pad, gact[group], mix[group], mix2[group], ow_all, out_bias, norm2_gain, norm2_bias,
+                up_weight, up_bias, *gs,
             ],
             room=16, scratch_shapes=[pltpu.VMEM((padded, 2 * span), BF16)],
         )
         gs = [total]
     gs = gs[0]
     gs2 = swap_sides(gs)
-    hidden, second, gmlp, act, gpre, upsum, downsum = zip(*mlp)
+    hidden, second, act, gpre, upsum = zip(*mlp)
 
     first_x = tuple(range(1, bits))
     first_z = (2, 1) + first_x[2:]
@@ -592,11 +599,22 @@
         )
         return Scatter(order, dp_size, bit_order, keep, send)
 
-    down_sum = weight_grads("down_weights", first_z, gmlp, act, 768)
-    up_sum = weight_grads("up_weights", first_x, second, gpre, 768)
+    down_sum = weight_grads("down_weights", first_x, gmlp, act, units // 2)
+    up_sum = weight_grads("up_weights", first_z, second, gpre, units // 2)
     down_sum.stage("down")
     up_sum.stage("up")
     mlp_part = order.call(mlp_part_kernel, "mlp_part", held(SENT_ROWS, width), [*act, down_weight], room=8)
+    mlp2 = swap_sides(mlp_part)
+
+    again = order.call(
+        again_kernel, "attn_again",
+        (
+            *(held(heads, p, p) for p in PADDED), *(held(p, width) for p in PADDED), *(held(p, 1) for p in PADDED),
+            held(ROWS, width),
+        ),
+        [qkv, *lse, *hidden, x_pad], room=8,
+    )
+    soft, normed, inverse, first_normed = again[:2], again[2:4], again[4:6], again[6]
 
     def go_back(group, *earlier):
         padded = PADDED[group]
@@ -608,16 +626,15 @@
                 held(padded, width), held(8, width), held(tall, width),
             ),
             [
-                gs, gs2, x_pad, hidden[group], ct_pad, norm2_gain, out_weight, qkv, lse[group], weights, *earlier,
+                gs, gs2, first_normed, normed[group], inverse[group], ct_pad, norm2_gain, out_weight, qkv, soft[group],
+                weights, *earlier,
             ],
             scratch_shapes=[pltpu.VMEM((padded, span), BF16)], room=16,
         )
 
+    *back1, gf = go_back(1)
     down_sum.stage("down")
     up_sum.stage("up")
-    mlp_part = order.call(relay_kernel, "mlp_relay", held(SENT_ROWS, width), [mlp_part], after=[gs2])
-    mlp2 = swap_sides(mlp_part)
-    *back1, gf = go_back(1)
     *back0, gf = go_back(0, gf)
     gf2 = swap_sides(gf)
     dqkv, gattn, gh, sums = zip(back0, back1)
@@ -625,52 +642,47 @@
     for n in range(3, bits - 1):
         down_sum.stage("down")
         up_sum.stage("up")
+    rows = width // 2
+    keep1, keep2, small, *send = order.call(
+        functools.partial(attn_weights_kernel, height, first_x), "attn_weights",
+        (
+            held(rows, 2 * span), held(rows, 2 * span), held(16, width),
+            held(rows + 16, 2 * span), held(rows, 2 * span),
+        ),
+        [first, *dqkv, *gattn, *mix, *sums, *upsum, *downsum], room=12,
+        scratch_shapes=[pltpu.VMEM((width, max(PADDED)), F32)],
+    )
+    attn1 = Scatter(order, dp_size, first_x, keep1, send[:1], small)
     half = (down_sum.keep.shape[0] // 2, 2 * units)
     both, keep_both = order.call(
         functools.partial(stage_both_kernel, first_x[-1]), "mlp_3", (held(*half), held(*half)),
         [down_sum.keep, up_sum.keep, *down_sum.got, *up_sum.got],
     )
     got_both = swap_bit(both, dp_size, first_x[-1])
-    rows = width // 2
-    keep1, keep2, small, *send = order.call(
-        functools.partial(attn_weights_kernel, height, first_x, first_z), "attn_weights",
-        (
-            held(rows, 2 * span), held(rows, 2 * span), held(16, width),
-            held(rows + 32, span), held(rows, span), held(rows, span), held(rows, span),
-        ),
-        [first, *dqkv, *gattn, *mix, *sums, *upsum, *downsum], room=12,
-        scratch_shapes=[pltpu.VMEM((width, max(PADDED)), F32)],
-    )
-    attn1 = Scatter(order, dp_size, first_x, keep1, send[:2], small)
-    attn2 = Scatter(order, dp_size, first_z, keep2, send[2:])
     attn1.stage("attn1")
+    attn2 = Scatter(order, dp_size, first_x, keep2, send[1:])
     attn2.stage("attn2")
     block_out = order.call(
         output_kernel, "block_out", shaped(*images_in.shape, dtype=BF16),
         [*hidden, mlp_part, mlp2, down_bias], room=8, scratch_shapes=[pltpu.VMEM(images_in.shape, F32)],
     )
-
-    def attn_rest():
-        for n in range(1, bits - 1):
-            attn1.stage("attn1")
-            attn2.stage("attn2")
-        done1, total = order.call(
-            functools.partial(stage_small_kernel, 0, 1, True), "attn1_end", (held(height, width), held(16, width)),
-            [attn1.keep, attn1.small, *attn1.got],
-        )
-        ends = order.call(
-            attn_last_kernel, "attn_end", (held(3, height, span), held(height, span)),
-            [done1, attn2.keep, *attn2.got],
-        )
-        return (*ends, total)
-
-    qkv_block, out_block, small = order.together(attn_rest, attn1, attn2)
-    small2 = swap_sides(small)
+    for _ in range(1, bits - 1):
+        attn1.stage("attn1")
+        attn2.stage("attn2")
     down_block, up_block = order.call(
         both_end_kernel, "mlp_end", (shaped(height, units),) * 2, [keep_both, got_both]
     )
     input_grad = order.call(
         input_kernel, "input_back", shaped(*images_in.shape), [x_pad, *gh, norm1_gain, gf, gf2], room=8
+    )
+    done1, small = order.call(
+        attn_done_kernel, "attn1_end", (held(height, width), held(16, width)),
+        [attn1.keep, attn1.small, *attn1.got],
+    )
+    small2 = swap_sides(small)
+    qkv_block, out_block = order.call(
+        attn_last_kernel, "attn_end", (shaped(3, height, span), shaped(height, span)),
+        [done1, attn2.keep, *attn2.got],
     )
     vector = shaped(width)
     small_out = order.call(

time: 191 us -> 157 us (0.82)
  waiting for transfers between devices: 86.2 us -> 62.9 us
  Pallas kernels: 64 us -> 59.1 us
  local copies, waits for them, and re-layouts: 8.54 us -> 4.62 us
    ppermute x22 -> x20, waiting for transfers between devices: 51 us -> 30.5 us  [swap_bit(): return lax.ppermute(value, 'dp', [(i, i ^ 1 << bit) for i in range(size)])]
    pallas_call x30 -> x31, Pallas kernels: 64 us -> 59.1 us  [call(): pl.pallas_call(body, out_shape=outs, name=name, in_specs=[SMEM_SPEC] + [p...]
    unnamed x50 -> x32, local copies, waits for them, and re-layouts: 8.46 us -> 4.54 us
    ppermute x7, waiting for transfers between devices: 35.1 us -> 32.4 us  [swap_sides(): return lax.ppermute(value, 'tensor', [(0, 1), (1, 0)])]
    ppermute x22 -> x20, starting transfers between devices: 20.1 us -> 17.9 us  [swap_bit(): return lax.ppermute(value, 'dp', [(i, i ^ 1 << bit) for i in range(size)])]
  transfers between devices with their start and end apart: 29 -> 27, of which waited for: 13 -> 17; matrix products, arithmetic and copies ran while one was open for 1% -> 0% of each run, Pallas kernels for 27% -> 34%
where the time goes in v4:
time: 157 us
  waiting for transfers between devices  62.9 us (40%)
  Pallas kernels  59.1 us (38%)
  starting transfers between devices  27.1 us (17%)
  local copies, waits for them, and re-layouts  4.62 us (3%)
  between operations  2.29 us (1%)
    pallas_call x31, Pallas kernels, call(): pl.pallas_call(body, out_shape=outs, name=name, in_specs=[SMEM_SPEC] + [p...  59.1 us
    ppermute x7, waiting for transfers between devices, swap_sides(): return lax.ppermute(value, 'tensor', [(0, 1), (1, 0)])  32.4 us
    ppermute x20, waiting for transfers between devices, swap_bit(): return lax.ppermute(value, 'dp', [(i, i ^ 1 << bit) for i in range(size)])  30.5 us
    ppermute x20, starting transfers between devices, swap_bit(): return lax.ppermute(value, 'dp', [(i, i ^ 1 << bit) for i in range(size)])  17.9 us
    ppermute x7, starting transfers between devices, swap_sides(): return lax.ppermute(value, 'tensor', [(0, 1), (1, 0)])  9.18 us
    unnamed x32, local copies, waits for them, and re-layouts  4.54 us
  transfers between devices with their start and end apart: 27, of which 17 were waited for; matrix products, arithmetic and copies ran while one was open for 0% of the time, Pallas kernels for 34%

profile of v4, /device:TPU:0, one launch (start us, length us, event | category | flops | bytes accessed | tf_op | source)
XLA Modules:
  0.0 156.9 jit_solution(17347616516664746369)
XLA Ops:
  1.6 3.0 %collective-permute-start = (f32[96,768]{1,0:T(8,128)S(1)}, f32[96,768]{1,0:T(8,128)S(1)}, u32[]{:S(2)}, u32[]{:S(2)}) collective-permute-start(f32[96,768]{1,0:T(8,128)S(1)} %dynamic-slice_convert_fusion), channel_id=1, source_target_pairs={{0,1},{1,0},{2,3},{3,2},{4,5},{5,4},{6,7},{7,6},{8,9},{9,8},{10,11... | collective-permute-start | bytes 884744 | tf_op jit(solution)/shard_map/ppermute | solution.py:466
  6.0 7.9 %attn_forward.1 = (bf16[544,768]{1,0:T(8,128)(2,1)S(1)}, bf16[3,544,384]{2,1,0:T(8,128)(2,1)S(1)}, bf16[544,768]{1,0:T(8,128)(2,1)S(1)}, bf16[544,768]{1,0:T(8,1...) custom-call(s32[8]{0:T(128)S(1)} %stack.27.refs_0_, ...), custom_call_target="tpu_custom_call" | custom-call | flops 1 | bytes 1 | tf_op jit(solution)/shard_map/attn_forward/pallas_call | solution.py:451
  18.1 4.9 %collective-permute-done.1.refs_1_ = f32[96,768]{1,0:T(8,128)S(1)} collective-permute-done((f32[96,768]{1,0:T(8,128)S(1)}, f32[96,768]{1,0:T(8,128)S(1)}, u32[]{:S(2)}, u32[]{:S(2)}) %collective-permute-start.1) | collective-permute-done | bytes 294944 | tf_op jit(solution)/shard_map/ppermute | solution.py:470
  26.0 2.3 %grad_act.1 = (bf16[208,768]{1,0:T(8,128)(2,1)S(1)}, f32[208,1536]{1,0:T(8,128)S(1)}, f32[1,768]{1,0:T(1,128)S(1)}, bf16[336,768]{1,0:T(8,128)(2,1)S(1)}, f32[336,1536]{1,0:T(8,128)S(1)}, /*index=5*/f32[1,768]{1,0:T(1,128)S(1)}) custom-call(s32[8]{0:T(128)S(1)} %stack.27.refs_0_, bf16[544,768]{1,0:T(8,128)(2,1)S(1)} %get-tuple-element.108.refs_1_.refs_6_, ...), custom_call_target="tpu_custom_call" | custom-call | flops 1 | bytes 1 | tf_op jit(solution)/shard_map/grad_act/pallas_call | solution.py:451
  28.3 2.2 %collective-permute-done.5.refs_4_ = f32[328,384]{1,0:T(8,128)S(1)} collective-permute-done((f32[328,384]{1,0:T(8,128)S(1)}, f32[328,384]{1,0:T(8,128)S(1)}, u32[]{:S(2)}, u32[]{:S(2)}) %collective-permute-start.5) | collective-permute-done | bytes 503840 | tf_op jit(solution)/shard_map/ppermute | solution.py:466
  30.5 4.2 %mlp_b.1 = (f32[336,768]{1,0:T(8,128)S(1)}, bf16[336,768]{1,0:T(8,128)(2,1)S(1)}, bf16[336,1536]{1,0:T(8,128)(2,1)S(1)}, bf16[336,1536]{1,0:T(8,128)(2,1)S(1)}, ...) custom-call(s32[8]{0:T(128)S(1)} %stack.27.refs_0_, bf16[544,768]{1,0:T(8,128)(2,1)S(1)} %get-tuple-element.107.refs_1_.refs_6_, ...), custom_call_target="tpu_custom_call" | custom-call | flops 1 | bytes 1 | tf_op jit(solution)/shard_map/mlp_b/pallas_call | solution.py:451
  35.3 3.3 %mlp_a.1 = (f32[208,768]{1,0:T(8,128)S(1)}, bf16[208,768]{1,0:T(8,128)(2,1)S(1)}, bf16[208,1536]{1,0:T(8,128)(2,1)S(1)}, bf16[208,1536]{1,0:T(8,128)(2,1)S(1)}, ...) custom-call(s32[8]{0:T(128)S(1)} %stack.27.refs_0_, bf16[544,768]{1,0:T(8,128)(2,1)S(1)} %get-tuple-element.107.refs_1_.refs_6_, ...), custom_call_target="tpu_custom_call" | custom-call | flops 1 | bytes 1 | tf_op jit(solution)/shard_map/mlp_a/pallas_call | solution.py:451
  39.1 3.0 %down_weights.1 = (f32[384,1536]{1,0:T(8,128)S(1)}, f32[384,768]{1,0:T(8,128)S(1)}, f32[384,768]{1,0:T(8,128)S(1)}) custom-call(s32[8]{0:T(128)S(1)} %stack.27.refs_0_, bf16[208,768]{1,0:T(8,128)(2,1)S(1)} %get-tuple-element.114.refs_11_.refs_1_, bf16[336,768]{1,0:T(8,128)(2,1)S(1)} %get-tuple-element.124.refs_2_, ...), custom_call_target="tpu_custom_call" | custom-call | flops 1 | bytes 1 | tf_op jit(solution)/shard_map/down_weights/pallas_call | solution.py:451
  42.7 2.8 %up_weights.1 = (f32[384,1536]{1,0:T(8,128)S(1)}, f32[384,768]{1,0:T(8,128)S(1)}, f32[384,768]{1,0:T(8,128)S(1)}) custom-call(s32[8]{0:T(128)S(1)} %stack.27.refs_0_, bf16[208,768]{1,0:T(8,128)(2,1)S(1)} %get-tuple-element.120.refs_1_, bf16[336,768]{1,0:T(8,128)(2,1)S(1)} %get-tuple-element.121.refs_2_, bf16[208,1536]{1,0:T(8,128)(2,1)S(1)} %get-tuple-element.122.refs_3_, ...), custom_call_target="tpu_custom_call" | custom-call | flops 1 | bytes 1 | tf_op jit(solution)/shard_map/up_weights/pallas_call | solution.py:451
  56.2 2.3 %attn_again.1 = (f32[6,208,208]{2,1,0:T(8,128)S(1)}, f32[6,336,336]{2,1,0:T(8,128)S(1)}, f32[208,768]{1,0:T(8,128)S(1)}, f32[336,768]{1,0:T(8,128)S(1)}, f32[208...) custom-call(s32[8]{0:T(128)S(1)} %stack.27.refs_0_, ...), custom_call_target="tpu_custom_call" | custom-call | flops 1 | bytes 1 | tf_op jit(solution)/shard_map/attn_again/pallas_call | solution.py:451
  58.5 18.5 %collective-permute-done.11.refs_2_ = f32[528,768]{1,0:T(8,128)S(1)} collective-permute-done((f32[528,768]{1,0:T(8,128)S(1)}, f32[528,768]{1,0:T(8,128)S(1)}, u32[]{:S(2)}, u32[]{:S(2)}) %collective-permute-start.11) | collective-permute-done | bytes 1622048 | tf_op jit(solution)/shard_map/ppermute | solution.py:466
  77.0 5.3 %attn_backward_b.1 = (bf16[3,336,384]{2,1,0:T(8,128)(2,1)S(1)}, bf16[336,768]{1,0:T(8,128)(2,1)S(1)}, f32[336,768]{1,0:T(8,128)S(1)}, f32[8,768]{1,0:T(8,128)S(1)}, f32[328,768]{1,0:T(8,128)S(1)}) custom-call(s32[8]{0:T(128)S(1)} %stack.27.refs_0_, f32[528,768]{1,0:T(8,128)S(1)} %get-tuple-element.133.refs_1_, ...), custom_call_target="tpu_custom_call" | custom-call | flops 99999997952 | bytes 1 | tf_op jit(solution)/shard_map/attn_backward_b/pallas_call | solution.py:451
  85.9 3.8 %attn_backward_a.1 = (bf16[3,208,384]{2,1,0:T(8,128)(2,1)S(1)}, bf16[208,768]{1,0:T(8,128)(2,1)S(1)}, f32[208,768]{1,0:T(8,128)S(1)}, f32[8,768]{1,0:T(8,128)S(1)}, f32[528,768]{1,0:T(8,128)S(1)}) custom-call(s32[8]{0:T(128)S(1)} %stack.27.refs_0_, f32[528,768]{1,0:T(8,128)S(1)} %get-tuple-element.133.refs_1_, ...), custom_call_target="tpu_custom_call" | custom-call | flops 1 | bytes 1 | tf_op jit(solution)/shard_map/attn_backward_a/pallas_call | solution.py:451
  89.8 3.3 %attn_weights.1 = (f32[384,768]{1,0:T(8,128)S(1)}, f32[384,768]{1,0:T(8,128)S(1)}, f32[16,768]{1,0:T(8,128)S(1)}, f32[400,768]{1,0:T(8,128)S(1)}, f32[384,768]{1,0:T(8,128)S(1)}) custom-call(s32[8]{0:T(128)S(1)} %stack.27.refs_0_, bf16[544,768]{1,0:T(8,128)(2,1)S(1)} %get-tuple-element.109.refs_2_.refs_1_, ...), custom_call_target="tpu_custom_call" | custom-call | flops 1 | bytes 1 | tf_op jit(solution)/shard_map/attn_weights/pallas_call | solution.py:451
  93.7 2.7 %collective-permute-done.17.refs_4_ = f32[96,1536]{1,0:T(8,128)S(1)} collective-permute-done((f32[96,1536]{1,0:T(8,128)S(1)}, f32[96,1536]{1,0:T(8,128)S(1)}, u32[]{:S(2)}, u32[]{:S(2)}) %collective-permute-start.17) | collective-permute-done | bytes 589856 | tf_op jit(solution)/shard_map/ppermute | solution.py:470
  98.6 2.7 %collective-permute-start.19 = (f32[48,3072]{1,0:T(8,128)S(1)}, f32[48,3072]{1,0:T(8,128)S(1)}, u32[]{:S(2)}, u32[]{:S(2)}) collective-permute-start(f32[48,3072]{1,0:T(8,128)S(1)} %get-tuple-element.166.refs_4_), channel_id=1, source_target_pairs={{0,16},{2,18},{4,20},{6,22},{8,24},{10,26},{12,28},{14,30},{16,0},... | collective-permute-start | bytes 1769480 | tf_op jit(solution)/shard_map/ppermute | solution.py:470
  104.8 6.9 %collective-permute-done.10.refs_4_ = f32[528,768]{1,0:T(8,128)S(1)} collective-permute-done((f32[528,768]{1,0:T(8,128)S(1)}, f32[528,768]{1,0:T(8,128)S(1)}, u32[]{:S(2)}, u32[]{:S(2)}) %collective-permute-start.10) | collective-permute-done | bytes 1622048 | tf_op jit(solution)/shard_map/ppermute | solution.py:466
  111.8 2.1 %block_out.1.refs_4_ = bf16[522,768]{1,0:T(8,128)(2,1)} custom-call(s32[8]{0:T(128)S(1)} %stack.27.refs_0_, f32[208,768]{1,0:T(8,128)S(1)} %get-tuple-element.117.refs_5_.refs_4_.refs_1_, f32[336,768]{1,0:T(8,128)S(1)} %get-tuple-element.116.refs_12_.refs_5_.refs_2_, f32[528,768]{1,0:T(8,128)S(1)} %mlp_part.1.refs_7_.refs_3_, ...), custom_call_target="tpu_custom_call" | custom-call | flops 99999997952 | bytes 1 | tf_op jit(solution)/shard_map/block_out/pallas_call | solution.py:451
  113.9 5.5 %collective-permute-done.21.refs_3_ = f32[208,768]{1,0:T(8,128)S(1)} collective-permute-done((f32[208,768]{1,0:T(8,128)S(1)}, f32[208,768]{1,0:T(8,128)S(1)}, u32[]{:S(2)}, u32[]{:S(2)}) %collective-permute-start.21) | collective-permute-done | bytes 639008 | tf_op jit(solution)/shard_map/ppermute | solution.py:470
  122.8 5.0 %collective-permute-done.20.refs_2_ = f32[192,768]{1,0:T(8,128)S(1)} collective-permute-done((f32[192,768]{1,0:T(8,128)S(1)}, f32[192,768]{1,0:T(8,128)S(1)}, u32[]{:S(2)}, u32[]{:S(2)}) %collective-permute-start.20) | collective-permute-done | bytes 589856 | tf_op jit(solution)/shard_map/ppermute | solution.py:470
  130.1 2.1 %collective-permute-done.23.refs_3_ = f32[112,768]{1,0:T(8,128)S(1)} collective-permute-done((f32[112,768]{1,0:T(8,128)S(1)}, f32[112,768]{1,0:T(8,128)S(1)}, u32[]{:S(2)}, u32[]{:S(2)}) %collective-permute-start.23) | collective-permute-done | bytes 344096 | tf_op jit(solution)/shard_map/ppermute | solution.py:470
  134.3 5.0 %collective-permute-done.22.refs_2_ = f32[96,768]{1,0:T(8,128)S(1)} collective-permute-done((f32[96,768]{1,0:T(8,128)S(1)}, f32[96,768]{1,0:T(8,128)S(1)}, u32[]{:S(2)}, u32[]{:S(2)}) %collective-permute-start.22) | collective-permute-done | bytes 294944 | tf_op jit(solution)/shard_map/ppermute | solution.py:470
  144.8 3.0 %input_back.1.refs_4_ = f32[522,768]{1,0:T(8,128)} custom-call(s32[8]{0:T(128)S(1)} %stack.27.refs_0_, bf16[544,768]{1,0:T(8,128)(2,1)S(1)} %copy-done.1, f32[208,768]{1,0:T(8,128)S(1)} %get-tuple-element.169.refs_2_, f32[336,768]{1,0:T(8,128)S(1)} %get-tuple-element.170.refs_3_, f32[768]{0:T(1024)S(1)} %copy-done.14, ...), custom_call_target="tpu_custom_call" | custom-call | flops 1 | bytes 1 | tf_op jit(solution)/shard_map/input_back/pallas_call | solution.py:451
  152.4 2.4 %collective-permute-done.25.refs_2_ = f32[16,768]{1,0:T(8,128)S(1)} collective-permute-done((f32[16,768]{1,0:T(8,128)S(1)}, f32[16,768]{1,0:T(8,128)S(1)}, u32[]{:S(2)}, u32[]{:S(2)}) %collective-permute-start.25) | collective-permute-done | bytes 49184 | tf_op jit(solution)/shard_map/ppermute | solution.py:466
  (95 shorter events, 50.3 us)
Async XLA Ops:
  1.6 12.3 %collective-permute-start = (f32[96,768]{1,0:T(8,128)S(1)}, f32[96,768]{1,0:T(8,128)S(1)}, u32[]{:S(2)}, u32[]{:S(2)}) collective-permute-start(f32[96,768]{1,0:T(8,128)S(1)} %dynamic-slice_convert_fusion), channel_id=1, source_target_pairs={{0,1},{1,0},{2,3},{3,2},{4,5},{5,4},{6,7},{7,6},{8,9},{9,8},{10,11... | collective-permute-start | bytes 884744 | tf_op jit(solution)/shard_map/ppermute | solution.py:466
  14.5 8.5 %collective-permute-start.1 = (f32[96,768]{1,0:T(8,128)S(1)}, f32[96,768]{1,0:T(8,128)S(1)}, u32[]{:S(2)}, u32[]{:S(2)}) collective-permute-start(f32[96,768]{1,0:T(8,128)S(1)} %out_weight_relay.1.refs_2_), channel_id=1, source_target_pairs={{0,4},{2,6},{4,0},{6,2},{8,12},{10,14},{12,8},{14,10},{16,20},{18,... | collective-permute-start | bytes 884744 | tf_op jit(solution)/shard_map/ppermute | solution.py:470
  16.0 14.4 %collective-permute-start.5 = (f32[328,384]{1,0:T(8,128)S(1)}, f32[328,384]{1,0:T(8,128)S(1)}, u32[]{:S(2)}, u32[]{:S(2)}) collective-permute-start(f32[328,384]{1,0:T(8,128)S(1)} %get-tuple-element.113.refs_3_.refs_7_), channel_id=1, source_target_pairs={{0,1},{1,0},{2,3},{3,2},{4,5},{5,4},{6,7},{7,6},{8,9},{9,8},{10,11... | collective-permute-start | bytes 1511432 | tf_op jit(solution)/shard_map/ppermute | solution.py:466
  16.5 18.7 %collective-permute-start.4 = (f32[200,384]{1,0:T(8,128)S(1)}, f32[200,384]{1,0:T(8,128)S(1)}, u32[]{:S(2)}, u32[]{:S(2)}) collective-permute-start(f32[200,384]{1,0:T(8,128)S(1)} %get-tuple-element.111.refs_3_.refs_6_), channel_id=1, source_target_pairs={{0,1},{1,0},{2,3},{3,2},{4,5},{5,4},{6,7},{7,6},{8,9},{9,8},{10,11... | collective-permute-start | bytes 921608 | tf_op jit(solution)/shard_map/ppermute | solution.py:466
  18.1 5.6 %collective-permute-start.2 = (f32[96,768]{1,0:T(8,128)S(1)}, f32[96,768]{1,0:T(8,128)S(1)}, u32[]{:S(2)}, u32[]{:S(2)}) collective-permute-start(f32[96,768]{1,0:T(8,128)S(1)} %out_weight_relay.1.refs_2_), channel_id=1, source_target_pairs={{0,2},{2,0},{4,6},{6,4},{8,10},{10,8},{12,14},{14,12},{16,18},{18,... | collective-permute-start | bytes 884744 | tf_op jit(solution)/shard_map/ppermute | solution.py:470
  38.5 38.5 %collective-permute-start.11 = (f32[528,768]{1,0:T(8,128)S(1)}, f32[528,768]{1,0:T(8,128)S(1)}, u32[]{:S(2)}, u32[]{:S(2)}) collective-permute-start(f32[528,768]{1,0:T(8,128)S(1)} %get-tuple-element.133.refs_1_), channel_id=1, source_target_pairs={{0,1},{1,0},{2,3},{3,2},{4,5},{5,4},{6,7},{7,6},{8,9},{9,8},{10,11... | collective-permute-start | bytes 4866056 | tf_op jit(solution)/shard_map/ppermute | solution.py:466
  42.2 4.5 %collective-permute-start.9 = (f32[384,768]{1,0:T(8,128)S(1)}, f32[384,768]{1,0:T(8,128)S(1)}, u32[]{:S(2)}, u32[]{:S(2)}) collective-permute-start(f32[384,768]{1,0:T(8,128)S(1)} %get-tuple-element.130), channel_id=1, source_target_pairs={{0,2},{2,0},{4,6},{6,4},{8,10},{10,8},{12,14},{14,12},{16,18},{18,... | collective-permute-start | bytes 3538952 | tf_op jit(solution)/shard_map/ppermute | solution.py:470
  45.7 4.5 %collective-permute-start.7 = (f32[384,768]{1,0:T(8,128)S(1)}, f32[384,768]{1,0:T(8,128)S(1)}, u32[]{:S(2)}, u32[]{:S(2)}) collective-permute-start(f32[384,768]{1,0:T(8,128)S(1)} %get-tuple-element.128), channel_id=1, source_target_pairs={{0,2},{2,0},{4,6},{6,4},{8,10},{10,8},{12,14},{14,12},{16,18},{18,... | collective-permute-start | bytes 3538952 | tf_op jit(solution)/shard_map/ppermute | solution.py:470
  47.6 34.8 %collective-permute-start.13 = (f32[192,1536]{1,0:T(8,128)S(1)}, f32[192,1536]{1,0:T(8,128)S(1)}, u32[]{:S(2)}, u32[]{:S(2)}) collective-permute-start(f32[192,1536]{1,0:T(8,128)S(1)} %get-tuple-element.131.refs_4_), channel_id=1, source_target_pairs={{0,4},{2,6},{4,0},{6,2},{8,12},{10,14},{12,8},{14,10},{16,20},{18,... | collective-permute-start | bytes 3538952 | tf_op jit(solution)/shard_map/ppermute | solution.py:470
  53.0 30.1 %collective-permute-start.12 = (f32[192,1536]{1,0:T(8,128)S(1)}, f32[192,1536]{1,0:T(8,128)S(1)}, u32[]{:S(2)}, u32[]{:S(2)}) collective-permute-start(f32[192,1536]{1,0:T(8,128)S(1)} %get-tuple-element.132.refs_4_), channel_id=1, source_target_pairs={{0,8},{2,10},{4,12},{6,14},{8,0},{10,2},{12,4},{14,6},{16,24},{18,... | collective-permute-start | bytes 3538952 | tf_op jit(solution)/shard_map/ppermute | solution.py:470
  54.7 57.1 %collective-permute-start.10 = (f32[528,768]{1,0:T(8,128)S(1)}, f32[528,768]{1,0:T(8,128)S(1)}, u32[]{:S(2)}, u32[]{:S(2)}) collective-permute-start(f32[528,768]{1,0:T(8,128)S(1)} %mlp_part.1.refs_7_.refs_3_), channel_id=1, source_target_pairs={{0,1},{1,0},{2,3},{3,2},{4,5},{5,4},{6,7},{7,6},{8,9},{9,8},{10,11... | collective-permute-start | bytes 4866056 | tf_op jit(solution)/shard_map/ppermute | solution.py:466
  83.8 12.6 %collective-permute-start.17 = (f32[96,1536]{1,0:T(8,128)S(1)}, f32[96,1536]{1,0:T(8,128)S(1)}, u32[]{:S(2)}, u32[]{:S(2)}) collective-permute-start(f32[96,1536]{1,0:T(8,128)S(1)} %get-tuple-element.149.refs_13_), channel_id=1, source_target_pairs={{0,4},{2,6},{4,0},{6,2},{8,12},{10,14},{12,8},{14,10},{16,20},{18,... | collective-permute-start | bytes 1769480 | tf_op jit(solution)/shard_map/ppermute | solution.py:470
  84.4 13.5 %collective-permute-start.16 = (f32[96,1536]{1,0:T(8,128)S(1)}, f32[96,1536]{1,0:T(8,128)S(1)}, u32[]{:S(2)}, u32[]{:S(2)}) collective-permute-start(f32[96,1536]{1,0:T(8,128)S(1)} %get-tuple-element.148.refs_3_), channel_id=1, source_target_pairs={{0,8},{2,10},{4,12},{6,14},{8,0},{10,2},{12,4},{14,6},{16,24},{18,... | collective-permute-start | bytes 1769480 | tf_op jit(solution)/shard_map/ppermute | solution.py:470
  93.1 8.2 %collective-permute-start.15 = (f32[400,768]{1,0:T(8,128)S(1)}, f32[400,768]{1,0:T(8,128)S(1)}, u32[]{:S(2)}, u32[]{:S(2)}) collective-permute-start(f32[400,768]{1,0:T(8,128)S(1)} %get-tuple-element.163), channel_id=1, source_target_pairs={{0,2},{2,0},{4,6},{6,4},{8,10},{10,8},{12,14},{14,12},{16,18},{18,... | collective-permute-start | bytes 3686408 | tf_op jit(solution)/shard_map/ppermute | solution.py:470
  93.2 9.4 %collective-permute-start.14 = (f32[384,768]{1,0:T(8,128)S(1)}, f32[384,768]{1,0:T(8,128)S(1)}, u32[]{:S(2)}, u32[]{:S(2)}) collective-permute-start(f32[384,768]{1,0:T(8,128)S(1)} %get-tuple-element.160), channel_id=1, source_target_pairs={{0,2},{2,0},{4,6},{6,4},{8,10},{10,8},{12,14},{14,12},{16,18},{18,... | collective-permute-start | bytes 3538952 | tf_op jit(solution)/shard_map/ppermute | solution.py:470
  96.4 47.5 %collective-permute-start.18 = (f32[528,768]{1,0:T(8,128)S(1)}, f32[528,768]{1,0:T(8,128)S(1)}, u32[]{:S(2)}, u32[]{:S(2)}) collective-permute-start(f32[528,768]{1,0:T(8,128)S(1)} %get-tuple-element.171.refs_5_), channel_id=1, source_target_pairs={{0,1},{1,0},{2,3},{3,2},{4,5},{5,4},{6,7},{7,6},{8,9},{9,8},{10,11... | collective-permute-start | bytes 4866056 | tf_op jit(solution)/shard_map/ppermute | solution.py:466
  98.6 42.0 %collective-permute-start.19 = (f32[48,3072]{1,0:T(8,128)S(1)}, f32[48,3072]{1,0:T(8,128)S(1)}, u32[]{:S(2)}, u32[]{:S(2)}) collective-permute-start(f32[48,3072]{1,0:T(8,128)S(1)} %get-tuple-element.166.refs_4_), channel_id=1, source_target_pairs={{0,16},{2,18},{4,20},{6,22},{8,24},{10,26},{12,28},{14,30},{16,0},... | collective-permute-start | bytes 1769480 | tf_op jit(solution)/shard_map/ppermute | solution.py:470
  102.0 17.4 %collective-permute-start.21 = (f32[208,768]{1,0:T(8,128)S(1)}, f32[208,768]{1,0:T(8,128)S(1)}, u32[]{:S(2)}, u32[]{:S(2)}) collective-permute-start(f32[208,768]{1,0:T(8,128)S(1)} %get-tuple-element.167.refs_3_), channel_id=1, source_target_pairs={{0,4},{2,6},{4,0},{6,2},{8,12},{10,14},{12,8},{14,10},{16,20},{18,... | collective-permute-start | bytes 1916936 | tf_op jit(solution)/shard_map/ppermute | solution.py:470
  103.3 24.5 %collective-permute-start.20 = (f32[192,768]{1,0:T(8,128)S(1)}, f32[192,768]{1,0:T(8,128)S(1)}, u32[]{:S(2)}, u32[]{:S(2)}) collective-permute-start(f32[192,768]{1,0:T(8,128)S(1)} %get-tuple-element.168.refs_6_), channel_id=1, source_target_pairs={{0,4},{2,6},{4,0},{6,2},{8,12},{10,14},{12,8},{14,10},{16,20},{18,... | collective-permute-start | bytes 1769480 | tf_op jit(solution)/shard_map/ppermute | solution.py:470
  121.1 11.0 %collective-permute-start.23 = (f32[112,768]{1,0:T(8,128)S(1)}, f32[112,768]{1,0:T(8,128)S(1)}, u32[]{:S(2)}, u32[]{:S(2)}) collective-permute-start(f32[112,768]{1,0:T(8,128)S(1)} %get-tuple-element.176.refs_3_), channel_id=1, source_target_pairs={{0,8},{2,10},{4,12},{6,14},{8,0},{10,2},{12,4},{14,6},{16,24},{18,... | collective-permute-start | bytes 1032200 | tf_op jit(solution)/shard_map/ppermute | solution.py:470
  128.4 10.9 %collective-permute-start.22 = (f32[96,768]{1,0:T(8,128)S(1)}, f32[96,768]{1,0:T(8,128)S(1)}, u32[]{:S(2)}, u32[]{:S(2)}) collective-permute-start(f32[96,768]{1,0:T(8,128)S(1)} %get-tuple-element.178.refs_4_), channel_id=1, source_target_pairs={{0,8},{2,10},{4,12},{6,14},{8,0},{10,2},{12,4},{14,6},{16,24},{18,... | collective-permute-start | bytes 884744 | tf_op jit(solution)/shard_map/ppermute | solution.py:470
  132.7 15.9 %collective-permute-start.24 = (f32[64,768]{1,0:T(8,128)S(1)}, f32[64,768]{1,0:T(8,128)S(1)}, u32[]{:S(2)}, u32[]{:S(2)}) collective-permute-start(f32[64,768]{1,0:T(8,128)S(1)} %get-tuple-element.181.refs_3_), channel_id=1, source_target_pairs={{0,16},{2,18},{4,20},{6,22},{8,24},{10,26},{12,28},{14,30},{16,0},... | collective-permute-start | bytes 589832 | tf_op jit(solution)/shard_map/ppermute | solution.py:470
  139.9 11.3 %collective-permute-start.26 = (f32[48,768]{1,0:T(8,128)S(1)}, f32[48,768]{1,0:T(8,128)S(1)}, u32[]{:S(2)}, u32[]{:S(2)}) collective-permute-start(f32[48,768]{1,0:T(8,128)S(1)} %get-tuple-element.182.refs_3_), channel_id=1, source_target_pairs={{0,16},{2,18},{4,20},{6,22},{8,24},{10,26},{12,28},{14,30},{16,0},... | collective-permute-start | bytes 442376 | tf_op jit(solution)/shard_map/ppermute | solution.py:470
  150.6 4.2 %collective-permute-start.25 = (f32[16,768]{1,0:T(8,128)S(1)}, f32[16,768]{1,0:T(8,128)S(1)}, u32[]{:S(2)}, u32[]{:S(2)}) collective-permute-start(f32[16,768]{1,0:T(8,128)S(1)} %get-tuple-element.186.refs_1_), channel_id=1, source_target_pairs={{0,1},{1,0},{2,3},{3,2},{4,5},{5,4},{6,7},{7,6},{8,9},{9,8},{10,11... | collective-permute-start | bytes 147464 | tf_op jit(solution)/shard_map/ppermute | solution.py:466
  (19 other events, 143.9 us)

commit v5 on v4

--- a/solution.py
+++ b/solution.py
@@ -20,7 +20,7 @@
 F32 = jnp.float32
 BF16 = jnp.bfloat16
 MIB = 1024 * 1024
-COST = {"attn_backward_b": 10**11, "block_out": 10**11, "mlp_3": 7 * 10**9}
+COST = {"attn_backward_b": 9 * 10**9, "block_out": 10**11, "mlp_3": 7 * 10**9}
 NT = ((1,), (1,))
 TN = ((0,), (0,))
 
@@ -120,21 +120,31 @@
             mix_ref[:, lanes] = mixed[: SENT[group]]
 
 
-def relay_kernel(info_ref, in_ref, out_ref):
+def relay_kernel(info_ref, in_ref, out_ref, *halves):
     out_ref[...] = in_ref[...]
-
-
-def join_kernel(info_ref, ow_ref, one_ref, two_ref, got1_ref, got2_ref, ow_all):
+    for n, ref in enumerate(halves):
+        ref[...] = in_ref[:, n * ref.shape[1] : (n + 1) * ref.shape[1]]
+
+
+def next_kernel(info_ref, in1_ref, in2_ref, out1_ref, out2_ref):
+    out1_ref[...] = in1_ref[...]
+    out2_ref[...] = in2_ref[...]
+
+
+def join_kernel(info_ref, ow_ref, one_ref, two1_ref, two2_ref, got_ref, got1_ref, got2_ref, ow_all):
     side, core, near = info_ref[0], info_ref[1], info_ref[5]
-    span = ow_ref.shape[0]
+    span, width = ow_ref.shape
     quarter = span // 4
     mine, other = side * span, (1 - side) * span
     ow_all[pl.ds(pl.multiple_of(mine, span), span), :] = ow_ref[...]
-    for ref, where, x in (
-        (one_ref, core, near), (two_ref, core, 1 - near), (got1_ref, 1 - core, near), (got2_ref, 1 - core, 1 - near),
+    for refs, where, x in (
+        ((one_ref,), core, near), ((two1_ref, two2_ref), core, 1 - near),
+        ((got_ref,), 1 - core, near), ((got1_ref, got2_ref), 1 - core, 1 - near),
     ):
         at = pl.multiple_of(other + (2 * where + x) * quarter, quarter)
-        ow_all[pl.ds(at, quarter), :] = ref[...].astype(BF16)
+        for n, ref in enumerate(refs):
+            cols = ref.shape[1]
+            ow_all[pl.ds(at, quarter), n * cols : (n + 1) * cols] = ref[...].astype(BF16)
 
 
 def grad_act_kernel(info_ref, ct_ref, down_ref, *refs):
@@ -243,9 +253,10 @@
 def again_kernel(
     info_ref, qkv_ref, lse0_ref, lse1_ref, hidden0_ref, hidden1_ref, x_ref,
     soft0_ref, soft1_ref, normed0_ref, normed1_ref, inverse0_ref, inverse1_ref, first_ref,
+    first_inverse_ref,
 ):
     scaling = HEAD_DIM ** (-0.5)
-    first_ref[...] = norm_parts(x_ref[...].astype(F32))[0]
+    first_ref[...], first_inverse_ref[...] = norm_parts(x_ref[...].astype(F32))
     for group, lse_ref, hidden_ref, soft_ref, normed_ref, inverse_ref in (
         (0, lse0_ref, hidden0_ref, soft0_ref, normed0_ref, inverse0_ref),
         (1, lse1_ref, hidden1_ref, soft1_ref, normed1_ref, inverse1_ref),
@@ -324,12 +335,11 @@
         out_ref[sent_of(group), :] = mm(act_ref[...], down_ref[...])[: SENT[group]]
 
 
-def small_end_kernel(info_ref, small_ref, other_ref, gain1, bias1, gain2, bias2, outb, qvb, upb, downb):
+def small_end_kernel(info_ref, small_ref, gain2, bias2, outb, qvb, upb, downb):
     total = small_ref[...]
     width = total.shape[1]
-    total = jnp.concatenate([total[0:2] + other_ref[0:2, :], total[2:]], axis=0)
-    for n, ref in enumerate((gain1, bias1, gain2, bias2, outb)):
-        ref[...] = total[n].reshape(width)
+    for n, ref in enumerate((gain2, bias2, outb)):
+        ref[...] = total[2 + n].reshape(width)
     qvb[0:1, :] = total[5:6, : width // 2]
     qvb[1:2, :] = total[5:6, width // 2 :]
     upb[:width] = total[6].reshape(width)
@@ -337,12 +347,18 @@
     downb[...] = total[8].reshape(width)
 
 
-def input_kernel(info_ref, x_ref, gh0_ref, gh1_ref, gain_ref, gf_ref, gf2_ref, grad_ref):
+def norm1_end_kernel(info_ref, small_ref, other_ref, gain1, bias1):
+    for n, ref in enumerate((gain1, bias1)):
+        ref[...] = (small_ref[n] + other_ref[n]).reshape(small_ref.shape[1])
+
+
+def input_kernel(info_ref, first_ref, inverse_ref, gh0_ref, gh1_ref, gain_ref, gf_ref, gf2_ref, grad_ref):
     start = 0
     for group, gh_ref in enumerate((gh0_ref, gh1_ref)):
         length, sent = LENGTHS[group], sent_of(group)
         grad_first = gf_ref[sent, :] + gf2_ref[sent, :]
-        normed, inverse = norm_parts(x_ref[of_group(group), :].astype(F32)[: SENT[group]])
+        mine = slice(STARTS[group], STARTS[group] + SENT[group])
+        normed, inverse = first_ref[mine, :], inverse_ref[mine, :]
         value = gh_ref[: SENT[group], :] + norm_back(grad_first, normed, inverse, row(gain_ref))
         grad_ref[start : start + length, :] = value[:length]
         start += length
@@ -545,16 +561,12 @@
     )
     lse, mix = rest[:2], rest[2:]
     mix2 = [swap_sides(m) for m in mix]
-    ow_one = order.call(relay_kernel, "out_weight_relay", held(quarter, width), [ow_one])
-    ow_two = swap_bit(ow_one, dp_size, 1)
+    ow_one, *halves = order.call(
+        relay_kernel, "out_weight_relay",
+        (held(quarter, width), held(quarter, width // 2), held(quarter, width // 2)), [ow_one],
+    )
+    ow_two = [swap_bit(v, dp_size, 1) for v in halves]
     ow_got1 = swap_bit(ow_one, dp_size, 0)
-    ow_two = order.call(relay_kernel, "out_weight_next", held(quarter, width), [ow_two])
-    ow_got2 = swap_bit(ow_two, dp_size, 0)
-    ow_all = order.call(
-        join_kernel, "out_weight_join", held(2 * span, width, dtype=BF16),
-        [out_weight, ow_one, ow_two, ow_got1, ow_got2],
-    )
-
     early = order.call(
         grad_act_kernel, "grad_act",
         tuple(
@@ -565,6 +577,13 @@
         [ct_pad, down_weight], room=8,
     )
     gmlp, gact, downsum = (early[i::3] for i in range(3))
+    ow_two = order.call(next_kernel, "out_weight_next", (held(quarter, width // 2),) * 2, ow_two)
+    ow_got2 = [swap_bit(v, dp_size, 0) for v in ow_two]
+    ow_all = order.call(
+        join_kernel, "out_weight_join", held(2 * span, width, dtype=BF16),
+        [out_weight, ow_one, *ow_two, ow_got1, *ow_got2],
+    )
+
     mlp, gs = [None, None], []
     for group in (1, 0):
         padded = PADDED[group]
@@ -610,11 +629,12 @@
         again_kernel, "attn_again",
         (
             *(held(heads, p, p) for p in PADDED), *(held(p, width) for p in PADDED), *(held(p, 1) for p in PADDED),
-            held(ROWS, width),
+            held(ROWS, width), held(ROWS, 1),
         ),
         [qkv, *lse, *hidden, x_pad], room=8,
     )
     soft, normed, inverse, first_normed = again[:2], again[2:4], again[4:6], again[6]
+    first_inverse = again[7]
 
     def go_back(group, *earlier):
         padded = PADDED[group]
@@ -673,7 +693,7 @@
         both_end_kernel, "mlp_end", (shaped(height, units),) * 2, [keep_both, got_both]
     )
     input_grad = order.call(
-        input_kernel, "input_back", shaped(*images_in.shape), [x_pad, *gh, norm1_gain, gf, gf2], room=8
+        input_kernel, "input_back", shaped(*images_in.shape), [first_normed, first_inverse, *gh, norm1_gain, gf, gf2], room=8
     )
     done1, small = order.call(
         attn_done_kernel, "attn1_end", (held(height, width), held(16, width)),
@@ -686,26 +706,24 @@
     )
     vector = shaped(width)
     small_out = order.call(
-        small_end_kernel, "small_end",
-        (vector, vector, vector, vector, vector, shaped(2, span), shaped(units), vector),
-        [small, small2],
-    )
+        small_end_kernel, "small_end", (vector, vector, vector, shaped(2, span), shaped(units), vector), [small]
+    )
+    norm1_out = order.call(norm1_end_kernel, "norm1_end", (vector, vector), [small, small2])
 
     return (
         block_out,
         input_grad,
+        *norm1_out,
+        qkv_block.transpose(1, 0, 2),
+        small_out[3],
+        out_block.T,
+        small_out[2],
         small_out[0],
         small_out[1],
-        qkv_block.transpose(1, 0, 2),
+        up_block,
+        small_out[4],
+        down_block.T,
         small_out[5],
-        out_block.T,
-        small_out[4],
-        small_out[2],
-        small_out[3],
-        up_block,
-        small_out[6],
-        down_block.T,
-        small_out[7],
     )
 
 

time: 157 us -> 155 us (0.987)
  waiting for transfers between devices: 62.9 us -> 57.8 us
    ppermute x20 -> x22, waiting for transfers between devices: 30.5 us -> 26.5 us  [swap_bit(): return lax.ppermute(value, 'dp', [(i, i ^ 1 << bit) for i in range(size)])]
    ppermute x20 -> x22, starting transfers between devices: 17.9 us -> 19 us  [swap_bit(): return lax.ppermute(value, 'dp', [(i, i ^ 1 << bit) for i in range(size)])]
    pallas_call x31 -> x32, Pallas kernels: 59.1 us -> 60 us  [call(): pl.pallas_call(body, out_shape=outs, name=name, in_specs=[SMEM_SPEC] + [p...]
    unnamed x32 -> x30, local copies, waits for them, and re-layouts: 4.54 us -> 5.2 us
  transfers between devices with their start and end apart: 27 -> 29, of which waited for: 17 -> 16; matrix products, arithmetic and copies ran while one was open for 0% -> 0% of each run, Pallas kernels for 34% -> 36%
where the time goes in v5:
time: 155 us
  Pallas kernels  60 us (39%)
  waiting for transfers between devices  57.8 us (37%)
  starting transfers between devices  28.5 us (18%)
  local copies, waits for them, and re-layouts  5.29 us (3%)
  between operations  2.22 us (1%)
    pallas_call x32, Pallas kernels, call(): pl.pallas_call(body, out_shape=outs, name=name, in_specs=[SMEM_SPEC] + [p...  60 us
    ppermute x7, waiting for transfers between devices, swap_sides(): return lax.ppermute(value, 'tensor', [(0, 1), (1, 0)])  31.2 us
    ppermute x22, waiting for transfers between devices, swap_bit(): return lax.ppermute(value, 'dp', [(i, i ^ 1 << bit) for i in range(size)])  26.5 us
    ppermute x22, starting transfers between devices, swap_bit(): return lax.ppermute(value, 'dp', [(i, i ^ 1 << bit) for i in range(size)])  19 us
    ppermute x7, starting transfers between devices, swap_sides(): return lax.ppermute(value, 'tensor', [(0, 1), (1, 0)])  9.52 us
    unnamed x30, local copies, waits for them, and re-layouts  5.2 us
  transfers between devices with their start and end apart: 29, of which 16 were waited for; matrix products, arithmetic and copies ran while one was open for 0% of the time, Pallas kernels for 36%

profile of v5, /device:TPU:0, one launch (start us, length us, event | category | flops | bytes accessed | tf_op | source)
XLA Modules:
  0.0 154.7 jit_solution(2818833664513911592)
XLA Ops:
  1.6 3.0 %collective-permute-start = (f32[96,768]{1,0:T(8,128)S(1)}, f32[96,768]{1,0:T(8,128)S(1)}, u32[]{:S(2)}, u32[]{:S(2)}) collective-permute-start(f32[96,768]{1,0:T(8,128)S(1)} %dynamic-slice_convert_fusion), channel_id=1, source_target_pairs={{0,1},{1,0},{2,3},{3,2},{4,5},{5,4},{6,7},{7,6},{8,9},{9,8},{10,11... | collective-permute-start | bytes 884744 | tf_op jit(solution)/shard_map/ppermute | solution.py:482
  6.0 8.0 %attn_forward.1 = (bf16[544,768]{1,0:T(8,128)(2,1)S(1)}, bf16[3,544,384]{2,1,0:T(8,128)(2,1)S(1)}, bf16[544,768]{1,0:T(8,128)(2,1)S(1)}, bf16[544,768]{1,0:T(8,1...) custom-call(s32[8]{0:T(128)S(1)} %stack.27.refs_0_, ...), custom_call_target="tpu_custom_call" | custom-call | flops 1 | bytes 1 | tf_op jit(solution)/shard_map/attn_forward/pallas_call | solution.py:467
  14.1 2.0 %collective-permute-start.1 = (f32[200,384]{1,0:T(8,128)S(1)}, f32[200,384]{1,0:T(8,128)S(1)}, u32[]{:S(2)}, u32[]{:S(2)}) collective-permute-start(f32[200,384]{1,0:T(8,128)S(1)} %get-tuple-element.118.refs_3_.refs_6_), channel_id=1, source_target_pairs={{0,1},{1,0},{2,3},{3,2},{4,5},{5,4},{6,7},{7,6},{8,9},{9,8},{10,11... | collective-permute-start | bytes 921608 | tf_op jit(solution)/shard_map/ppermute | solution.py:482
  18.8 2.3 %grad_act.1 = (bf16[208,768]{1,0:T(8,128)(2,1)S(1)}, f32[208,1536]{1,0:T(8,128)S(1)}, f32[1,768]{1,0:T(1,128)S(1)}, bf16[336,768]{1,0:T(8,128)(2,1)S(1)}, f32[336,1536]{1,0:T(8,128)S(1)}, /*index=5*/f32[1,768]{1,0:T(1,128)S(1)}) custom-call(s32[8]{0:T(128)S(1)} %stack.27.refs_0_, bf16[544,768]{1,0:T(8,128)(2,1)S(1)} %get-tuple-element.114.refs_1_.refs_6_, ...), custom_call_target="tpu_custom_call" | custom-call | flops 1 | bytes 1 | tf_op jit(solution)/shard_map/grad_act/pallas_call | solution.py:467
  21.1 2.0 %collective-permute-done.2.refs_1_ = f32[96,384]{1,0:T(8,128)S(1)} collective-permute-done((f32[96,384]{1,0:T(8,128)S(1)}, f32[96,384]{1,0:T(8,128)S(1)}, u32[]{:S(2)}, u32[]{:S(2)}) %collective-permute-start.2) | collective-permute-done | bytes 147488 | tf_op jit(solution)/shard_map/ppermute | solution.py:486
  28.5 4.2 %mlp_b.1 = (f32[336,768]{1,0:T(8,128)S(1)}, bf16[336,768]{1,0:T(8,128)(2,1)S(1)}, bf16[336,1536]{1,0:T(8,128)(2,1)S(1)}, bf16[336,1536]{1,0:T(8,128)(2,1)S(1)}, ...) custom-call(s32[8]{0:T(128)S(1)} %stack.27.refs_0_, bf16[544,768]{1,0:T(8,128)(2,1)S(1)} %get-tuple-element.113.refs_1_.refs_6_, ...), custom_call_target="tpu_custom_call" | custom-call | flops 1 | bytes 1 | tf_op jit(solution)/shard_map/mlp_b/pallas_call | solution.py:467
  33.6 3.2 %mlp_a.1 = (f32[208,768]{1,0:T(8,128)S(1)}, bf16[208,768]{1,0:T(8,128)(2,1)S(1)}, bf16[208,1536]{1,0:T(8,128)(2,1)S(1)}, bf16[208,1536]{1,0:T(8,128)(2,1)S(1)}, ...) custom-call(s32[8]{0:T(128)S(1)} %stack.27.refs_0_, bf16[544,768]{1,0:T(8,128)(2,1)S(1)} %get-tuple-element.113.refs_1_.refs_6_, ...), custom_call_target="tpu_custom_call" | custom-call | flops 1 | bytes 1 | tf_op jit(solution)/shard_map/mlp_a/pallas_call | solution.py:467
  37.2 3.0 %down_weights.1 = (f32[384,1536]{1,0:T(8,128)S(1)}, f32[384,768]{1,0:T(8,128)S(1)}, f32[384,768]{1,0:T(8,128)S(1)}) custom-call(s32[8]{0:T(128)S(1)} %stack.27.refs_0_, bf16[208,768]{1,0:T(8,128)(2,1)S(1)} %get-tuple-element.121.refs_3_.refs_1_, bf16[336,768]{1,0:T(8,128)(2,1)S(1)} %get-tuple-element.135.refs_2_, ...), custom_call_target="tpu_custom_call" | custom-call | flops 1 | bytes 1 | tf_op jit(solution)/shard_map/down_weights/pallas_call | solution.py:467
  40.8 2.8 %up_weights.1 = (f32[384,1536]{1,0:T(8,128)S(1)}, f32[384,768]{1,0:T(8,128)S(1)}, f32[384,768]{1,0:T(8,128)S(1)}) custom-call(s32[8]{0:T(128)S(1)} %stack.27.refs_0_, bf16[208,768]{1,0:T(8,128)(2,1)S(1)} %get-tuple-element.131.refs_1_, bf16[336,768]{1,0:T(8,128)(2,1)S(1)} %get-tuple-element.132.refs_2_, bf16[208,1536]{1,0:T(8,128)(2,1)S(1)} %get-tuple-element.133.refs_3_, ...), custom_call_target="tpu_custom_call" | custom-call | flops 1 | bytes 1 | tf_op jit(solution)/shard_map/up_weights/pallas_call | solution.py:467
  50.9 2.0 %mlp_part.1.refs_7_.refs_3_ = f32[528,768]{1,0:T(8,128)S(1)} custom-call(s32[8]{0:T(128)S(1)} %stack.27.refs_0_, bf16[208,1536]{1,0:T(8,128)(2,1)S(1)} %get-tuple-element.129.refs_3_.refs_1_, bf16[336,1536]{1,0:T(8,128)(2,1)S(1)} %get-tuple-element.130.refs_4_.refs_2_, bf16[1536,768]{1,0:T(8,128)(2,1)S(1)} %copy-done.1, ...), custom_call_target="tpu_custom_call" | custom-call | flops 1 | bytes 1 | tf_op jit(solution)/shard_map/mlp_part/pallas_call | solution.py:467
  54.5 2.3 %attn_again.1 = (f32[6,208,208]{2,1,0:T(8,128)S(1)}, f32[6,336,336]{2,1,0:T(8,128)S(1)}, f32[208,768]{1,0:T(8,128)S(1)}, f32[336,768]{1,0:T(8,128)S(1)}, f32[208...) custom-call(s32[8]{0:T(128)S(1)} %stack.27.refs_0_, ...), custom_call_target="tpu_custom_call" | custom-call | flops 1 | bytes 1 | tf_op jit(solution)/shard_map/attn_again/pallas_call | solution.py:467
  56.8 18.5 %collective-permute-done.13.refs_2_ = f32[528,768]{1,0:T(8,128)S(1)} collective-permute-done((f32[528,768]{1,0:T(8,128)S(1)}, f32[528,768]{1,0:T(8,128)S(1)}, u32[]{:S(2)}, u32[]{:S(2)}) %collective-permute-start.13) | collective-permute-done | bytes 1622048 | tf_op jit(solution)/shard_map/ppermute | solution.py:482
  75.3 5.3 %attn_backward_b.1 = (bf16[3,336,384]{2,1,0:T(8,128)(2,1)S(1)}, bf16[336,768]{1,0:T(8,128)(2,1)S(1)}, f32[336,768]{1,0:T(8,128)S(1)}, f32[8,768]{1,0:T(8,128)S(1)}, f32[328,768]{1,0:T(8,128)S(1)}) custom-call(s32[8]{0:T(128)S(1)} %stack.27.refs_0_, f32[528,768]{1,0:T(8,128)S(1)} %get-tuple-element.144.refs_1_, ...), custom_call_target="tpu_custom_call" | custom-call | flops 8999999488 | bytes 1 | tf_op jit(solution)/shard_map/attn_backward_b/pallas_call | solution.py:467
  85.2 3.8 %attn_backward_a.1 = (bf16[3,208,384]{2,1,0:T(8,128)(2,1)S(1)}, bf16[208,768]{1,0:T(8,128)(2,1)S(1)}, f32[208,768]{1,0:T(8,128)S(1)}, f32[8,768]{1,0:T(8,128)S(1)}, f32[528,768]{1,0:T(8,128)S(1)}) custom-call(s32[8]{0:T(128)S(1)} %stack.27.refs_0_, f32[528,768]{1,0:T(8,128)S(1)} %get-tuple-element.144.refs_1_, ...), custom_call_target="tpu_custom_call" | custom-call | flops 1 | bytes 1 | tf_op jit(solution)/shard_map/attn_backward_a/pallas_call | solution.py:467
  89.0 3.3 %attn_weights.1 = (f32[384,768]{1,0:T(8,128)S(1)}, f32[384,768]{1,0:T(8,128)S(1)}, f32[16,768]{1,0:T(8,128)S(1)}, f32[400,768]{1,0:T(8,128)S(1)}, f32[384,768]{1,0:T(8,128)S(1)}) custom-call(s32[8]{0:T(128)S(1)} %stack.27.refs_0_, bf16[544,768]{1,0:T(8,128)(2,1)S(1)} %get-tuple-element.115.refs_2_.refs_1_, ...), custom_call_target="tpu_custom_call" | custom-call | flops 1 | bytes 1 | tf_op jit(solution)/shard_map/attn_weights/pallas_call | solution.py:467
  94.9 2.7 %collective-permute-start.21 = (f32[48,3072]{1,0:T(8,128)S(1)}, f32[48,3072]{1,0:T(8,128)S(1)}, u32[]{:S(2)}, u32[]{:S(2)}) collective-permute-start(f32[48,3072]{1,0:T(8,128)S(1)} %get-tuple-element.177.refs_4_), channel_id=1, source_target_pairs={{0,16},{2,18},{4,20},{6,22},{8,24},{10,26},{12,28},{14,30},{16,0},... | collective-permute-start | bytes 1769480 | tf_op jit(solution)/shard_map/ppermute | solution.py:486
  101.1 8.9 %collective-permute-done.12.refs_4_ = f32[528,768]{1,0:T(8,128)S(1)} collective-permute-done((f32[528,768]{1,0:T(8,128)S(1)}, f32[528,768]{1,0:T(8,128)S(1)}, u32[]{:S(2)}, u32[]{:S(2)}) %collective-permute-start.12) | collective-permute-done | bytes 1622048 | tf_op jit(solution)/shard_map/ppermute | solution.py:482
  110.1 2.1 %block_out.1.refs_4_ = bf16[522,768]{1,0:T(8,128)(2,1)} custom-call(s32[8]{0:T(128)S(1)} %stack.27.refs_0_, f32[208,768]{1,0:T(8,128)S(1)} %get-tuple-element.128.refs_5_.refs_4_.refs_1_, f32[336,768]{1,0:T(8,128)S(1)} %get-tuple-element.127.refs_12_.refs_5_.refs_2_, f32[528,768]{1,0:T(8,128)S(1)} %mlp_part.1.refs_7_.refs_3_, ...), custom_call_target="tpu_custom_call" | custom-call | flops 99999997952 | bytes 1 | tf_op jit(solution)/shard_map/block_out/pallas_call | solution.py:467
  112.1 3.5 %collective-permute-done.23.refs_3_ = f32[208,768]{1,0:T(8,128)S(1)} collective-permute-done((f32[208,768]{1,0:T(8,128)S(1)}, f32[208,768]{1,0:T(8,128)S(1)}, u32[]{:S(2)}, u32[]{:S(2)}) %collective-permute-start.23) | collective-permute-done | bytes 639008 | tf_op jit(solution)/shard_map/ppermute | solution.py:486
  119.0 6.9 %collective-permute-done.22.refs_2_ = f32[192,768]{1,0:T(8,128)S(1)} collective-permute-done((f32[192,768]{1,0:T(8,128)S(1)}, f32[192,768]{1,0:T(8,128)S(1)}, u32[]{:S(2)}, u32[]{:S(2)}) %collective-permute-start.22) | collective-permute-done | bytes 589856 | tf_op jit(solution)/shard_map/ppermute | solution.py:486
  127.1 2.9 %collective-permute-done.25.refs_3_ = f32[112,768]{1,0:T(8,128)S(1)} collective-permute-done((f32[112,768]{1,0:T(8,128)S(1)}, f32[112,768]{1,0:T(8,128)S(1)}, u32[]{:S(2)}, u32[]{:S(2)}) %collective-permute-start.25) | collective-permute-done | bytes 344096 | tf_op jit(solution)/shard_map/ppermute | solution.py:486
  131.4 6.9 %collective-permute-done.24.refs_2_ = f32[96,768]{1,0:T(8,128)S(1)} collective-permute-done((f32[96,768]{1,0:T(8,128)S(1)}, f32[96,768]{1,0:T(8,128)S(1)}, u32[]{:S(2)}, u32[]{:S(2)}) %collective-permute-start.24) | collective-permute-done | bytes 294944 | tf_op jit(solution)/shard_map/ppermute | solution.py:486
  140.4 2.0 %collective-permute-done.20.refs_7_ = f32[528,768]{1,0:T(8,128)S(1)} collective-permute-done((f32[528,768]{1,0:T(8,128)S(1)}, f32[528,768]{1,0:T(8,128)S(1)}, u32[]{:S(2)}, u32[]{:S(2)}) %collective-permute-start.20) | collective-permute-done | bytes 1622048 | tf_op jit(solution)/shard_map/ppermute | solution.py:482
  143.4 2.7 %input_back.1.refs_4_ = f32[522,768]{1,0:T(8,128)} custom-call(s32[8]{0:T(128)S(1)} %stack.27.refs_0_, f32[544,768]{1,0:T(8,128)S(1)} %get-tuple-element.148.refs_3_.refs_1_, f32[544,1]{1,0:T(8,128)S(1)} %get-tuple-element.180.refs_2_, f32[208,768]{1,0:T(8,128)S(1)} %get-tuple-element.181.refs_3_, f32[336,768]{1,0:T(8,128)S(1)} %get-tuple-element.182.refs_4_, ...), custom_call_target="tpu_custom_call" | custom-call | flops 1 | bytes 1 | tf_op jit(solution)/shard_map/input_back/pallas_call | solution.py:467
  (98 shorter events, 48.1 us)
Async XLA Ops:
  1.6 14.5 %collective-permute-start = (f32[96,768]{1,0:T(8,128)S(1)}, f32[96,768]{1,0:T(8,128)S(1)}, u32[]{:S(2)}, u32[]{:S(2)}) collective-permute-start(f32[96,768]{1,0:T(8,128)S(1)} %dynamic-slice_convert_fusion), channel_id=1, source_target_pairs={{0,1},{1,0},{2,3},{3,2},{4,5},{5,4},{6,7},{7,6},{8,9},{9,8},{10,11... | collective-permute-start | bytes 884744 | tf_op jit(solution)/shard_map/ppermute | solution.py:482
  14.0 14.5 %collective-permute-start.7 = (f32[328,384]{1,0:T(8,128)S(1)}, f32[328,384]{1,0:T(8,128)S(1)}, u32[]{:S(2)}, u32[]{:S(2)}) collective-permute-start(f32[328,384]{1,0:T(8,128)S(1)} %get-tuple-element.125.refs_3_.refs_7_), channel_id=1, source_target_pairs={{0,1},{1,0},{2,3},{3,2},{4,5},{5,4},{6,7},{7,6},{8,9},{9,8},{10,11... | collective-permute-start | bytes 1511432 | tf_op jit(solution)/shard_map/ppermute | solution.py:482
  14.1 19.5 %collective-permute-start.1 = (f32[200,384]{1,0:T(8,128)S(1)}, f32[200,384]{1,0:T(8,128)S(1)}, u32[]{:S(2)}, u32[]{:S(2)}) collective-permute-start(f32[200,384]{1,0:T(8,128)S(1)} %get-tuple-element.118.refs_3_.refs_6_), channel_id=1, source_target_pairs={{0,1},{1,0},{2,3},{3,2},{4,5},{5,4},{6,7},{7,6},{8,9},{9,8},{10,11... | collective-permute-start | bytes 921608 | tf_op jit(solution)/shard_map/ppermute | solution.py:482
  16.7 6.4 %collective-permute-start.2 = (f32[96,384]{1,0:T(8,128)S(1)}, f32[96,384]{1,0:T(8,128)S(1)}, u32[]{:S(2)}, u32[]{:S(2)}) collective-permute-start(f32[96,384]{1,0:T(8,128)S(1)} %get-tuple-element.119), channel_id=1, source_target_pairs={{0,4},{2,6},{4,0},{6,2},{8,12},{10,14},{12,8},{14,10},{16,20},{18,... | collective-permute-start | bytes 442376 | tf_op jit(solution)/shard_map/ppermute | solution.py:486
  18.3 6.4 %collective-permute-start.3 = (f32[96,384]{1,0:T(8,128)S(1)}, f32[96,384]{1,0:T(8,128)S(1)}, u32[]{:S(2)}, u32[]{:S(2)}) collective-permute-start(f32[96,384]{1,0:T(8,128)S(1)} %get-tuple-element.120), channel_id=1, source_target_pairs={{0,4},{2,6},{4,0},{6,2},{8,12},{10,14},{12,8},{14,10},{16,20},{18,... | collective-permute-start | bytes 442376 | tf_op jit(solution)/shard_map/ppermute | solution.py:486
  18.8 8.1 %collective-permute-start.4 = (f32[96,768]{1,0:T(8,128)S(1)}, f32[96,768]{1,0:T(8,128)S(1)}, u32[]{:S(2)}, u32[]{:S(2)}) collective-permute-start(f32[96,768]{1,0:T(8,128)S(1)} %get-tuple-element.116.refs_3_.refs_2_), channel_id=1, source_target_pairs={{0,2},{2,0},{4,6},{6,4},{8,10},{10,8},{12,14},{14,12},{16,18},{18,... | collective-permute-start | bytes 884744 | tf_op jit(solution)/shard_map/ppermute | solution.py:486
  36.9 38.5 %collective-permute-start.13 = (f32[528,768]{1,0:T(8,128)S(1)}, f32[528,768]{1,0:T(8,128)S(1)}, u32[]{:S(2)}, u32[]{:S(2)}) collective-permute-start(f32[528,768]{1,0:T(8,128)S(1)} %get-tuple-element.144.refs_1_), channel_id=1, source_target_pairs={{0,1},{1,0},{2,3},{3,2},{4,5},{5,4},{6,7},{7,6},{8,9},{9,8},{10,11... | collective-permute-start | bytes 4866056 | tf_op jit(solution)/shard_map/ppermute | solution.py:482
  40.3 4.5 %collective-permute-start.11 = (f32[384,768]{1,0:T(8,128)S(1)}, f32[384,768]{1,0:T(8,128)S(1)}, u32[]{:S(2)}, u32[]{:S(2)}) collective-permute-start(f32[384,768]{1,0:T(8,128)S(1)} %get-tuple-element.141), channel_id=1, source_target_pairs={{0,2},{2,0},{4,6},{6,4},{8,10},{10,8},{12,14},{14,12},{16,18},{18,... | collective-permute-start | bytes 3538952 | tf_op jit(solution)/shard_map/ppermute | solution.py:486
  45.7 34.9 %collective-permute-start.15 = (f32[192,1536]{1,0:T(8,128)S(1)}, f32[192,1536]{1,0:T(8,128)S(1)}, u32[]{:S(2)}, u32[]{:S(2)}) collective-permute-start(f32[192,1536]{1,0:T(8,128)S(1)} %get-tuple-element.142.refs_4_), channel_id=1, source_target_pairs={{0,4},{2,6},{4,0},{6,2},{8,12},{10,14},{12,8},{14,10},{16,20},{18,... | collective-permute-start | bytes 3538952 | tf_op jit(solution)/shard_map/ppermute | solution.py:486
  49.0 32.3 %collective-permute-start.14 = (f32[192,1536]{1,0:T(8,128)S(1)}, f32[192,1536]{1,0:T(8,128)S(1)}, u32[]{:S(2)}, u32[]{:S(2)}) collective-permute-start(f32[192,1536]{1,0:T(8,128)S(1)} %get-tuple-element.143.refs_4_), channel_id=1, source_target_pairs={{0,8},{2,10},{4,12},{6,14},{8,0},{10,2},{12,4},{14,6},{16,24},{18,... | collective-permute-start | bytes 3538952 | tf_op jit(solution)/shard_map/ppermute | solution.py:486
  52.9 57.2 %collective-permute-start.12 = (f32[528,768]{1,0:T(8,128)S(1)}, f32[528,768]{1,0:T(8,128)S(1)}, u32[]{:S(2)}, u32[]{:S(2)}) collective-permute-start(f32[528,768]{1,0:T(8,128)S(1)} %mlp_part.1.refs_7_.refs_3_), channel_id=1, source_target_pairs={{0,1},{1,0},{2,3},{3,2},{4,5},{5,4},{6,7},{7,6},{8,9},{9,8},{10,11... | collective-permute-start | bytes 4866056 | tf_op jit(solution)/shard_map/ppermute | solution.py:482
  82.1 10.8 %collective-permute-start.19 = (f32[96,1536]{1,0:T(8,128)S(1)}, f32[96,1536]{1,0:T(8,128)S(1)}, u32[]{:S(2)}, u32[]{:S(2)}) collective-permute-start(f32[96,1536]{1,0:T(8,128)S(1)} %get-tuple-element.160.refs_13_), channel_id=1, source_target_pairs={{0,4},{2,6},{4,0},{6,2},{8,12},{10,14},{12,8},{14,10},{16,20},{18,... | collective-permute-start | bytes 1769480 | tf_op jit(solution)/shard_map/ppermute | solution.py:486
  83.6 10.5 %collective-permute-start.18 = (f32[96,1536]{1,0:T(8,128)S(1)}, f32[96,1536]{1,0:T(8,128)S(1)}, u32[]{:S(2)}, u32[]{:S(2)}) collective-permute-start(f32[96,1536]{1,0:T(8,128)S(1)} %get-tuple-element.159.refs_3_), channel_id=1, source_target_pairs={{0,8},{2,10},{4,12},{6,14},{8,0},{10,2},{12,4},{14,6},{16,24},{18,... | collective-permute-start | bytes 1769480 | tf_op jit(solution)/shard_map/ppermute | solution.py:486
  92.3 5.2 %collective-permute-start.17 = (f32[400,768]{1,0:T(8,128)S(1)}, f32[400,768]{1,0:T(8,128)S(1)}, u32[]{:S(2)}, u32[]{:S(2)}) collective-permute-start(f32[400,768]{1,0:T(8,128)S(1)} %get-tuple-element.174), channel_id=1, source_target_pairs={{0,2},{2,0},{4,6},{6,4},{8,10},{10,8},{12,14},{14,12},{16,18},{18,... | collective-permute-start | bytes 3686408 | tf_op jit(solution)/shard_map/ppermute | solution.py:486
  92.4 7.4 %collective-permute-start.16 = (f32[384,768]{1,0:T(8,128)S(1)}, f32[384,768]{1,0:T(8,128)S(1)}, u32[]{:S(2)}, u32[]{:S(2)}) collective-permute-start(f32[384,768]{1,0:T(8,128)S(1)} %get-tuple-element.171), channel_id=1, source_target_pairs={{0,2},{2,0},{4,6},{6,4},{8,10},{10,8},{12,14},{14,12},{16,18},{18,... | collective-permute-start | bytes 3538952 | tf_op jit(solution)/shard_map/ppermute | solution.py:486
  92.9 49.6 %collective-permute-start.20 = (f32[528,768]{1,0:T(8,128)S(1)}, f32[528,768]{1,0:T(8,128)S(1)}, u32[]{:S(2)}, u32[]{:S(2)}) collective-permute-start(f32[528,768]{1,0:T(8,128)S(1)} %get-tuple-element.183.refs_6_), channel_id=1, source_target_pairs={{0,1},{1,0},{2,3},{3,2},{4,5},{5,4},{6,7},{7,6},{8,9},{9,8},{10,11... | collective-permute-start | bytes 4866056 | tf_op jit(solution)/shard_map/ppermute | solution.py:482
  94.9 44.2 %collective-permute-start.21 = (f32[48,3072]{1,0:T(8,128)S(1)}, f32[48,3072]{1,0:T(8,128)S(1)}, u32[]{:S(2)}, u32[]{:S(2)}) collective-permute-start(f32[48,3072]{1,0:T(8,128)S(1)} %get-tuple-element.177.refs_4_), channel_id=1, source_target_pairs={{0,16},{2,18},{4,20},{6,22},{8,24},{10,26},{12,28},{14,30},{16,0},... | collective-permute-start | bytes 1769480 | tf_op jit(solution)/shard_map/ppermute | solution.py:486
  98.2 17.4 %collective-permute-start.23 = (f32[208,768]{1,0:T(8,128)S(1)}, f32[208,768]{1,0:T(8,128)S(1)}, u32[]{:S(2)}, u32[]{:S(2)}) collective-permute-start(f32[208,768]{1,0:T(8,128)S(1)} %get-tuple-element.178.refs_3_), channel_id=1, source_target_pairs={{0,4},{2,6},{4,0},{6,2},{8,12},{10,14},{12,8},{14,10},{16,20},{18,... | collective-permute-start | bytes 1916936 | tf_op jit(solution)/shard_map/ppermute | solution.py:486
  100.5 25.4 %collective-permute-start.22 = (f32[192,768]{1,0:T(8,128)S(1)}, f32[192,768]{1,0:T(8,128)S(1)}, u32[]{:S(2)}, u32[]{:S(2)}) collective-permute-start(f32[192,768]{1,0:T(8,128)S(1)} %get-tuple-element.179.refs_6_), channel_id=1, source_target_pairs={{0,4},{2,6},{4,0},{6,2},{8,12},{10,14},{12,8},{14,10},{16,20},{18,... | collective-permute-start | bytes 1769480 | tf_op jit(solution)/shard_map/ppermute | solution.py:486
  117.4 12.7 %collective-permute-start.25 = (f32[112,768]{1,0:T(8,128)S(1)}, f32[112,768]{1,0:T(8,128)S(1)}, u32[]{:S(2)}, u32[]{:S(2)}) collective-permute-start(f32[112,768]{1,0:T(8,128)S(1)} %get-tuple-element.188.refs_3_), channel_id=1, source_target_pairs={{0,8},{2,10},{4,12},{6,14},{8,0},{10,2},{12,4},{14,6},{16,24},{18,... | collective-permute-start | bytes 1032200 | tf_op jit(solution)/shard_map/ppermute | solution.py:486
  126.6 11.7 %collective-permute-start.24 = (f32[96,768]{1,0:T(8,128)S(1)}, f32[96,768]{1,0:T(8,128)S(1)}, u32[]{:S(2)}, u32[]{:S(2)}) collective-permute-start(f32[96,768]{1,0:T(8,128)S(1)} %get-tuple-element.190.refs_4_), channel_id=1, source_target_pairs={{0,8},{2,10},{4,12},{6,14},{8,0},{10,2},{12,4},{14,6},{16,24},{18,... | collective-permute-start | bytes 884744 | tf_op jit(solution)/shard_map/ppermute | solution.py:486
  130.7 15.7 %collective-permute-start.26 = (f32[64,768]{1,0:T(8,128)S(1)}, f32[64,768]{1,0:T(8,128)S(1)}, u32[]{:S(2)}, u32[]{:S(2)}) collective-permute-start(f32[64,768]{1,0:T(8,128)S(1)} %get-tuple-element.193.refs_3_), channel_id=1, source_target_pairs={{0,16},{2,18},{4,20},{6,22},{8,24},{10,26},{12,28},{14,30},{16,0},... | collective-permute-start | bytes 589832 | tf_op jit(solution)/shard_map/ppermute | solution.py:486
  138.9 10.6 %collective-permute-start.28 = (f32[48,768]{1,0:T(8,128)S(1)}, f32[48,768]{1,0:T(8,128)S(1)}, u32[]{:S(2)}, u32[]{:S(2)}) collective-permute-start(f32[48,768]{1,0:T(8,128)S(1)} %get-tuple-element.194.refs_3_), channel_id=1, source_target_pairs={{0,16},{2,18},{4,20},{6,22},{8,24},{10,26},{12,28},{14,30},{16,0},... | collective-permute-start | bytes 442376 | tf_op jit(solution)/shard_map/ppermute | solution.py:486
  148.4 4.5 %collective-permute-start.27 = (f32[16,768]{1,0:T(8,128)S(1)}, f32[16,768]{1,0:T(8,128)S(1)}, u32[]{:S(2)}, u32[]{:S(2)}) collective-permute-start(f32[16,768]{1,0:T(8,128)S(1)} %get-tuple-element.198.refs_1_), channel_id=1, source_target_pairs={{0,1},{1,0},{2,3},{3,2},{4,5},{5,4},{6,7},{7,6},{8,9},{9,8},{10,11... | collective-permute-start | bytes 147464 | tf_op jit(solution)/shard_map/ppermute | solution.py:482
  (20 other events, 100.0 us)

commit v6 on v5

--- a/solution.py
+++ b/solution.py
@@ -335,7 +335,7 @@
         out_ref[sent_of(group), :] = mm(act_ref[...], down_ref[...])[: SENT[group]]
 
 
-def small_end_kernel(info_ref, small_ref, gain2, bias2, outb, qvb, upb, downb):
+def small_end_kernel(small_ref, gain2, bias2, outb, qvb, upb, downb):
     total = small_ref[...]
     width = total.shape[1]
     for n, ref in enumerate((gain2, bias2, outb)):
@@ -421,12 +421,13 @@
     total_ref[...] = small_ref[...] + piece_ref[rows:, :]
 
 
-def attn_last_kernel(info_ref, done1_ref, keep2_ref, got2_ref, qkv_ref, out_ref):
+def attn_last_kernel(info_ref, done1_ref, keep2_ref, got2_ref, small_ref, qkv_ref, out_ref, *rest):
     span = out_ref.shape[1]
     qkv_ref[0] = done1_ref[:, :span]
     qkv_ref[1] = done1_ref[:, span:]
     qkv_ref[2] = keep2_ref[:, :span] + got2_ref[:, :span]
     out_ref[...] = keep2_ref[:, span:] + got2_ref[:, span:]
+    small_end_kernel(small_ref, *rest)
 
 
 SMEM_SPEC = pl.BlockSpec(memory_space=pltpu.SMEM)
@@ -700,13 +701,14 @@
         [attn1.keep, attn1.small, *attn1.got],
     )
     small2 = swap_sides(small)
-    qkv_block, out_block = order.call(
-        attn_last_kernel, "attn_end", (shaped(3, height, span), shaped(height, span)),
-        [done1, attn2.keep, *attn2.got],
-    )
     vector = shaped(width)
-    small_out = order.call(
-        small_end_kernel, "small_end", (vector, vector, vector, shaped(2, span), shaped(units), vector), [small]
+    qkv_block, out_block, *small_out = order.call(
+        attn_last_kernel, "attn_end",
+        (
+            shaped(3, height, span), shaped(height, span),
+            vector, vector, vector, shaped(2, span), shaped(units), vector,
+        ),
+        [done1, attn2.keep, *attn2.got, small],
     )
     norm1_out = order.call(norm1_end_kernel, "norm1_end", (vector, vector), [small, small2])
 

time: 155 us -> 155 us (level)
  waiting for transfers between devices: 57.8 us -> 59.6 us
    ppermute x7, waiting for transfers between devices: 31.2 us -> 33 us  [swap_sides(): return lax.ppermute(value, 'tensor', [(0, 1), (1, 0)])]
    pallas_call x32 -> x31, Pallas kernels: 60 us -> 58.9 us  [call(): pl.pallas_call(body, out_shape=outs, name=name, in_specs=[SMEM_SPEC] + [p...]
    unnamed x30 -> x28, local copies, waits for them, and re-layouts: 5.2 us -> 4.52 us
  transfers between devices with their start and end apart: 29 -> 29, of which waited for: 16 -> 17; matrix products, arithmetic and copies ran while one was open for 0% -> 0% of each run, Pallas kernels for 36% -> 35%
where the time goes in v6:
time: 155 us
  waiting for transfers between devices  59.6 us (38%)
  Pallas kernels  58.9 us (38%)
  starting transfers between devices  28.4 us (18%)
  local copies, waits for them, and re-layouts  4.6 us (3%)
  between operations  2.22 us (1%)
    pallas_call x31, Pallas kernels, call(): pl.pallas_call(body, out_shape=outs, name=name, in_specs=[SMEM_SPEC] + [p...  58.9 us
    ppermute x7, waiting for transfers between devices, swap_sides(): return lax.ppermute(value, 'tensor', [(0, 1), (1, 0)])  33 us
    ppermute x22, waiting for transfers between devices, swap_bit(): return lax.ppermute(value, 'dp', [(i, i ^ 1 << bit) for i in range(size)])  26.5 us
    ppermute x22, starting transfers between devices, swap_bit(): return lax.ppermute(value, 'dp', [(i, i ^ 1 << bit) for i in range(size)])  18.9 us
    ppermute x7, starting transfers between devices, swap_sides(): return lax.ppermute(value, 'tensor', [(0, 1), (1, 0)])  9.51 us
    unnamed x28, local copies, waits for them, and re-layouts  4.52 us
  transfers between devices with their start and end apart: 29, of which 17 were waited for; matrix products, arithmetic and copies ran while one was open for 0% of the time, Pallas kernels for 35%

profile of v6, /device:TPU:0, one launch (start us, length us, event | category | flops | bytes accessed | tf_op | source)
XLA Modules:
  0.0 154.6 jit_solution(14295971085829161374)
XLA Ops:
  1.6 3.0 %collective-permute-start = (f32[96,768]{1,0:T(8,128)S(1)}, f32[96,768]{1,0:T(8,128)S(1)}, u32[]{:S(2)}, u32[]{:S(2)}) collective-permute-start(f32[96,768]{1,0:T(8,128)S(1)} %dynamic-slice_convert_fusion), channel_id=1, source_target_pairs={{0,1},{1,0},{2,3},{3,2},{4,5},{5,4},{6,7},{7,6},{8,9},{9,8},{10,11... | collective-permute-start | bytes 884744 | tf_op jit(solution)/shard_map/ppermute | solution.py:483
  6.0 8.0 %attn_forward.1 = (bf16[544,768]{1,0:T(8,128)(2,1)S(1)}, bf16[3,544,384]{2,1,0:T(8,128)(2,1)S(1)}, bf16[544,768]{1,0:T(8,128)(2,1)S(1)}, bf16[544,768]{1,0:T(8,1...) custom-call(s32[8]{0:T(128)S(1)} %stack.27.refs_0_, ...), custom_call_target="tpu_custom_call" | custom-call | flops 1 | bytes 1 | tf_op jit(solution)/shard_map/attn_forward/pallas_call | solution.py:468
  14.1 2.0 %collective-permute-start.1 = (f32[200,384]{1,0:T(8,128)S(1)}, f32[200,384]{1,0:T(8,128)S(1)}, u32[]{:S(2)}, u32[]{:S(2)}) collective-permute-start(f32[200,384]{1,0:T(8,128)S(1)} %get-tuple-element.118.refs_3_.refs_6_), channel_id=1, source_target_pairs={{0,1},{1,0},{2,3},{3,2},{4,5},{5,4},{6,7},{7,6},{8,9},{9,8},{10,11... | collective-permute-start | bytes 921608 | tf_op jit(solution)/shard_map/ppermute | solution.py:483
  18.8 2.3 %grad_act.1 = (bf16[208,768]{1,0:T(8,128)(2,1)S(1)}, f32[208,1536]{1,0:T(8,128)S(1)}, f32[1,768]{1,0:T(1,128)S(1)}, bf16[336,768]{1,0:T(8,128)(2,1)S(1)}, f32[336,1536]{1,0:T(8,128)S(1)}, /*index=5*/f32[1,768]{1,0:T(1,128)S(1)}) custom-call(s32[8]{0:T(128)S(1)} %stack.27.refs_0_, bf16[544,768]{1,0:T(8,128)(2,1)S(1)} %get-tuple-element.114.refs_1_.refs_6_, ...), custom_call_target="tpu_custom_call" | custom-call | flops 1 | bytes 1 | tf_op jit(solution)/shard_map/grad_act/pallas_call | solution.py:468
  21.1 2.0 %collective-permute-done.2.refs_1_ = f32[96,384]{1,0:T(8,128)S(1)} collective-permute-done((f32[96,384]{1,0:T(8,128)S(1)}, f32[96,384]{1,0:T(8,128)S(1)}, u32[]{:S(2)}, u32[]{:S(2)}) %collective-permute-start.2) | collective-permute-done | bytes 147488 | tf_op jit(solution)/shard_map/ppermute | solution.py:487
  28.5 4.2 %mlp_b.1 = (f32[336,768]{1,0:T(8,128)S(1)}, bf16[336,768]{1,0:T(8,128)(2,1)S(1)}, bf16[336,1536]{1,0:T(8,128)(2,1)S(1)}, bf16[336,1536]{1,0:T(8,128)(2,1)S(1)}, ...) custom-call(s32[8]{0:T(128)S(1)} %stack.27.refs_0_, bf16[544,768]{1,0:T(8,128)(2,1)S(1)} %get-tuple-element.113.refs_1_.refs_6_, ...), custom_call_target="tpu_custom_call" | custom-call | flops 1 | bytes 1 | tf_op jit(solution)/shard_map/mlp_b/pallas_call | solution.py:468
  33.6 3.2 %mlp_a.1 = (f32[208,768]{1,0:T(8,128)S(1)}, bf16[208,768]{1,0:T(8,128)(2,1)S(1)}, bf16[208,1536]{1,0:T(8,128)(2,1)S(1)}, bf16[208,1536]{1,0:T(8,128)(2,1)S(1)}, ...) custom-call(s32[8]{0:T(128)S(1)} %stack.27.refs_0_, bf16[544,768]{1,0:T(8,128)(2,1)S(1)} %get-tuple-element.113.refs_1_.refs_6_, ...), custom_call_target="tpu_custom_call" | custom-call | flops 1 | bytes 1 | tf_op jit(solution)/shard_map/mlp_a/pallas_call | solution.py:468
  37.2 3.0 %down_weights.1 = (f32[384,1536]{1,0:T(8,128)S(1)}, f32[384,768]{1,0:T(8,128)S(1)}, f32[384,768]{1,0:T(8,128)S(1)}) custom-call(s32[8]{0:T(128)S(1)} %stack.27.refs_0_, bf16[208,768]{1,0:T(8,128)(2,1)S(1)} %get-tuple-element.121.refs_3_.refs_1_, bf16[336,768]{1,0:T(8,128)(2,1)S(1)} %get-tuple-element.135.refs_2_, ...), custom_call_target="tpu_custom_call" | custom-call | flops 1 | bytes 1 | tf_op jit(solution)/shard_map/down_weights/pallas_call | solution.py:468
  40.8 2.8 %up_weights.1 = (f32[384,1536]{1,0:T(8,128)S(1)}, f32[384,768]{1,0:T(8,128)S(1)}, f32[384,768]{1,0:T(8,128)S(1)}) custom-call(s32[8]{0:T(128)S(1)} %stack.27.refs_0_, bf16[208,768]{1,0:T(8,128)(2,1)S(1)} %get-tuple-element.131.refs_1_, bf16[336,768]{1,0:T(8,128)(2,1)S(1)} %get-tuple-element.132.refs_2_, bf16[208,1536]{1,0:T(8,128)(2,1)S(1)} %get-tuple-element.133.refs_3_, ...), custom_call_target="tpu_custom_call" | custom-call | flops 1 | bytes 1 | tf_op jit(solution)/shard_map/up_weights/pallas_call | solution.py:468
  50.9 2.0 %mlp_part.1.refs_7_.refs_3_ = f32[528,768]{1,0:T(8,128)S(1)} custom-call(s32[8]{0:T(128)S(1)} %stack.27.refs_0_, bf16[208,1536]{1,0:T(8,128)(2,1)S(1)} %get-tuple-element.129.refs_3_.refs_1_, bf16[336,1536]{1,0:T(8,128)(2,1)S(1)} %get-tuple-element.130.refs_4_.refs_2_, bf16[1536,768]{1,0:T(8,128)(2,1)S(1)} %copy-done.1, ...), custom_call_target="tpu_custom_call" | custom-call | flops 1 | bytes 1 | tf_op jit(solution)/shard_map/mlp_part/pallas_call | solution.py:468
  54.5 2.3 %attn_again.1 = (f32[6,208,208]{2,1,0:T(8,128)S(1)}, f32[6,336,336]{2,1,0:T(8,128)S(1)}, f32[208,768]{1,0:T(8,128)S(1)}, f32[336,768]{1,0:T(8,128)S(1)}, f32[208...) custom-call(s32[8]{0:T(128)S(1)} %stack.27.refs_0_, ...), custom_call_target="tpu_custom_call" | custom-call | flops 1 | bytes 1 | tf_op jit(solution)/shard_map/attn_again/pallas_call | solution.py:468
  56.8 18.5 %collective-permute-done.13.refs_2_ = f32[528,768]{1,0:T(8,128)S(1)} collective-permute-done((f32[528,768]{1,0:T(8,128)S(1)}, f32[528,768]{1,0:T(8,128)S(1)}, u32[]{:S(2)}, u32[]{:S(2)}) %collective-permute-start.13) | collective-permute-done | bytes 1622048 | tf_op jit(solution)/shard_map/ppermute | solution.py:483
  75.3 5.3 %attn_backward_b.1 = (bf16[3,336,384]{2,1,0:T(8,128)(2,1)S(1)}, bf16[336,768]{1,0:T(8,128)(2,1)S(1)}, f32[336,768]{1,0:T(8,128)S(1)}, f32[8,768]{1,0:T(8,128)S(1)}, f32[328,768]{1,0:T(8,128)S(1)}) custom-call(s32[8]{0:T(128)S(1)} %stack.27.refs_0_, f32[528,768]{1,0:T(8,128)S(1)} %get-tuple-element.144.refs_1_, ...), custom_call_target="tpu_custom_call" | custom-call | flops 8999999488 | bytes 1 | tf_op jit(solution)/shard_map/attn_backward_b/pallas_call | solution.py:468
  85.2 3.8 %attn_backward_a.1 = (bf16[3,208,384]{2,1,0:T(8,128)(2,1)S(1)}, bf16[208,768]{1,0:T(8,128)(2,1)S(1)}, f32[208,768]{1,0:T(8,128)S(1)}, f32[8,768]{1,0:T(8,128)S(1)}, f32[528,768]{1,0:T(8,128)S(1)}) custom-call(s32[8]{0:T(128)S(1)} %stack.27.refs_0_, f32[528,768]{1,0:T(8,128)S(1)} %get-tuple-element.144.refs_1_, ...), custom_call_target="tpu_custom_call" | custom-call | flops 1 | bytes 1 | tf_op jit(solution)/shard_map/attn_backward_a/pallas_call | solution.py:468
  89.0 3.3 %attn_weights.1 = (f32[384,768]{1,0:T(8,128)S(1)}, f32[384,768]{1,0:T(8,128)S(1)}, f32[16,768]{1,0:T(8,128)S(1)}, f32[400,768]{1,0:T(8,128)S(1)}, f32[384,768]{1,0:T(8,128)S(1)}) custom-call(s32[8]{0:T(128)S(1)} %stack.27.refs_0_, bf16[544,768]{1,0:T(8,128)(2,1)S(1)} %get-tuple-element.115.refs_2_.refs_1_, ...), custom_call_target="tpu_custom_call" | custom-call | flops 1 | bytes 1 | tf_op jit(solution)/shard_map/attn_weights/pallas_call | solution.py:468
  94.9 2.6 %collective-permute-start.21 = (f32[48,3072]{1,0:T(8,128)S(1)}, f32[48,3072]{1,0:T(8,128)S(1)}, u32[]{:S(2)}, u32[]{:S(2)}) collective-permute-start(f32[48,3072]{1,0:T(8,128)S(1)} %get-tuple-element.177.refs_4_), channel_id=1, source_target_pairs={{0,16},{2,18},{4,20},{6,22},{8,24},{10,26},{12,28},{14,30},{16,0},... | collective-permute-start | bytes 1769480 | tf_op jit(solution)/shard_map/ppermute | solution.py:487
  101.1 9.0 %collective-permute-done.12.refs_4_ = f32[528,768]{1,0:T(8,128)S(1)} collective-permute-done((f32[528,768]{1,0:T(8,128)S(1)}, f32[528,768]{1,0:T(8,128)S(1)}, u32[]{:S(2)}, u32[]{:S(2)}) %collective-permute-start.12) | collective-permute-done | bytes 1622048 | tf_op jit(solution)/shard_map/ppermute | solution.py:483
  110.1 2.1 %block_out.1.refs_4_ = bf16[522,768]{1,0:T(8,128)(2,1)} custom-call(s32[8]{0:T(128)S(1)} %stack.27.refs_0_, f32[208,768]{1,0:T(8,128)S(1)} %get-tuple-element.128.refs_5_.refs_4_.refs_1_, f32[336,768]{1,0:T(8,128)S(1)} %get-tuple-element.127.refs_12_.refs_5_.refs_2_, f32[528,768]{1,0:T(8,128)S(1)} %mlp_part.1.refs_7_.refs_3_, ...), custom_call_target="tpu_custom_call" | custom-call | flops 99999997952 | bytes 1 | tf_op jit(solution)/shard_map/block_out/pallas_call | solution.py:468
  112.1 3.5 %collective-permute-done.23.refs_3_ = f32[208,768]{1,0:T(8,128)S(1)} collective-permute-done((f32[208,768]{1,0:T(8,128)S(1)}, f32[208,768]{1,0:T(8,128)S(1)}, u32[]{:S(2)}, u32[]{:S(2)}) %collective-permute-start.23) | collective-permute-done | bytes 639008 | tf_op jit(solution)/shard_map/ppermute | solution.py:487
  119.0 6.9 %collective-permute-done.22.refs_2_ = f32[192,768]{1,0:T(8,128)S(1)} collective-permute-done((f32[192,768]{1,0:T(8,128)S(1)}, f32[192,768]{1,0:T(8,128)S(1)}, u32[]{:S(2)}, u32[]{:S(2)}) %collective-permute-start.22) | collective-permute-done | bytes 589856 | tf_op jit(solution)/shard_map/ppermute | solution.py:487
  127.1 3.0 %collective-permute-done.25.refs_3_ = f32[112,768]{1,0:T(8,128)S(1)} collective-permute-done((f32[112,768]{1,0:T(8,128)S(1)}, f32[112,768]{1,0:T(8,128)S(1)}, u32[]{:S(2)}, u32[]{:S(2)}) %collective-permute-start.25) | collective-permute-done | bytes 344096 | tf_op jit(solution)/shard_map/ppermute | solution.py:487
  131.4 6.9 %collective-permute-done.24.refs_2_ = f32[96,768]{1,0:T(8,128)S(1)} collective-permute-done((f32[96,768]{1,0:T(8,128)S(1)}, f32[96,768]{1,0:T(8,128)S(1)}, u32[]{:S(2)}, u32[]{:S(2)}) %collective-permute-start.24) | collective-permute-done | bytes 294944 | tf_op jit(solution)/shard_map/ppermute | solution.py:487
  140.4 2.0 %collective-permute-done.20.refs_7_ = f32[528,768]{1,0:T(8,128)S(1)} collective-permute-done((f32[528,768]{1,0:T(8,128)S(1)}, f32[528,768]{1,0:T(8,128)S(1)}, u32[]{:S(2)}, u32[]{:S(2)}) %collective-permute-start.20) | collective-permute-done | bytes 1622048 | tf_op jit(solution)/shard_map/ppermute | solution.py:483
  143.4 2.7 %input_back.1.refs_4_ = f32[522,768]{1,0:T(8,128)} custom-call(s32[8]{0:T(128)S(1)} %stack.27.refs_0_, f32[544,768]{1,0:T(8,128)S(1)} %get-tuple-element.148.refs_3_.refs_1_, f32[544,1]{1,0:T(8,128)S(1)} %get-tuple-element.180.refs_2_, f32[208,768]{1,0:T(8,128)S(1)} %get-tuple-element.181.refs_3_, f32[336,768]{1,0:T(8,128)S(1)} %get-tuple-element.182.refs_4_, ...), custom_call_target="tpu_custom_call" | custom-call | flops 1 | bytes 1 | tf_op jit(solution)/shard_map/input_back/pallas_call | solution.py:468
  (95 shorter events, 48.0 us)
Async XLA Ops:
  1.6 14.5 %collective-permute-start = (f32[96,768]{1,0:T(8,128)S(1)}, f32[96,768]{1,0:T(8,128)S(1)}, u32[]{:S(2)}, u32[]{:S(2)}) collective-permute-start(f32[96,768]{1,0:T(8,128)S(1)} %dynamic-slice_convert_fusion), channel_id=1, source_target_pairs={{0,1},{1,0},{2,3},{3,2},{4,5},{5,4},{6,7},{7,6},{8,9},{9,8},{10,11... | collective-permute-start | bytes 884744 | tf_op jit(solution)/shard_map/ppermute | solution.py:483
  14.0 14.5 %collective-permute-start.7 = (f32[328,384]{1,0:T(8,128)S(1)}, f32[328,384]{1,0:T(8,128)S(1)}, u32[]{:S(2)}, u32[]{:S(2)}) collective-permute-start(f32[328,384]{1,0:T(8,128)S(1)} %get-tuple-element.125.refs_3_.refs_7_), channel_id=1, source_target_pairs={{0,1},{1,0},{2,3},{3,2},{4,5},{5,4},{6,7},{7,6},{8,9},{9,8},{10,11... | collective-permute-start | bytes 1511432 | tf_op jit(solution)/shard_map/ppermute | solution.py:483
  14.1 19.5 %collective-permute-start.1 = (f32[200,384]{1,0:T(8,128)S(1)}, f32[200,384]{1,0:T(8,128)S(1)}, u32[]{:S(2)}, u32[]{:S(2)}) collective-permute-start(f32[200,384]{1,0:T(8,128)S(1)} %get-tuple-element.118.refs_3_.refs_6_), channel_id=1, source_target_pairs={{0,1},{1,0},{2,3},{3,2},{4,5},{5,4},{6,7},{7,6},{8,9},{9,8},{10,11... | collective-permute-start | bytes 921608 | tf_op jit(solution)/shard_map/ppermute | solution.py:483
  16.7 6.4 %collective-permute-start.2 = (f32[96,384]{1,0:T(8,128)S(1)}, f32[96,384]{1,0:T(8,128)S(1)}, u32[]{:S(2)}, u32[]{:S(2)}) collective-permute-start(f32[96,384]{1,0:T(8,128)S(1)} %get-tuple-element.119), channel_id=1, source_target_pairs={{0,4},{2,6},{4,0},{6,2},{8,12},{10,14},{12,8},{14,10},{16,20},{18,... | collective-permute-start | bytes 442376 | tf_op jit(solution)/shard_map/ppermute | solution.py:487
  18.3 6.4 %collective-permute-start.3 = (f32[96,384]{1,0:T(8,128)S(1)}, f32[96,384]{1,0:T(8,128)S(1)}, u32[]{:S(2)}, u32[]{:S(2)}) collective-permute-start(f32[96,384]{1,0:T(8,128)S(1)} %get-tuple-element.120), channel_id=1, source_target_pairs={{0,4},{2,6},{4,0},{6,2},{8,12},{10,14},{12,8},{14,10},{16,20},{18,... | collective-permute-start | bytes 442376 | tf_op jit(solution)/shard_map/ppermute | solution.py:487
  18.8 8.1 %collective-permute-start.4 = (f32[96,768]{1,0:T(8,128)S(1)}, f32[96,768]{1,0:T(8,128)S(1)}, u32[]{:S(2)}, u32[]{:S(2)}) collective-permute-start(f32[96,768]{1,0:T(8,128)S(1)} %get-tuple-element.116.refs_3_.refs_2_), channel_id=1, source_target_pairs={{0,2},{2,0},{4,6},{6,4},{8,10},{10,8},{12,14},{14,12},{16,18},{18,... | collective-permute-start | bytes 884744 | tf_op jit(solution)/shard_map/ppermute | solution.py:487
  36.9 38.5 %collective-permute-start.13 = (f32[528,768]{1,0:T(8,128)S(1)}, f32[528,768]{1,0:T(8,128)S(1)}, u32[]{:S(2)}, u32[]{:S(2)}) collective-permute-start(f32[528,768]{1,0:T(8,128)S(1)} %get-tuple-element.144.refs_1_), channel_id=1, source_target_pairs={{0,1},{1,0},{2,3},{3,2},{4,5},{5,4},{6,7},{7,6},{8,9},{9,8},{10,11... | collective-permute-start | bytes 4866056 | tf_op jit(solution)/shard_map/ppermute | solution.py:483
  40.3 4.5 %collective-permute-start.11 = (f32[384,768]{1,0:T(8,128)S(1)}, f32[384,768]{1,0:T(8,128)S(1)}, u32[]{:S(2)}, u32[]{:S(2)}) collective-permute-start(f32[384,768]{1,0:T(8,128)S(1)} %get-tuple-element.141), channel_id=1, source_target_pairs={{0,2},{2,0},{4,6},{6,4},{8,10},{10,8},{12,14},{14,12},{16,18},{18,... | collective-permute-start | bytes 3538952 | tf_op jit(solution)/shard_map/ppermute | solution.py:487
  43.8 4.5 %collective-permute-start.9 = (f32[384,768]{1,0:T(8,128)S(1)}, f32[384,768]{1,0:T(8,128)S(1)}, u32[]{:S(2)}, u32[]{:S(2)}) collective-permute-start(f32[384,768]{1,0:T(8,128)S(1)} %get-tuple-element.139), channel_id=1, source_target_pairs={{0,2},{2,0},{4,6},{6,4},{8,10},{10,8},{12,14},{14,12},{16,18},{18,... | collective-permute-start | bytes 3538952 | tf_op jit(solution)/shard_map/ppermute | solution.py:487
  45.7 34.9 %collective-permute-start.15 = (f32[192,1536]{1,0:T(8,128)S(1)}, f32[192,1536]{1,0:T(8,128)S(1)}, u32[]{:S(2)}, u32[]{:S(2)}) collective-permute-start(f32[192,1536]{1,0:T(8,128)S(1)} %get-tuple-element.142.refs_4_), channel_id=1, source_target_pairs={{0,4},{2,6},{4,0},{6,2},{8,12},{10,14},{12,8},{14,10},{16,20},{18,... | collective-permute-start | bytes 3538952 | tf_op jit(solution)/shard_map/ppermute | solution.py:487
  49.0 32.3 %collective-permute-start.14 = (f32[192,1536]{1,0:T(8,128)S(1)}, f32[192,1536]{1,0:T(8,128)S(1)}, u32[]{:S(2)}, u32[]{:S(2)}) collective-permute-start(f32[192,1536]{1,0:T(8,128)S(1)} %get-tuple-element.143.refs_4_), channel_id=1, source_target_pairs={{0,8},{2,10},{4,12},{6,14},{8,0},{10,2},{12,4},{14,6},{16,24},{18,... | collective-permute-start | bytes 3538952 | tf_op jit(solution)/shard_map/ppermute | solution.py:487
  52.9 57.2 %collective-permute-start.12 = (f32[528,768]{1,0:T(8,128)S(1)}, f32[528,768]{1,0:T(8,128)S(1)}, u32[]{:S(2)}, u32[]{:S(2)}) collective-permute-start(f32[528,768]{1,0:T(8,128)S(1)} %mlp_part.1.refs_7_.refs_3_), channel_id=1, source_target_pairs={{0,1},{1,0},{2,3},{3,2},{4,5},{5,4},{6,7},{7,6},{8,9},{9,8},{10,11... | collective-permute-start | bytes 4866056 | tf_op jit(solution)/shard_map/ppermute | solution.py:483
  82.1 10.8 %collective-permute-start.19 = (f32[96,1536]{1,0:T(8,128)S(1)}, f32[96,1536]{1,0:T(8,128)S(1)}, u32[]{:S(2)}, u32[]{:S(2)}) collective-permute-start(f32[96,1536]{1,0:T(8,128)S(1)} %get-tuple-element.160.refs_13_), channel_id=1, source_target_pairs={{0,4},{2,6},{4,0},{6,2},{8,12},{10,14},{12,8},{14,10},{16,20},{18,... | collective-permute-start | bytes 1769480 | tf_op jit(solution)/shard_map/ppermute | solution.py:487
  83.6 10.5 %collective-permute-start.18 = (f32[96,1536]{1,0:T(8,128)S(1)}, f32[96,1536]{1,0:T(8,128)S(1)}, u32[]{:S(2)}, u32[]{:S(2)}) collective-permute-start(f32[96,1536]{1,0:T(8,128)S(1)} %get-tuple-element.159.refs_3_), channel_id=1, source_target_pairs={{0,8},{2,10},{4,12},{6,14},{8,0},{10,2},{12,4},{14,6},{16,24},{18,... | collective-permute-start | bytes 1769480 | tf_op jit(solution)/shard_map/ppermute | solution.py:487
  92.3 5.2 %collective-permute-start.17 = (f32[400,768]{1,0:T(8,128)S(1)}, f32[400,768]{1,0:T(8,128)S(1)}, u32[]{:S(2)}, u32[]{:S(2)}) collective-permute-start(f32[400,768]{1,0:T(8,128)S(1)} %get-tuple-element.174), channel_id=1, source_target_pairs={{0,2},{2,0},{4,6},{6,4},{8,10},{10,8},{12,14},{14,12},{16,18},{18,... | collective-permute-start | bytes 3686408 | tf_op jit(solution)/shard_map/ppermute | solution.py:487
  92.4 7.4 %collective-permute-start.16 = (f32[384,768]{1,0:T(8,128)S(1)}, f32[384,768]{1,0:T(8,128)S(1)}, u32[]{:S(2)}, u32[]{:S(2)}) collective-permute-start(f32[384,768]{1,0:T(8,128)S(1)} %get-tuple-element.171), channel_id=1, source_target_pairs={{0,2},{2,0},{4,6},{6,4},{8,10},{10,8},{12,14},{14,12},{16,18},{18,... | collective-permute-start | bytes 3538952 | tf_op jit(solution)/shard_map/ppermute | solution.py:487
  92.9 49.6 %collective-permute-start.20 = (f32[528,768]{1,0:T(8,128)S(1)}, f32[528,768]{1,0:T(8,128)S(1)}, u32[]{:S(2)}, u32[]{:S(2)}) collective-permute-start(f32[528,768]{1,0:T(8,128)S(1)} %get-tuple-element.183.refs_6_), channel_id=1, source_target_pairs={{0,1},{1,0},{2,3},{3,2},{4,5},{5,4},{6,7},{7,6},{8,9},{9,8},{10,11... | collective-permute-start | bytes 4866056 | tf_op jit(solution)/shard_map/ppermute | solution.py:483
  94.9 44.1 %collective-permute-start.21 = (f32[48,3072]{1,0:T(8,128)S(1)}, f32[48,3072]{1,0:T(8,128)S(1)}, u32[]{:S(2)}, u32[]{:S(2)}) collective-permute-start(f32[48,3072]{1,0:T(8,128)S(1)} %get-tuple-element.177.refs_4_), channel_id=1, source_target_pairs={{0,16},{2,18},{4,20},{6,22},{8,24},{10,26},{12,28},{14,30},{16,0},... | collective-permute-start | bytes 1769480 | tf_op jit(solution)/shard_map/ppermute | solution.py:487
  98.2 17.4 %collective-permute-start.23 = (f32[208,768]{1,0:T(8,128)S(1)}, f32[208,768]{1,0:T(8,128)S(1)}, u32[]{:S(2)}, u32[]{:S(2)}) collective-permute-start(f32[208,768]{1,0:T(8,128)S(1)} %get-tuple-element.178.refs_3_), channel_id=1, source_target_pairs={{0,4},{2,6},{4,0},{6,2},{8,12},{10,14},{12,8},{14,10},{16,20},{18,... | collective-permute-start | bytes 1916936 | tf_op jit(solution)/shard_map/ppermute | solution.py:487
  100.5 25.4 %collective-permute-start.22 = (f32[192,768]{1,0:T(8,128)S(1)}, f32[192,768]{1,0:T(8,128)S(1)}, u32[]{:S(2)}, u32[]{:S(2)}) collective-permute-start(f32[192,768]{1,0:T(8,128)S(1)} %get-tuple-element.179.refs_6_), channel_id=1, source_target_pairs={{0,4},{2,6},{4,0},{6,2},{8,12},{10,14},{12,8},{14,10},{16,20},{18,... | collective-permute-start | bytes 1769480 | tf_op jit(solution)/shard_map/ppermute | solution.py:487
  117.4 12.7 %collective-permute-start.25 = (f32[112,768]{1,0:T(8,128)S(1)}, f32[112,768]{1,0:T(8,128)S(1)}, u32[]{:S(2)}, u32[]{:S(2)}) collective-permute-start(f32[112,768]{1,0:T(8,128)S(1)} %get-tuple-element.188.refs_3_), channel_id=1, source_target_pairs={{0,8},{2,10},{4,12},{6,14},{8,0},{10,2},{12,4},{14,6},{16,24},{18,... | collective-permute-start | bytes 1032200 | tf_op jit(solution)/shard_map/ppermute | solution.py:487
  126.6 11.7 %collective-permute-start.24 = (f32[96,768]{1,0:T(8,128)S(1)}, f32[96,768]{1,0:T(8,128)S(1)}, u32[]{:S(2)}, u32[]{:S(2)}) collective-permute-start(f32[96,768]{1,0:T(8,128)S(1)} %get-tuple-element.190.refs_4_), channel_id=1, source_target_pairs={{0,8},{2,10},{4,12},{6,14},{8,0},{10,2},{12,4},{14,6},{16,24},{18,... | collective-permute-start | bytes 884744 | tf_op jit(solution)/shard_map/ppermute | solution.py:487
  130.7 15.7 %collective-permute-start.26 = (f32[64,768]{1,0:T(8,128)S(1)}, f32[64,768]{1,0:T(8,128)S(1)}, u32[]{:S(2)}, u32[]{:S(2)}) collective-permute-start(f32[64,768]{1,0:T(8,128)S(1)} %get-tuple-element.193.refs_3_), channel_id=1, source_target_pairs={{0,16},{2,18},{4,20},{6,22},{8,24},{10,26},{12,28},{14,30},{16,0},... | collective-permute-start | bytes 589832 | tf_op jit(solution)/shard_map/ppermute | solution.py:487
  138.9 10.6 %collective-permute-start.28 = (f32[48,768]{1,0:T(8,128)S(1)}, f32[48,768]{1,0:T(8,128)S(1)}, u32[]{:S(2)}, u32[]{:S(2)}) collective-permute-start(f32[48,768]{1,0:T(8,128)S(1)} %get-tuple-element.194.refs_3_), channel_id=1, source_target_pairs={{0,16},{2,18},{4,20},{6,22},{8,24},{10,26},{12,28},{14,30},{16,0},... | collective-permute-start | bytes 442376 | tf_op jit(solution)/shard_map/ppermute | solution.py:487
  (19 other events, 98.9 us)
